TPU v7x, 128 devices: a whole 4x4x4 slice. The times are simulated.
128 devices in a mesh: outer: 2 (over core), inner: 64 (over z, y, x).
Axes of the slice: x: 4, y: 4, z: 4, core: 2. Of those that a mesh axis runs over, the one named last changes fastest.
Arguments:
- matrix: float32 [65536, 1024], P(('outer', 'inner'))
- sign_flip: int32 [65536], P(('outer', 'inner')), may hold values from -1 to 1, as said below
- keep_list: int32 [128, 2], replicated, may hold values from 0 to 3, as said below
- ridge_weights: float32 [1024], replicated, may hold values from 0.05 to 1
Outputs:
- sketch: float32 [32768, 1024], P(('outer', 'inner'))
- factor: float32 [1024, 1024], P(('outer', 'inner'))
Inputs may be any that keep to these rules, and one draw needn't show every extreme that they name: `sign_flip`: each entry is 1 or -1. `keep_list`: row s lists 2 different block numbers of device s's rows in increasing order.
All inputs are finite; a program needn't handle non-finite values.
Results may differ from a plain program's by a relative error of at most 0.00026.
Values sent between devices are 32-bit elements; how exact they have to be, the bound alone decides.
No kernel may reach another device: no remote copies, remote signals or barrier semaphores. Data moves between devices by JAX's collectives and lax.ppermute only.
A program may use at most 128 MiB of HBM per device.

v0:
```python
import math

import jax
import jax.numpy as jnp
from jax import lax
from jax.sharding import PartitionSpec as P

precise = lax.Precision.HIGHEST


def joined(part, axis, combine):
    gathered = lax.all_gather(part, axis)

    def take(source):
        return lax.dynamic_index_in_dim(gathered, source, 0, False)

    return lax.fori_loop(
        1, lax.axis_size(axis), lambda source, state: combine(state, take(source)), take(0)
    )


def sign_table(extent):
    index_list = lax.iota(jnp.int32, extent)
    common_bits = jnp.bitwise_and(index_list[:, None], index_list[None, :])
    parity = jnp.zeros((extent, extent), jnp.int32)
    for shift_by in range(max(extent.bit_length() - 1, 0)):
        parity = parity + jnp.bitwise_and(jnp.right_shift(common_bits, shift_by), 1)
    return (1 - 2 * (parity % 2)).astype(jnp.float32)


def mix_local(slab_block):
    rows_dev, features = slab_block.shape
    first_len = 2 ** ((rows_dev.bit_length() - 1) // 2)
    second = rows_dev // first_len
    shaped = slab_block.reshape(first_len, second, features)
    shaped = jnp.einsum("qb,abf->aqf", sign_table(second), shaped, precision=precise)
    shaped = jnp.einsum("pa,aqf->pqf", sign_table(first_len), shaped, precision=precise)
    return shaped.reshape(rows_dev, features)


def mix_inner(values):
    return jnp.einsum("ia,a...->i...", sign_table(values.shape[0]), values, precision=precise)


def join_factors(first_factor, second_factor):
    stacked = jnp.concatenate([first_factor, second_factor], axis=0)
    summed = lax.dot_general(
        stacked,
        stacked,
        (((0,), (0,)), ((), ())),
        precision=precise,
        preferred_element_type=jnp.float32,
    )
    return jnp.transpose(jnp.linalg.cholesky(summed))


def local(matrix, sign_flip, keep_list, ridge_weights):
    rows_dev, features = matrix.shape
    n_inner = lax.axis_size("inner")
    n_outer = lax.axis_size("outer")
    shards = n_inner * n_outer
    piece_rows = rows_dev // n_inner
    spread = piece_rows // n_outer
    norm_scale = 1.0 / math.sqrt(rows_dev * shards)
    position = lax.axis_index(("outer", "inner"))
    own_blocks = lax.dynamic_index_in_dim(keep_list, position, 0, keepdims=False)
    flipped = matrix * sign_flip.astype(jnp.float32)[:, None]
    mixed_rows = mix_local(flipped)
    row_grid = mixed_rows.reshape(n_inner, piece_rows, features)
    inner_done = mix_inner(
        lax.all_to_all(row_grid, "inner", split_axis=0, concat_axis=0, tiled=True)
    )
    split_rows = inner_done.reshape(n_inner, n_outer, spread, features)
    values = lax.all_to_all(split_rows, "outer", split_axis=1, concat_axis=1, tiled=True)
    pattern = sign_table(values.shape[1])
    mixed_out = jnp.einsum("ob,mb...->mo...", pattern, values, precision=precise) * norm_scale
    block_rows = mixed_out.reshape(rows_dev // 128, 128, features)
    sketch = jnp.take(block_rows, own_blocks, axis=0).reshape(-1, features)
    local_gram = lax.dot_general(
        sketch,
        sketch,
        (((0,), (0,)), ((), ())),
        precision=precise,
        preferred_element_type=jnp.float32,
    ) / (sketch.shape[0] * shards)
    summed = lax.psum(local_gram, "inner")
    leaf_factor = jnp.transpose(jnp.linalg.cholesky(summed + jnp.diag(ridge_weights) / n_outer))
    factor = joined(leaf_factor, "outer", join_factors)
    rows_out = features // shards
    return (sketch, lax.dynamic_slice_in_dim(factor, position * rows_out, rows_out, 0))


def solution(mesh):
    return jax.shard_map(
        local,
        mesh=mesh,
        in_specs=(P(("outer", "inner"), None), P(("outer", "inner")), P(), P()),
        out_specs=(P(("outer", "inner"), None), P(("outer", "inner"), None)),
        check_vma=False,
    )
```

profile of v0, /device:TPU:1, one launch (start us, length us, event | category | flops | bytes accessed | tf_op | source)
XLA Modules:
  0.0 727.8 jit_solution(4521386483065559199)
XLA Ops:
  17.1 12.0 %all-to-all-start = ((f32[64,8,1024]{2,1,0:T(8,128)}), f32[64,8,1024]{2,1,0:T(8,128)S(1)}, u32[]{:S(2)}, u32[]{:S(2)}) async-start(f32[64,8,1024]{2,1,0:T(8,128)} %bitcast.120), calls=%async_computation | async-start | bytes 4194304 | tf_op jit(solution)/shard_map/all_to_all | solution.py:71
  29.7 27.9 %all-to-all-done = f32[64,8,1024]{2,1,0:T(8,128)S(1)} async-done(((f32[64,8,1024]{2,1,0:T(8,128)}), f32[64,8,1024]{2,1,0:T(8,128)S(1)}, u32[]{:S(2)}, u32[]{:S(2)}) %all-to-all-start) | async-done | bytes 2097184 | tf_op jit(solution)/shard_map/all_to_all | solution.py:71
  88.5 133.9 %all-reduce.3.cloned.1.call-done = f32[1024,1024]{0,1:T(8,128)} async-done(((f32[1024,1024]{0,1:T(8,128)}), f32[1024,1024]{0,1:T(8,128)}) %all-reduce.3.cloned.1.call-update) | async-done | bytes 4194320 | tf_op jit(solution)/shard_map/psum | solution.py:86
  239.1 11.7 %cholesky.619 = f32[128,128]{1,0:T(8,128)S(1)} custom-call(f32[128,128]{1,0:T(8,128)S(1)} %cholesky.911), custom_call_target="Cholesky" | custom-call | tf_op jit(solution)/shard_map/jit(cholesky)/cholesky | solution.py:87
  250.9 9.8 %custom-call.51 = f32[1,128,128]{1,2,0:T(8,128)S(1)} custom-call(f32[1,128,128]{2,1,0:T(8,128)S(1)} %get-tuple-element.64), custom_call_target="InvertDiagBlocksLowerTriangular" | custom-call | tf_op jit(solution)/shard_map/jit(cholesky)/cholesky | solution.py:87
  267.1 11.9 %cholesky.638 = f32[128,128]{1,0:T(8,128)S(1)} custom-call(f32[128,128]{1,0:T(8,128)S(1)} %cholesky.915), custom_call_target="Cholesky" | custom-call | tf_op jit(solution)/shard_map/jit(cholesky)/cholesky | solution.py:87
  292.8 11.7 %cholesky.659 = f32[128,128]{1,0:T(8,128)S(1)} custom-call(f32[128,128]{1,0:T(8,128)S(1)} %cholesky.920), custom_call_target="Cholesky" | custom-call | tf_op jit(solution)/shard_map/jit(cholesky)/cholesky | solution.py:87
  319.2 12.1 %cholesky.678 = f32[128,128]{1,0:T(8,128)S(1)} custom-call(f32[128,128]{1,0:T(8,128)S(1)} %cholesky.925), custom_call_target="Cholesky" | custom-call | tf_op jit(solution)/shard_map/jit(cholesky)/cholesky | solution.py:87
  345.8 11.7 %cholesky.697 = f32[128,128]{1,0:T(8,128)S(1)} custom-call(f32[128,128]{1,0:T(8,128)S(1)} %cholesky.930), custom_call_target="Cholesky" | custom-call | tf_op jit(solution)/shard_map/jit(cholesky)/cholesky | solution.py:87
  358.8 10.0 %custom-call.55 = f32[1,128,128]{1,2,0:T(8,128)S(1)} custom-call(f32[1,128,128]{2,1,0:T(8,128)S(1)} %get-tuple-element.52), custom_call_target="InvertDiagBlocksLowerTriangular" | custom-call | tf_op jit(solution)/shard_map/jit(cholesky)/cholesky | solution.py:87
  372.1 11.7 %cholesky.716 = f32[128,128]{1,0:T(8,128)S(1)} custom-call(f32[128,128]{1,0:T(8,128)S(1)} %cholesky.935), custom_call_target="Cholesky" | custom-call | tf_op jit(solution)/shard_map/jit(cholesky)/cholesky | solution.py:87
  397.9 12.1 %cholesky.735 = f32[128,128]{1,0:T(8,128)S(1)} custom-call(f32[128,128]{1,0:T(8,128)S(1)} %cholesky.940), custom_call_target="Cholesky" | custom-call | tf_op jit(solution)/shard_map/jit(cholesky)/cholesky | solution.py:87
  423.7 11.7 %cholesky.752 = f32[128,128]{1,0:T(8,128)S(1)} custom-call(f32[128,128]{1,0:T(8,128)S(1)} %convolution_subtract_fusion.13), custom_call_target="Cholesky" | custom-call | tf_op jit(solution)/shard_map/jit(cholesky)/cholesky | solution.py:87
  448.7 20.5 %all-gather.3.cloned.1.call-done = f32[2048,1024]{0,1:T(8,128)} async-done(((f32[1024,1024]{0,1:T(8,128)}), f32[2048,1024]{0,1:T(8,128)}) %all-gather.3.cloned.1.call-update) | async-done | bytes 8388624 | tf_op jit(solution)/shard_map/all_gather | solution.py:12
  469.2 33.1 %fusion.162 = f32[1024,1024]{1,0:T(8,128)} fusion(f32[2048,1024]{0,1:T(8,128)} %all-gather.3.cloned.1.call-done), kind=kOutput, calls=%fused_computation.269 | convolution fusion | flops 25769803776 | bytes 12582912 | tf_op jit(solution)/shard_map/while/body/eval_jaxpr/dot_general | solution.py:47
  514.1 11.7 %cholesky.767 = f32[128,128]{1,0:T(8,128)S(1)} custom-call(f32[128,128]{1,0:T(8,128)S(1)} %cholesky.944), custom_call_target="Cholesky" | custom-call | tf_op jit(solution)/shard_map/while/body/eval_jaxpr/jit(cholesky)/cholesky | solution.py:54
  541.9 11.9 %cholesky.786 = f32[128,128]{1,0:T(8,128)S(1)} custom-call(f32[128,128]{1,0:T(8,128)S(1)} %cholesky.948), custom_call_target="Cholesky" | custom-call | tf_op jit(solution)/shard_map/while/body/eval_jaxpr/jit(cholesky)/cholesky | solution.py:54
  569.8 11.7 %cholesky.807 = f32[128,128]{1,0:T(8,128)S(1)} custom-call(f32[128,128]{1,0:T(8,128)S(1)} %cholesky.953), custom_call_target="Cholesky" | custom-call | tf_op jit(solution)/shard_map/while/body/eval_jaxpr/jit(cholesky)/cholesky | solution.py:54
  596.2 12.1 %cholesky.826 = f32[128,128]{1,0:T(8,128)S(1)} custom-call(f32[128,128]{1,0:T(8,128)S(1)} %cholesky.958), custom_call_target="Cholesky" | custom-call | tf_op jit(solution)/shard_map/while/body/eval_jaxpr/jit(cholesky)/cholesky | solution.py:54
  622.8 11.7 %cholesky.845 = f32[128,128]{1,0:T(8,128)S(1)} custom-call(f32[128,128]{1,0:T(8,128)S(1)} %cholesky.963), custom_call_target="Cholesky" | custom-call | tf_op jit(solution)/shard_map/while/body/eval_jaxpr/jit(cholesky)/cholesky | solution.py:54
  635.8 9.9 %custom-call.62 = f32[1,128,128]{1,2,0:T(8,128)S(1)} custom-call(f32[1,128,128]{2,1,0:T(8,128)S(1)} %get-tuple-element.30), custom_call_target="InvertDiagBlocksLowerTriangular" | custom-call | tf_op jit(solution)/shard_map/while/body/eval_jaxpr/jit(cholesky)/cholesky | solution.py:54
  649.1 11.7 %cholesky.864 = f32[128,128]{1,0:T(8,128)S(1)} custom-call(f32[128,128]{1,0:T(8,128)S(1)} %cholesky.968), custom_call_target="Cholesky" | custom-call | tf_op jit(solution)/shard_map/while/body/eval_jaxpr/jit(cholesky)/cholesky | solution.py:54
  674.9 11.9 %cholesky.883 = f32[128,128]{1,0:T(8,128)S(1)} custom-call(f32[128,128]{1,0:T(8,128)S(1)} %cholesky.973), custom_call_target="Cholesky" | custom-call | tf_op jit(solution)/shard_map/while/body/eval_jaxpr/jit(cholesky)/cholesky | solution.py:54
  700.5 11.7 %cholesky.900 = f32[128,128]{1,0:T(8,128)S(1)} custom-call(f32[128,128]{1,0:T(8,128)S(1)} %convolution_subtract_fusion.12), custom_call_target="Cholesky" | custom-call | tf_op jit(solution)/shard_map/while/body/eval_jaxpr/jit(cholesky)/cholesky | solution.py:54
  (130 shorter events, 257.1 us)
Async XLA Ops:
  7.2 22.3 %copy-start = (s32[128,2]{0,1:T(2,128)S(1)}, s32[128,2]{0,1:T(2,128)}, u32[]{:S(2)}) copy-start(s32[128,2]{0,1:T(2,128)} %param.7) | copy-start | bytes 3076
  17.1 40.4 %all-to-all-start = ((f32[64,8,1024]{2,1,0:T(8,128)}), f32[64,8,1024]{2,1,0:T(8,128)S(1)}, u32[]{:S(2)}, u32[]{:S(2)}) async-start(f32[64,8,1024]{2,1,0:T(8,128)} %bitcast.120), calls=%async_computation | async-start | bytes 4194304 | tf_op jit(solution)/shard_map/all_to_all | solution.py:71
  29.1 193.3 %all-reduce.3.cloned.1.call-start = ((), (), s32[]{:S(2)}) async-start(), calls=%async_computation.2 | async-start | bytes 8388608 | tf_op jit(solution)/shard_map/psum | solution.py:86
  82.8 139.6 %copy-start.4 = (f32[1024]{0:T(1024)S(1)}, f32[1024]{0:T(1024)}, u32[]{:S(2)}) copy-start(f32[1024]{0:T(1024)} %param.8) | copy-start | bytes 12292
  88.4 380.8 %all-gather.3.cloned.1.call-start = ((), (), s32[]{:S(2)}) async-start(), calls=%async_computation.3 | async-start | bytes 12582912 | tf_op jit(solution)/shard_map/all_gather | solution.py:12
  237.2 1.9 copy-start.3
  512.2 1.9 copy-start.2
  620.5 100.3 %copy-start.1 = (s32[128,2]{0,1:T(2,128)S(1)}, s32[128,2]{0,1:T(2,128)}, u32[]{:S(2)}) copy-start(s32[128,2]{0,1:T(2,128)} %param.7) | copy-start | bytes 3076
Sparse Core Ops, SparseCore 0:
  88.5 133.7 all-reduce.2
  447.3 21.8 all-gather.2
where the time goes:
time: 735 us; the launch traced here: 728 us
  other arithmetic  369 us (50%)
  waiting for transfers between devices  182 us (25%)
  matrix products  100 us (14%)
  local copies, waits for them, and re-layouts  30.9 us (4%)
  between operations  24.6 us (3%)
  starting transfers between devices  12.3 us (2%)
  blocking collectives  8.01 us (1%)
    another operation x31, other arithmetic, join_factors(): return jnp.transpose(jnp.linalg.cholesky(summed))  173 us
    another operation x30, other arithmetic, local(): jnp.linalg.cholesky(summed + jnp.diag(ridge_weights) / n_outer)  172 us
    psum x1, waiting for transfers between devices, local(): summed = lax.psum(local_gram, 'inner')  134 us
    dot_general x1, matrix products, join_factors(): lax.dot_general(stacked, stacked, (((0,), (0,)), ((), ())), precision=pre...  33.1 us
    all_to_all x1, waiting for transfers between devices, local(): lax.all_to_all(row_grid, 'inner', split_axis=0, concat_axis=0, tiled=True)  27.9 us
    another operation x14, matrix products, local(): jnp.linalg.cholesky(summed + jnp.diag(ridge_weights) / n_outer)  23.1 us
    another operation x14, matrix products, join_factors(): return jnp.transpose(jnp.linalg.cholesky(summed))  22.8 us
    all_gather x1, waiting for transfers between devices, joined(): gathered = lax.all_gather(part, axis)  20.5 us
  transfers between devices with their start and end apart: 3, of which 3 were waited for; matrix products, arithmetic and copies ran while one was open for 0% of the time, Pallas kernels for 0%

commit v1 on v0

v1 whole, which is shorter than its diff:
```python
import functools

import jax
import jax.numpy as jnp
import numpy as np
from jax import lax
from jax.experimental import pallas as pl
from jax.experimental.pallas import tpu as pltpu
from jax.sharding import PartitionSpec as P

precise = lax.Precision.HIGHEST
f32 = jnp.float32
bf16 = jnp.bfloat16
VMEM = pl.BlockSpec(memory_space=pltpu.VMEM)
SMEM = pl.BlockSpec(memory_space=pltpu.SMEM)
FEAT = 1024
NB = 128
PANELS = FEAT // NB
STRIPS = ((0, 3, 4, 7), (1, 2, 5, 6))
HALF_BLOCKS = 18
Z_GROUPS = [[i + 16 * j for j in range(4)] for i in range(16)]
PLANES = [[16 * j + i for i in range(16)] for j in range(4)]


def params(mib=48):
    return pltpu.CompilerParams(vmem_limit_bytes=mib << 20)


def parity_sign(left, right):
    common = left & right
    parity = np.zeros_like(common)
    for shift_by in range(10):
        parity ^= (common >> shift_by) & 1
    return 1 - 2 * parity


def local_table():
    az, c, axy, e = np.meshgrid(range(4), range(2), range(16), range(4), indexing="ij")
    k = (az * 128 + axy * 8 + c * 4 + e).reshape(-1, 1)
    return parity_sign(k, np.arange(512)[None, :]).astype(np.float32).astype(bf16)


def final_table():
    j, i, o, e = (v.reshape(-1, 1) for v in np.meshgrid(range(2), range(16), range(2), range(4), indexing="ij"))
    ip, op, jp, ep = (v.reshape(1, -1) for v in np.meshgrid(range(16), range(2), range(2), range(4), indexing="ij"))
    table = parity_sign(i, ip) * parity_sign(o, op) * (j == jp) * (e == ep)
    return table.astype(np.float32).astype(bf16)


def halves(x):
    high = x.astype(bf16)
    return high, (x - high.astype(f32)).astype(bf16)


def mm(a, b):
    return jnp.dot(a, b, preferred_element_type=f32)


def tmm(a, b):
    return lax.dot_general(a, b, (((0,), (0,)), ((), ())), preferred_element_type=f32)


def local_mix_kernel(table_ref, sign_ref, x_ref, o_ref, signed):
    @pl.when(pl.program_id(0) == 0)
    def _():
        signed[...] = (table_ref[...].astype(f32) * (sign_ref[...].astype(f32) * 2.0**-13)).astype(bf16)

    high, low = halves(x_ref[...])
    o_ref[...] = mm(signed[...], high) + mm(signed[...], low)


def local_mix(matrix, sign_flip):
    rows, features = matrix.shape
    cols = 256
    return pl.pallas_call(
        local_mix_kernel,
        grid=(features // cols,),
        out_shape=jax.ShapeDtypeStruct((rows, features), f32),
        in_specs=[
            pl.BlockSpec((rows, rows), lambda g: (0, 0)),
            pl.BlockSpec((1, rows), lambda g: (0, 0)),
            pl.BlockSpec((rows, cols), lambda g: (0, g)),
        ],
        out_specs=pl.BlockSpec((rows, cols), lambda g: (0, g)),
        scratch_shapes=[pltpu.VMEM((rows, rows), bf16)],
        compiler_params=params(),
    )(jnp.asarray(local_table()), sign_flip.reshape(1, rows), matrix)


def select_kernel(keep_ref, y_ref, v_ref):
    y0, y1, y2, y3 = (y_ref[z] for z in range(4))
    s, d, s2, d2 = y0 + y1, y0 - y1, y2 + y3, y2 - y3

    def combo(which):
        low = (which & 1) == 1
        first = jnp.where(low, d, s)
        second = jnp.where(low, d2, s2)
        return first + jnp.where((which & 2) == 2, -second, second)

    shape = s.shape
    v0 = combo(jnp.broadcast_to(keep_ref[:, 0:1], shape))
    v1 = combo(jnp.broadcast_to(keep_ref[:, 1:2], shape))
    upper = (lax.broadcasted_iota(jnp.int32, shape, 0) & 7) < 4
    even = jnp.where(upper, v0, pltpu.roll(v1, 4, axis=0))
    odd = jnp.where(upper, pltpu.roll(v0, shape[0] - 4, axis=0), v1)
    v_ref[:, 0] = even.reshape(16, 8, shape[1])
    v_ref[:, 1] = odd.reshape(16, 8, shape[1])


def select_rows(keep_rows, y):
    cols = 256
    features = y.shape[2]
    return pl.pallas_call(
        select_kernel,
        grid=(features // cols,),
        out_shape=jax.ShapeDtypeStruct((16, 2, 8, features), f32),
        in_specs=[
            pl.BlockSpec((128, 2), lambda g: (0, 0)),
            pl.BlockSpec((4, 128, cols), lambda g: (0, 0, g)),
        ],
        out_specs=pl.BlockSpec((16, 2, 8, cols), lambda g: (0, 0, 0, g)),
        compiler_params=params(),
    )(keep_rows, y)


def gram_kernel(ids_ref, v_ref, w_ref, g_ref, s_ref, high, low):
    core = ids_ref[0]
    for part, ref in enumerate((v_ref, w_ref)):
        h, l = halves(ref[...])
        high[256 * part : 256 * part + 256, :] = h
        low[256 * part : 256 * part + 256, :] = l
        own = ref[pl.ds(pl.multiple_of(core * 128, 128), 128), :]
        s_ref[:, part] = own.reshape(16, 8, FEAT)
    for which, strips in enumerate(STRIPS):

        @pl.when(core == which)
        def _():
            slot = 0
            for strip in strips:
                at = NB * strip
                h, l = high[:, at : at + NB], low[:, at : at + NB]
                right, right_low = high[:, at:], low[:, at:]
                total = tmm(h, right) + (tmm(h, right_low) + tmm(l, right))
                for block in range(PANELS - strip):
                    g_ref[slot] = total[:, NB * block : NB * block + NB]
                    slot += 1


def gram_half(ids, mine, theirs):
    rows = mine.shape[0]
    return pl.pallas_call(
        gram_kernel,
        out_shape=(
            jax.ShapeDtypeStruct((HALF_BLOCKS, NB, NB), f32),
            jax.ShapeDtypeStruct((16, 2, 8, FEAT), f32),
        ),
        in_specs=[SMEM, VMEM, VMEM],
        out_specs=(VMEM, VMEM),
        scratch_shapes=[pltpu.VMEM((2 * rows, FEAT), bf16)] * 2,
        compiler_params=params(),
    )(ids, mine, theirs)


def final_kernel(ids_ref, table_ref, r_ref, o_ref):
    high, low = halves(r_ref[...])
    total = mm(table_ref[...], high) + mm(table_ref[...], low)
    odd = (lax.broadcasted_iota(jnp.int32, total.shape, 0) >> 2) & 1
    flip = (odd * ids_ref[0]) == 1
    o_ref[...] = total * jnp.where(flip, -32.0, 32.0)


def final_mix(ids, received):
    rows, features = received.shape
    cols = 256
    return pl.pallas_call(
        final_kernel,
        grid=(features // cols,),
        out_shape=jax.ShapeDtypeStruct((rows, features), f32),
        in_specs=[
            SMEM,
            pl.BlockSpec((rows, rows), lambda g: (0, 0)),
            pl.BlockSpec((rows, cols), lambda g: (0, g)),
        ],
        out_specs=pl.BlockSpec((rows, cols), lambda g: (0, g)),
        compiler_params=params(),
    )(ids, jnp.asarray(final_table()), received)


def lane_splat(x, lane):
    return jnp.broadcast_to(x[:, lane : lane + 1], (8, NB))


def factor_block(w, upper, inverse):
    lane = lax.broadcasted_iota(jnp.int32, (8, NB), 1)
    sub = lax.broadcasted_iota(jnp.int32, (8, NB), 0)
    pairs = [(a, b) for a in range(8) for b in range(a, 8)]

    def row_splat(row):
        return jnp.broadcast_to(w[row : row + 1, :], (8, NB))

    rho = [row_splat(b) for b in range(8)]
    e = {(a, b): lane_splat(rho[a], b) for a, b in pairs}
    for step in range(16):
        base = 8 * step
        inside = (lane >= base) & (lane < base + 8)
        aug = [jnp.where(inside, jnp.where(lane == base + b, 1.0, 0.0), rho[b]) for b in range(8)]
        if step < 15:
            coming = [jnp.where(inside, 0.0, row_splat(base + 8 + a)) for a in range(8)]
            start = {(a, b): lane_splat(coming[a], base + 8 + b) for a, b in pairs}
        u, t = [None] * 8, [None] * 8
        for b in range(8):
            r = lax.rsqrt(e[b, b])
            u[b], t[b] = rho[b] * r, aug[b] * r
            c = {a: e[b, a] * r for a in range(b + 1, 8)}
            for a in range(b + 1, 8):
                for a2 in range(a, 8):
                    e[a, a2] = e[a, a2] - c[a] * c[a2]
            for a in range(b + 1, 8):
                rho[a] = rho[a] - c[a] * u[b]
                aug[a] = aug[a] - c[a] * t[b]
        for b in range(8):
            upper[base + b : base + b + 1, :] = jnp.where(lane >= base + b, u[b], 0.0)[0:1]
            inverse[base + b : base + b + 1, :] = jnp.where(lane <= base + b, t[b], 0.0)[0:1]
        if step < 15:
            c = {(b, a): lane_splat(u[b], base + 8 + a) for b in range(8) for a in range(8)}
            e = {}
            for a, a2 in pairs:
                total = c[0, a] * c[0, a2]
                for b in range(1, 8):
                    total = total + c[b, a] * c[b, a2]
                e[a, a2] = start[a, a2] - total
            for a in range(8):
                total = c[0, a] * t[0]
                for b in range(1, 8):
                    total = total + c[b, a] * t[b]
                coming[a] = coming[a] - total
            rho = coming
        if step < 14:
            after = base + 16
            left, right = u[0], t[0]
            for b in range(1, 8):
                left = jnp.where(sub == b, u[b], left)
                right = jnp.where(sub == b, t[b], right)
            update = lax.dot_general(
                left, right, (((0,), (0,)), ((), ())), precision=precise, preferred_element_type=f32
            )
            rest = lax.broadcasted_iota(jnp.int32, (NB - after, NB), 1)
            cleared = jnp.where((rest >= base) & (rest < base + 8), 0.0, w[after:, :])
            w[after:, :] = cleared - update[after:, :]


def factor_kernel(ids_ref, ridge_ref, own_ref, other_ref, o_ref, a, w, upper, inverse):
    core, position = ids_ref[0], ids_ref[1]
    eye = lax.broadcasted_iota(jnp.int32, (NB, NB), 0) == lax.broadcasted_iota(jnp.int32, (NB, NB), 1)
    for which in range(2):

        @pl.when(core == which)
        def _():
            for ref, strips in ((own_ref, STRIPS[which]), (other_ref, STRIPS[1 - which])):
                slot = 0
                for strip in strips:
                    for block in range(strip, PANELS):
                        piece = ref[slot]
                        if block == strip:
                            ridge = ridge_ref[0:1, NB * strip : NB * strip + NB]
                            piece = piece + jnp.where(eye, ridge, 0.0)
                        a[NB * strip : NB * strip + NB, NB * block : NB * block + NB] = piece
                        slot += 1

    def body(panel, carry):
        at = pl.multiple_of(panel * NB, NB)
        w[...] = a[pl.ds(at, NB), pl.ds(at, NB)]
        factor_block(w, upper, inverse)
        for fixed in range(PANELS):

            @pl.when(panel == fixed)
            def _():
                s0, s1 = NB * fixed, NB * fixed + NB
                a[s0:s1, s0:s1] = upper[...]
                if fixed < PANELS - 1:
                    rows = jnp.dot(inverse[...], a[s0:s1, s1:], precision=precise, preferred_element_type=f32)
                    a[s0:s1, s1:] = rows
                    for strip in range(fixed + 1, PANELS):
                        b0, t0 = NB * (strip - fixed - 1), NB * strip
                        a[t0 : t0 + NB, t0:] = a[t0 : t0 + NB, t0:] - lax.dot_general(
                            rows[:, b0 : b0 + NB],
                            rows[:, b0:],
                            (((0,), (0,)), ((), ())),
                            precision=precise,
                            preferred_element_type=f32,
                        )

        return carry

    lax.fori_loop(0, PANELS, body, 0)
    out = a[pl.ds(pl.multiple_of(position * 8, 8), 8), :]
    lane = lax.broadcasted_iota(jnp.int32, out.shape, 1)
    o_ref[...] = jnp.where(lane >= (position // 16) * NB, out, 0.0)


def factor_rows(ids, ridge, own, other):
    return pl.pallas_call(
        factor_kernel,
        out_shape=jax.ShapeDtypeStruct((8, FEAT), f32),
        in_specs=[SMEM, VMEM, VMEM, VMEM],
        out_specs=VMEM,
        scratch_shapes=[pltpu.VMEM((FEAT, FEAT), f32)] + [pltpu.VMEM((NB, NB), f32)] * 3,
        compiler_params=params(),
        cost_estimate=pl.CostEstimate(flops=40_000_000_000, bytes_accessed=2 << 20, transcendentals=0),
    )(ids, ridge, own, other)


def swap_cores(x):
    return lax.ppermute(x, "outer", [(0, 1), (1, 0)])


def along_z(x, distance):
    return lax.ppermute(x, "inner", [(i, (i + 16 * distance) % 64) for i in range(64)])


def plane_exchange(x):
    return lax.all_to_all(x, "inner", 0, 0, axis_index_groups=PLANES, tiled=True)


def local(matrix, sign_flip, keep_list, ridge_weights):
    core, inner = lax.axis_index("outer"), lax.axis_index("inner")
    ids = jnp.stack([core, core * 64 + inner]).astype(jnp.int32)
    keep_here = lax.dynamic_index_in_dim(keep_list.reshape(2, 4, 16, 2), inner // 16, 1, False)
    keep_rows = jnp.repeat(keep_here.reshape(32, 2), 4, axis=0)
    mixed = local_mix(matrix, sign_flip)
    along = lax.all_to_all(
        mixed.reshape(4, 128, FEAT), "inner", 0, 0, axis_index_groups=Z_GROUPS, tiled=True
    )
    mine = select_rows(keep_rows, along).reshape(256, FEAT)
    theirs = swap_cores(mine)
    gram, to_send = gram_half(ids, mine, theirs)
    pieces = plane_exchange(gram.reshape(16, 144, 128))
    piece = jnp.sum(pieces, axis=0)
    piece = (piece + along_z(piece, 2)) + (along_z(piece, 1) + along_z(piece, 3))
    own = plane_exchange(jnp.broadcast_to(piece[None], (16, 144, 128))).reshape(HALF_BLOCKS, NB, NB)
    other = swap_cores(own)
    to_send, own, other = lax.optimization_barrier((to_send, own, other))
    received = plane_exchange(to_send)
    factor = factor_rows(ids, ridge_weights.reshape(1, FEAT), own, other)
    sketch = final_mix(ids, received.reshape(256, FEAT))
    return sketch, factor


def solution(mesh):
    return jax.shard_map(
        local,
        mesh=mesh,
        in_specs=(P(("outer", "inner"), None), P(("outer", "inner")), P(), P()),
        out_specs=(P(("outer", "inner"), None), P(("outer", "inner"), None)),
        check_vma=False,
    )
```

time: 735 us -> 162 us (0.22)
  other arithmetic: 369 us -> 0.16 us
  waiting for transfers between devices: 182 us -> 32.4 us
  matrix products: 100 us -> 0 us
  Pallas kernels: 0 us -> 55 us
  blocking collectives: 8.01 us -> 45 us
  between operations: 24.6 us -> 0.73 us
  local copies, waits for them, and re-layouts: 30.9 us -> 10.4 us
    another operation x61 -> x1, other arithmetic: 345 us -> 0.07 us  [local(): ids = jnp.stack([core, core * 64 + inner]).astype(jnp.int32)]
    psum x1 -> x0, waiting for transfers between devices: 134 us -> none  [local(): summed = lax.psum(local_gram, 'inner')]
    pallas_call x0 -> x5, Pallas kernels: none -> 55 us  [the longest x1 47 us: factor_rows(): pl.pallas_call(factor_kernel, out_shape=jax.ShapeDtypeStruct((8, FEAT), f...]
    dot_general x6 -> x0, matrix products: 54.4 us -> none  [the longest x1 33.1 us: join_factors(): lax.dot_general(stacked, stacked, (((0,), (0,)), ((), ())), precision=pre...]
    another operation x28 -> x0, matrix products: 45.9 us -> none  [the longest x14 23.1 us: local(): jnp.linalg.cholesky(summed + jnp.diag(ridge_weights) / n_outer)]
    all_to_all x1 -> x2, blocking collectives: 8.01 us -> 45 us  [plane_exchange(): lax.all_to_all(x, 'inner', 0, 0, axis_index_groups=PLANES, tiled=True)]
    all_gather x1 -> x0, waiting for transfers between devices: 20.5 us -> none  [joined(): gathered = lax.all_gather(part, axis)]
    div x2 -> x0, other arithmetic: 8.88 us -> none  [the longest x1 4.45 us: local(): jnp.linalg.cholesky(summed + jnp.diag(ridge_weights) / n_outer)]
  transfers between devices with their start and end apart: 3 -> 7, of which waited for: 3 -> 5; matrix products, arithmetic and copies ran while one was open for 0% -> 0% of each run, Pallas kernels for 0% -> 29%
where the time goes in v1:
time: 162 us; the launch traced here: 161 us
  Pallas kernels  55 us (34%)
  blocking collectives  45 us (28%)
  waiting for transfers between devices  32.4 us (20%)
  starting transfers between devices  17.7 us (11%)
  local copies, waits for them, and re-layouts  10.4 us (6%)
    pallas_call x1, Pallas kernels, factor_rows(): pl.pallas_call(factor_kernel, out_shape=jax.ShapeDtypeStruct((8, FEAT), f...  47 us
    all_to_all x2, blocking collectives, plane_exchange(): lax.all_to_all(x, 'inner', 0, 0, axis_index_groups=PLANES, tiled=True)  45 us
    all_to_all x1, waiting for transfers between devices, local(): lax.all_to_all(mixed.reshape(4, 128, FEAT), 'inner', 0, 0, axis_index_gro...  25.2 us
    unnamed x24, local copies, waits for them, and re-layouts  10.1 us
    all_to_all x1, starting transfers between devices, local(): lax.all_to_all(mixed.reshape(4, 128, FEAT), 'inner', 0, 0, axis_index_gro...  5.99 us
    ppermute x2, starting transfers between devices, swap_cores(): return lax.ppermute(x, 'outer', [(0, 1), (1, 0)])  4.99 us
    ppermute x2, waiting for transfers between devices, swap_cores(): return lax.ppermute(x, 'outer', [(0, 1), (1, 0)])  4.69 us
    all_to_all x1, starting transfers between devices, plane_exchange(): lax.all_to_all(x, 'inner', 0, 0, axis_index_groups=PLANES, tiled=True)  3.66 us
  transfers between devices with their start and end apart: 7, of which 5 were waited for; matrix products, arithmetic and copies ran while one was open for 0% of the time, Pallas kernels for 29%

profile of v1, /device:TPU:1, one launch (start us, length us, event | category | flops | bytes accessed | tf_op | source)
XLA Modules:
  0.0 161.5 jit_solution(13972684637625699284)
XLA Ops:
  0.6 1.6 copy-done.1
  2.2 1.0 copy-done.5
  3.9 2.2 %shard_map.77 = f32[512,1024]{1,0:T(8,128)S(1)} custom-call(bf16[512,512]{1,0:T(8,128)(2,1)S(1)} %copy-done.5, s32[1,512]{1,0:T(1,128)S(1)} %bitcast.22, f32[512,1024]{1,0:T(8,128)S(1)} %copy-done.1), custom_call_target="tpu_custom_call" | custom-call | tf_op jit(solution)/shard_map/pallas_call | solution.py:75
  6.2 1.3 copy-done
  7.5 6.0 %all-to-all-start = ((f32[4,128,1024]{2,1,0:T(8,128)}), f32[4,128,1024]{2,1,0:T(8,128)S(1)}, u32[]{:S(2)}, u32[]{:S(2)}) async-start(f32[4,128,1024]{2,1,0:T(8,128)} %bitcast.14), calls=%async_computation | async-start | bytes 4194304 | tf_op jit(solution)/shard_map/all_to_all | solution.py:331
  13.7 25.2 %all-to-all-done.y_ref = f32[4,128,1024]{2,1,0:T(8,128)S(1)} async-done(((f32[4,128,1024]{2,1,0:T(8,128)}), f32[4,128,1024]{2,1,0:T(8,128)S(1)}, u32[]{:S(2)}, u32[]{:S(2)}) %all-to-all-start) | async-done | bytes 2097184 | tf_op jit(solution)/shard_map/all_to_all | solution.py:331
  39.9 1.9 %collective-permute-start = (f32[256,1024]{1,0:T(8,128)S(1)}, f32[256,1024]{1,0:T(8,128)S(1)}, u32[]{:S(2)}, u32[]{:S(2)}) collective-permute-start(f32[256,1024]{1,0:T(8,128)S(1)} %bitcast.15), channel_id=1, source_target_pairs={{0,64},{64,0},{1,65},{65,1},{2,66},{66,2},{3,67},{67,3},{4,68},{68... | collective-permute-start | bytes 3145736 | tf_op jit(solution)/shard_map/ppermute | solution.py:314
  41.9 2.2 %collective-permute-done.w_ref = f32[256,1024]{1,0:T(8,128)S(1)} collective-permute-done((f32[256,1024]{1,0:T(8,128)S(1)}, f32[256,1024]{1,0:T(8,128)S(1)}, u32[]{:S(2)}, u32[]{:S(2)}) %collective-permute-start) | collective-permute-done | bytes 1048608 | tf_op jit(solution)/shard_map/ppermute | solution.py:314
  44.1 1.0 copy-done.2
  45.1 1.2 copy-done.3
  46.3 2.1 %shard_map.79 = (f32[18,128,128]{2,1,0:T(8,128)S(1)}, f32[16,2,8,1024]{3,2,1,0:T(8,128)S(1)}) custom-call(s32[2]{0:T(128)S(1)} %pad_add_fusion.ids_ref, f32[256,1024]{1,0:T(8,128)S(1)} %bitcast.16, f32[256,1024]{1,0:T(8,128)S(1)} %copy-done.3), custom_call_target="tpu_custom_call" | custom-call | tf_op jit(solution)/shard_map/pallas_call | solution.py:151
  48.4 1.0 copy-done.4
  49.4 24.6 %all_to_all.20 = f32[16,144,128]{2,1,0:T(8,128)S(1)} all-to-all(f32[16,144,128]{2,1,0:T(8,128)S(1)} %bitcast.20), channel_id=1, replica_groups={{0,1,2,3,4,5,6,7,8,9,10,11,12,13,14,15},{16,17,18,19,20,21,22,23,24,25,..., dimensions={0} | all-to-all | bytes 2359296 | tf_op jit(solution)/shard_map/all_to_all | solution.py:322
  74.4 1.2 collective-permute-start.2
  75.6 1.5 collective-permute-start.3
  77.1 1.9 %collective-permute-done.1 = f32[144,128]{1,0:T(8,128)S(1)} collective-permute-done((f32[144,128]{1,0:T(8,128)S(1)}, f32[144,128]{1,0:T(8,128)S(1)}, u32[]{:S(2)}, u32[]{:S(2)}) %collective-permute-start.1) | collective-permute-done | bytes 73760 | tf_op jit(solution)/shard_map/ppermute | solution.py:318
  79.8 20.4 %all_to_all.21 = f32[16,144,128]{2,1,0:T(8,128)S(1)} all-to-all(f32[16,144,128]{2,1,0:T(8,128)S(1)} %broadcast_in_dim.10), channel_id=1, replica_groups={{0,1,2,3,4,5,6,7,8,9,10,11,12,13,14,15},{16,17,18,19,20,21,22,23,24,25,..., dimensions={0} | all-to-all | bytes 2359296 | tf_op jit(solution)/shard_map/all_to_all | solution.py:322
  100.2 3.0 %collective-permute-start.4 = (f32[18,128,128]{2,1,0:T(8,128)S(1)}, f32[18,128,128]{2,1,0:T(8,128)S(1)}, u32[]{:S(2)}, u32[]{:S(2)}) collective-permute-start(f32[18,128,128]{2,1,0:T(8,128)S(1)} %bitcast.18), channel_id=1, source_target_pairs={{0,64},{64,0},{1,65},{65,1},{2,66},{66,2},{3,67},{67,3},{4,68},{68... | collective-permute-start | bytes 3538952 | tf_op jit(solution)/shard_map/ppermute | solution.py:314
  103.2 2.5 %collective-permute-done.4.other_ref = f32[18,128,128]{2,1,0:T(8,128)S(1)} collective-permute-done((f32[18,128,128]{2,1,0:T(8,128)S(1)}, f32[18,128,128]{2,1,0:T(8,128)S(1)}, u32[]{:S(2)}, u32[]{:S(2)}) %collective-permute-start.4) | collective-permute-done | bytes 1179680 | tf_op jit(solution)/shard_map/ppermute | solution.py:314
  105.7 1.0 copy-done.8
  106.8 3.7 %all-to-all-start.3 = ((f32[16,2,8,1024]{3,2,1,0:T(8,128)}), f32[16,2,8,1024]{3,2,1,0:T(8,128)S(1)}, u32[]{:S(2)}, u32[]{:S(2)}) async-start(f32[16,2,8,1024]{3,2,1,0:T(8,128)} %copy-done.4), calls=%async_computation.3 | async-start | bytes 2097152 | tf_op jit(solution)/shard_map/all_to_all | solution.py:322
  110.4 1.3 copy-done.9
  111.7 47.0 %shard_map.81 = f32[8,1024]{1,0:T(8,128)} custom-call(s32[2]{0:T(128)S(1)} %pad_add_fusion.ids_ref, f32[1,1024]{1,0:T(1,128)S(1)} %bitcast.23, f32[18,128,128]{2,1,0:T(8,128)S(1)} %bitcast.19, f32[18,128,128]{2,1,0:T(8,128)S(1)} %copy-done.9), custom_call_target="tpu_custom_call" | custom-call | flops 40000000000 | bytes 2097152 | tf_op jit(solution)/shard_map/pallas_call | solution.py:302
  158.7 2.7 %shard_map.80 = f32[256,1024]{1,0:T(8,128)} custom-call(s32[2]{0:T(128)S(1)} %pad_add_fusion.ids_ref, bf16[256,256]{1,0:T(8,128)(2,1)S(1)} %copy-done.6, f32[256,1024]{1,0:T(8,128)S(1)} %bitcast.17), custom_call_target="tpu_custom_call" | custom-call | tf_op jit(solution)/shard_map/pallas_call | solution.py:175
  (29 shorter events, 3.1 us)
Async XLA Ops:
  0.6 1.6 copy-start.1
  2.2 1.0 copy-start.5
  3.3 0.7 copy-start.7
  6.1 1.3 copy-start
  7.5 6.0 %copy-start.11 = (s32[128,2]{0,1:T(2,128)S(1)}, s32[128,2]{0,1:T(2,128)}, u32[]{:S(2)}) copy-start(s32[128,2]{0,1:T(2,128)} %param.8) | copy-start | bytes 3076
  7.5 31.4 %all-to-all-start = ((f32[4,128,1024]{2,1,0:T(8,128)}), f32[4,128,1024]{2,1,0:T(8,128)S(1)}, u32[]{:S(2)}, u32[]{:S(2)}) async-start(f32[4,128,1024]{2,1,0:T(8,128)} %bitcast.14), calls=%async_computation | async-start | bytes 4194304 | tf_op jit(solution)/shard_map/all_to_all | solution.py:331
  39.9 4.2 %collective-permute-start = (f32[256,1024]{1,0:T(8,128)S(1)}, f32[256,1024]{1,0:T(8,128)S(1)}, u32[]{:S(2)}, u32[]{:S(2)}) collective-permute-start(f32[256,1024]{1,0:T(8,128)S(1)} %bitcast.15), channel_id=1, source_target_pairs={{0,64},{64,0},{1,65},{65,1},{2,66},{66,2},{3,67},{67,3},{4,68},{68... | collective-permute-start | bytes 3145736 | tf_op jit(solution)/shard_map/ppermute | solution.py:314
  44.1 1.0 copy-start.2
  45.1 1.2 copy-start.3
  48.4 1.0 copy-start.4
  74.1 4.9 %collective-permute-start.1 = (f32[144,128]{1,0:T(8,128)S(1)}, f32[144,128]{1,0:T(8,128)S(1)}, u32[]{:S(2)}, u32[]{:S(2)}) collective-permute-start(f32[144,128]{1,0:T(8,128)S(1)} %reduce_sum.9), channel_id=1, source_target_pairs={{0,32},{1,33},{2,34},{3,35},{4,36},{5,37},{6,38},{7,39},{8,40},{9,... | collective-permute-start | bytes 221192 | tf_op jit(solution)/shard_map/ppermute | solution.py:318
  74.4 5.2 %collective-permute-start.2 = (f32[144,128]{1,0:T(8,128)S(1)}, f32[144,128]{1,0:T(8,128)S(1)}, u32[]{:S(2)}, u32[]{:S(2)}) collective-permute-start(f32[144,128]{1,0:T(8,128)S(1)} %reduce_sum.9), channel_id=1, source_target_pairs={{0,16},{1,17},{2,18},{3,19},{4,20},{5,21},{6,22},{7,23},{8,24},{9,... | collective-permute-start | bytes 221192 | tf_op jit(solution)/shard_map/ppermute | solution.py:318
  75.6 4.0 %collective-permute-start.3 = (f32[144,128]{1,0:T(8,128)S(1)}, f32[144,128]{1,0:T(8,128)S(1)}, u32[]{:S(2)}, u32[]{:S(2)}) collective-permute-start(f32[144,128]{1,0:T(8,128)S(1)} %reduce_sum.9), channel_id=1, source_target_pairs={{0,48},{1,49},{2,50},{3,51},{4,52},{5,53},{6,54},{7,55},{8,56},{9,... | collective-permute-start | bytes 221192 | tf_op jit(solution)/shard_map/ppermute | solution.py:318
  100.2 10.2 %copy-start.10 = (f32[1024]{0:T(1024)S(1)}, f32[1024]{0:T(1024)}, u32[]{:S(2)}) copy-start(f32[1024]{0:T(1024)} %param.9) | copy-start | bytes 12292
  100.2 5.5 %collective-permute-start.4 = (f32[18,128,128]{2,1,0:T(8,128)S(1)}, f32[18,128,128]{2,1,0:T(8,128)S(1)}, u32[]{:S(2)}, u32[]{:S(2)}) collective-permute-start(f32[18,128,128]{2,1,0:T(8,128)S(1)} %bitcast.18), channel_id=1, source_target_pairs={{0,64},{64,0},{1,65},{65,1},{2,66},{66,2},{3,67},{67,3},{4,68},{68... | collective-permute-start | bytes 3538952 | tf_op jit(solution)/shard_map/ppermute | solution.py:314
  105.7 1.1 copy-start.8
  106.8 52.0 %all-to-all-start.3 = ((f32[16,2,8,1024]{3,2,1,0:T(8,128)}), f32[16,2,8,1024]{3,2,1,0:T(8,128)S(1)}, u32[]{:S(2)}, u32[]{:S(2)}) async-start(f32[16,2,8,1024]{3,2,1,0:T(8,128)} %copy-done.4), calls=%async_computation.3 | async-start | bytes 2097152 | tf_op jit(solution)/shard_map/all_to_all | solution.py:322
  110.4 1.3 copy-start.9
  111.7 47.0 %copy-start.6 = (bf16[256,256]{1,0:T(8,128)(2,1)S(1)}, bf16[256,256]{1,0:T(8,128)(2,1)}, u32[]{:S(2)}) copy-start(bf16[256,256]{1,0:T(8,128)(2,1)} %constant.38.clone.table_ref) | copy-start | bytes 393220

commit v2 on v1

v2 whole, which is shorter than its diff:
```python
import jax
import jax.numpy as jnp
import numpy as np
from jax import lax
from jax.experimental import pallas as pl
from jax.experimental.pallas import tpu as pltpu
from jax.sharding import PartitionSpec as P

precise = lax.Precision.HIGHEST
f32 = jnp.float32
bf16 = jnp.bfloat16
VMEM = pl.BlockSpec(memory_space=pltpu.VMEM)
SMEM = pl.BlockSpec(memory_space=pltpu.SMEM)
FEAT = 1024
NB = 128
HALF = FEAT // 2
PAIRS = ((0, 3), (1, 2))
Z_GROUPS = [[i + 16 * j for j in range(4)] for i in range(16)]
PLANES = [[16 * j + i for i in range(16)] for j in range(4)]


def params(mib=48):
    return pltpu.CompilerParams(vmem_limit_bytes=mib << 20)


def parity_sign(left, right):
    common = left & right
    parity = np.zeros_like(common)
    for shift_by in range(10):
        parity ^= (common >> shift_by) & 1
    return 1 - 2 * parity


def local_table():
    az, c, axy, e = np.meshgrid(range(4), range(2), range(16), range(4), indexing="ij")
    k = (az * 128 + axy * 8 + c * 4 + e).reshape(-1, 1)
    return parity_sign(k, np.arange(512)[None, :]).astype(np.float32).astype(bf16)


def final_table():
    j, i, o, e = (v.reshape(-1, 1) for v in np.meshgrid(range(2), range(16), range(2), range(4), indexing="ij"))
    ip, op, jp, ep = (v.reshape(1, -1) for v in np.meshgrid(range(16), range(2), range(2), range(4), indexing="ij"))
    table = parity_sign(i, ip) * parity_sign(o, op) * (j == jp) * (e == ep)
    return table.astype(np.float32).astype(bf16)


def halves(x):
    high = x.astype(bf16)
    return high, (x - high.astype(f32)).astype(bf16)


def mm(a, b):
    return jnp.dot(a, b, preferred_element_type=f32)


def tmm(a, b):
    return lax.dot_general(a, b, (((0,), (0,)), ((), ())), preferred_element_type=f32)


def turn(index, step):
    return (index + step) & 3


def local_mix_kernel(ids_ref, table_ref, sign_ref, x_ref, *rest):
    outs, signed = rest[:4], rest[4]

    @pl.when(pl.program_id(0) == 0)
    def _():
        signed[...] = (table_ref[...].astype(f32) * (sign_ref[...].astype(f32) * 2.0**-13)).astype(bf16)

    high, low = halves(x_ref[...])
    for step in range(4):
        rows = signed[pl.ds(pl.multiple_of(turn(ids_ref[4], step) * 128, 128), 128), :]
        outs[step][...] = mm(rows, high) + mm(rows, low)


def local_mix(ids, table, signs, matrix, half):
    rows = matrix.shape[0]
    cols = 256
    return pl.pallas_call(
        local_mix_kernel,
        grid=(HALF // cols,),
        out_shape=(jax.ShapeDtypeStruct((128, HALF), f32),) * 4,
        in_specs=[
            SMEM,
            pl.BlockSpec((rows, rows), lambda g: (0, 0)),
            pl.BlockSpec((1, rows), lambda g: (0, 0)),
            pl.BlockSpec((rows, cols), lambda g: (0, g + half * (HALF // cols))),
        ],
        out_specs=(pl.BlockSpec((128, cols), lambda g: (0, g)),) * 4,
        scratch_shapes=[pltpu.VMEM((rows, rows), bf16)],
        compiler_params=params(),
    )(ids, table, signs, matrix)


def select_kernel(ids_ref, keep_ref, y0_ref, y1_ref, y2_ref, y3_ref, v_ref):
    parts = [ref[...] for ref in (y0_ref, y1_ref, y2_ref, y3_ref)]
    shape = parts[0].shape

    def combo(which):
        total = None
        for step, part in enumerate(parts):
            common = which & turn(ids_ref[4], 4 - step)
            sign = (1 - 2 * ((common ^ (common >> 1)) & 1)).astype(f32)
            term = part * jnp.broadcast_to(sign, shape)
            total = term if total is None else total + term
        return total

    v0, v1 = combo(keep_ref[:, 0:1]), combo(keep_ref[:, 1:2])
    upper = (lax.broadcasted_iota(jnp.int32, shape, 0) & 7) < 4
    even = jnp.where(upper, v0, pltpu.roll(v1, 4, axis=0))
    odd = jnp.where(upper, pltpu.roll(v0, shape[0] - 4, axis=0), v1)
    v_ref[:, 0] = even.reshape(16, 8, shape[1])
    v_ref[:, 1] = odd.reshape(16, 8, shape[1])


def select_rows(ids, keep_rows, parts):
    cols = 256
    features = parts[0].shape[1]
    return pl.pallas_call(
        select_kernel,
        grid=(features // cols,),
        out_shape=jax.ShapeDtypeStruct((16, 2, 8, features), f32),
        in_specs=[SMEM, pl.BlockSpec((128, 2), lambda g: (0, 0))]
        + [pl.BlockSpec((128, cols), lambda g: (0, g))] * 4,
        out_specs=pl.BlockSpec((16, 2, 8, cols), lambda g: (0, 0, 0, g)),
        compiler_params=params(),
    )(ids, keep_rows, *parts)


def load_halves(mine_ref, theirs_ref, high, low):
    for part, ref in enumerate((mine_ref, theirs_ref)):
        h, l = halves(ref[...])
        high[256 * part : 256 * part + 256, :] = h
        low[256 * part : 256 * part + 256, :] = l


def strip_blocks(left, right, at, start, g_ref, slot):
    high, low = left
    high_right, low_right = right
    h, l = high[:, at : at + NB], low[:, at : at + NB]
    total = tmm(h, high_right[:, start:]) + (tmm(h, low_right[:, start:]) + tmm(l, high_right[:, start:]))
    for block in range((HALF - start) // NB):
        row = NB * (slot + block)
        g_ref[row : row + NB, :] = total[:, NB * block : NB * block + NB]
    return slot + (HALF - start) // NB


def first_gram_kernel(ids_ref, v_ref, w_ref, *rest):
    outs, (high, low, blocks) = rest[:4], rest[4:]
    load_halves(v_ref, w_ref, high, low)
    for which, strips in enumerate(PAIRS):

        @pl.when(ids_ref[0] == which)
        def _():
            slot = 0
            for strip in strips:
                slot = strip_blocks((high, low), (high, low), NB * strip, NB * strip, blocks, slot)

    for step in range(4):
        outs[step][...] = blocks[pl.ds(pl.multiple_of(turn(ids_ref[2], step) * 160, 8), 160), :]


def sum_split_kernel(ids_ref, *rest):
    parts, outs, total = rest[:4], rest[4:8], rest[8]
    total[...] = (parts[0][...] + parts[1][...]) + (parts[2][...] + parts[3][...])
    for step in range(4):
        outs[step][...] = total[pl.ds(pl.multiple_of(turn(ids_ref[3], step) * 40, 8), 40), :]


def sum_split(ids, parts):
    return pl.pallas_call(
        sum_split_kernel,
        out_shape=(jax.ShapeDtypeStruct((40, NB), f32),) * 4,
        in_specs=[SMEM] + [VMEM] * 4,
        out_specs=(VMEM,) * 4,
        scratch_shapes=[pltpu.VMEM((160, NB), f32)],
        compiler_params=params(),
    )(ids, *parts)


def second_gram_kernel(ids_ref, v1_ref, w1_ref, v2_ref, w2_ref, g_ref, s_ref, high1, low1, high2, low2):
    load_halves(v1_ref, w1_ref, high1, low1)
    load_halves(v2_ref, w2_ref, high2, low2)
    own = pl.ds(pl.multiple_of(ids_ref[0] * 128, 128), 128)
    for half, refs in enumerate(((v1_ref, w1_ref), (v2_ref, w2_ref))):
        for part, ref in enumerate(refs):
            s_ref[:, part, :, half * HALF : half * HALF + HALF] = ref[own, :].reshape(16, 8, HALF)
    for which, strips in enumerate(PAIRS):

        @pl.when(ids_ref[0] == which)
        def _():
            slot = 0
            for strip in strips:
                slot = strip_blocks((high1, low1), (high2, low2), NB * strip, 0, g_ref, slot)
            for strip in strips:
                slot = strip_blocks((high2, low2), (high2, low2), NB * strip, NB * strip, g_ref, slot)


def first_gram(ids, mine, theirs):
    return pl.pallas_call(
        first_gram_kernel,
        out_shape=(jax.ShapeDtypeStruct((160, NB), f32),) * 4,
        in_specs=[SMEM, VMEM, VMEM],
        out_specs=(VMEM,) * 4,
        scratch_shapes=[pltpu.VMEM((512, HALF), bf16)] * 2 + [pltpu.VMEM((5 * NB, NB), f32)],
        compiler_params=params(),
    )(ids, mine, theirs)


def second_gram(ids, mine1, theirs1, mine2, theirs2):
    return pl.pallas_call(
        second_gram_kernel,
        out_shape=(
            jax.ShapeDtypeStruct((13 * NB, NB), f32),
            jax.ShapeDtypeStruct((16, 2, 8, FEAT), f32),
        ),
        in_specs=[SMEM] + [VMEM] * 4,
        out_specs=(VMEM, VMEM),
        scratch_shapes=[pltpu.VMEM((512, HALF), bf16)] * 4,
        compiler_params=params(),
    )(ids, mine1, theirs1, mine2, theirs2)


def final_kernel(ids_ref, table_ref, r_ref, o_ref):
    high, low = halves(r_ref[...])
    total = mm(table_ref[...], high) + mm(table_ref[...], low)
    odd = (lax.broadcasted_iota(jnp.int32, total.shape, 0) >> 2) & 1
    flip = (odd * ids_ref[0]) == 1
    o_ref[...] = total * jnp.where(flip, -32.0, 32.0)


def final_mix(ids, received):
    rows, features = received.shape
    cols = 256
    return pl.pallas_call(
        final_kernel,
        grid=(features // cols,),
        out_shape=jax.ShapeDtypeStruct((rows, features), f32),
        in_specs=[
            SMEM,
            pl.BlockSpec((rows, rows), lambda g: (0, 0)),
            pl.BlockSpec((rows, cols), lambda g: (0, g)),
        ],
        out_specs=pl.BlockSpec((rows, cols), lambda g: (0, g)),
        compiler_params=params(),
    )(ids, jnp.asarray(final_table()), received)


def lane_splat(x, lane):
    return jnp.broadcast_to(x[:, lane : lane + 1], (8, NB))


def thirds(x):
    high = x.astype(bf16).astype(f32)
    rest = x - high
    middle = rest.astype(bf16).astype(f32)
    return high, middle, rest - middle


def outer_sum(left, right):
    lh, lm, ll = thirds(left)
    rh, rm, rl = thirds(right)
    stacked_left = jnp.concatenate([lh, lh, lh, lm, lm, ll], axis=0).astype(bf16)
    stacked_right = jnp.concatenate([rh, rm, rl, rh, rm, rh], axis=0).astype(bf16)
    return tmm(stacked_left, stacked_right)


def tree_sum(terms):
    while len(terms) > 1:
        terms = [x + y for x, y in zip(terms[::2], terms[1::2])]
    return terms[0]


def factor_block(w, upper, inverse):
    lane = lax.broadcasted_iota(jnp.int32, (8, NB), 1)
    sub = lax.broadcasted_iota(jnp.int32, (8, NB), 0)
    pairs = [(a, b) for a in range(8) for b in range(a, 8)]

    def row_splat(row):
        return jnp.broadcast_to(w[row : row + 1, :], (8, NB))

    rho = [row_splat(b) for b in range(8)]
    e = {(a, b): lane_splat(rho[a], b) for a, b in pairs}
    for step in range(16):
        base = 8 * step
        inside = (lane >= base) & (lane < base + 8)
        aug = [jnp.where(inside, jnp.where(lane == base + b, 1.0, 0.0), rho[b]) for b in range(8)]
        u, t = [None] * 8, [None] * 8
        for b in range(8):
            r = lax.rsqrt(e[b, b])
            u[b], t[b] = rho[b] * r, aug[b] * r
            c = {a: e[b, a] * r for a in range(b + 1, 8)}
            for a in range(b + 1, 8):
                for a2 in range(a, 8):
                    e[a, a2] = e[a, a2] - c[a] * c[a2]
            for a in range(b + 1, 8):
                rho[a] = rho[a] - c[a] * u[b]
                aug[a] = aug[a] - c[a] * t[b]
        left, right = u[0], t[0]
        for b in range(1, 8):
            left = jnp.where(sub == b, u[b], left)
            right = jnp.where(sub == b, t[b], right)
        upper[base : base + 8, :] = jnp.where(lane >= base + sub, left, 0.0)
        inverse[base : base + 8, :] = jnp.where(lane <= base + sub, right, 0.0)
        if step == 15:
            break
        if step < 14:
            update = outer_sum(left, right)
        coming = [jnp.where(inside, 0.0, row_splat(base + 8 + a)) for a in range(8)]
        c = {(b, a): lane_splat(u[b], base + 8 + a) for b in range(8) for a in range(8)}
        e = {(a, a2): lane_splat(coming[a], base + 8 + a2) for a, a2 in pairs}
        e = {(a, a2): e[a, a2] - tree_sum([c[b, a] * c[b, a2] for b in range(8)]) for a, a2 in pairs}
        rho = [coming[a] - tree_sum([c[b, a] * t[b] for b in range(8)]) for a in range(8)]
        if step < 14:
            after = base + 16
            rest = lax.broadcasted_iota(jnp.int32, (NB - after, NB), 1)
            cleared = jnp.where((rest >= base) & (rest < base + 8), 0.0, w[after:, :])
            w[after:, :] = cleared - update[after:, :]


def place(ref, slot, a, strip, block, ridge_ref):
    piece = ref[NB * slot : NB * slot + NB, :]
    if ridge_ref is not None and strip == block:
        rows = lax.broadcasted_iota(jnp.int32, (NB, NB), 0)
        cols = lax.broadcasted_iota(jnp.int32, (NB, NB), 1)
        piece = piece + jnp.where(rows == cols, ridge_ref[0:1, NB * strip : NB * strip + NB], 0.0)
    a[NB * strip : NB * strip + NB, NB * block : NB * block + NB] = piece


def highest(left, right, contract):
    return lax.dot_general(
        left, right, ((contract, (0,)), ((), ())), precision=precise, preferred_element_type=f32
    )


def panels(a, w, upper, inverse, first, last, inv_ref=None):
    count = HALF // NB

    def body(panel, carry):
        at = pl.multiple_of(panel * NB, NB)
        w[...] = a[pl.ds(at, NB), pl.ds(at, NB)]
        factor_block(w, upper, inverse)
        if inv_ref is not None:
            inv_ref[panel - first] = inverse[...]
        for fixed in range(first, last):

            @pl.when(panel == fixed)
            def _():
                s0, s1 = NB * fixed, NB * fixed + NB
                a[s0:s1, s0:s1] = upper[...]
                if fixed < count - 1:
                    rows = highest(inverse[...], a[s0:s1, s1:], (1,))
                    a[s0:s1, s1:] = rows
                    for strip in range(fixed + 1, count):
                        b0, t0 = NB * (strip - fixed - 1), NB * strip
                        update = highest(rows[:, b0 : b0 + NB], rows[:, b0:], (0,))
                        a[t0 : t0 + NB, t0:] = a[t0 : t0 + NB, t0:] - update

        return carry

    lax.fori_loop(first, last, body, 0)


def first_factor_kernel(ids_ref, ridge_ref, own_rel, other_rel, a, inv_ref, own_ref, other_ref, w, upper, inverse):
    for back_x in range(4):
        for back_y in range(4):
            source = 160 * back_x + 40 * back_y
            row = turn(ids_ref[2], 4 - back_x) * 160 + turn(ids_ref[3], 4 - back_y) * 40
            target = pl.ds(pl.multiple_of(row, 8), 40)
            own_ref[target, :] = own_rel[source : source + 40, :]
            other_ref[target, :] = other_rel[source : source + 40, :]
    for which in range(2):

        @pl.when(ids_ref[0] == which)
        def _():
            for ref, strips in ((own_ref, PAIRS[which]), (other_ref, PAIRS[1 - which])):
                slot = 0
                for strip in strips:
                    for block in range(strip, 4):
                        place(ref, slot, a, strip, block, ridge_ref)
                        slot += 1

    panels(a, w, upper, inverse, 0, 2, inv_ref)


def middle_factor_kernel(given_ref, a, inv_ref, w, upper, inverse):
    a[...] = given_ref[...]
    panels(a, w, upper, inverse, 2, 4, inv_ref)


def last_factor_kernel(ids_ref, ridge_ref, own_ref, other_ref, u_ref, inv1_ref, inv2_ref, o_ref, r, a, w, upper, inverse):
    position = ids_ref[1]
    for which in range(2):

        @pl.when(ids_ref[0] == which)
        def _():
            for ref, strips in ((own_ref, PAIRS[which]), (other_ref, PAIRS[1 - which])):
                slot = 0
                for strip in strips:
                    for block in range(4):
                        place(ref, slot, r, strip, block, None)
                        slot += 1
                for strip in strips:
                    for block in range(strip, 4):
                        place(ref, slot, a, strip, block, ridge_ref)
                        slot += 1

    for panel in range(4):
        at = NB * panel
        rows = r[at : at + NB, :]
        if panel:
            rows = rows - highest(u_ref[:at, at : at + NB], r[:at, :], (0,))
        inv_ref = (inv1_ref, inv2_ref)[panel // 2]
        r[at : at + NB, :] = highest(inv_ref[panel % 2], rows, (1,))
    for strip in range(4):
        at = NB * strip
        update = highest(r[:, at : at + NB], r[:, at:], (0,))
        a[at : at + NB, at:] = a[at : at + NB, at:] - update
    panels(a, w, upper, inverse, 0, 4)
    lane = lax.broadcasted_iota(jnp.int32, (8, HALF), 1)
    row = pl.multiple_of((position % 64) * 8, 8)
    edge = ((position % 64) // 16) * NB

    @pl.when(position < 64)
    def _():
        o_ref[:, :HALF] = jnp.where(lane >= edge, u_ref[pl.ds(row, 8), :], 0.0)
        o_ref[:, HALF:] = r[pl.ds(row, 8), :]

    @pl.when(position >= 64)
    def _():
        o_ref[:, :HALF] = jnp.zeros((8, HALF), f32)
        o_ref[:, HALF:] = jnp.where(lane >= edge, a[pl.ds(row, 8), :], 0.0)


BLOCK_SCRATCH = [pltpu.VMEM((NB, NB), f32)] * 3
SQUARE = jax.ShapeDtypeStruct((HALF, HALF), f32)
INVERSES = jax.ShapeDtypeStruct((2, NB, NB), f32)


def cost(us):
    return pl.CostEstimate(flops=us * 1_000_000_000, bytes_accessed=2 << 20, transcendentals=0)


def first_factor(ids, ridge, own, other):
    return pl.pallas_call(
        first_factor_kernel,
        out_shape=(SQUARE, INVERSES),
        in_specs=[SMEM, VMEM, VMEM, VMEM],
        out_specs=(VMEM, VMEM),
        scratch_shapes=[pltpu.VMEM((5 * NB, NB), f32)] * 2 + BLOCK_SCRATCH,
        compiler_params=params(),
        cost_estimate=cost(12),
    )(ids, ridge, own, other)


def middle_factor(given):
    return pl.pallas_call(
        middle_factor_kernel,
        out_shape=(SQUARE, INVERSES),
        in_specs=[VMEM],
        out_specs=(VMEM, VMEM),
        scratch_shapes=BLOCK_SCRATCH,
        compiler_params=params(),
        cost_estimate=cost(12),
    )(given)


def last_factor(ids, ridge, own, other, u, inv1, inv2):
    return pl.pallas_call(
        last_factor_kernel,
        out_shape=jax.ShapeDtypeStruct((8, FEAT), f32),
        in_specs=[SMEM] + [VMEM] * 6,
        out_specs=VMEM,
        scratch_shapes=[pltpu.VMEM((HALF, HALF), f32)] * 2 + BLOCK_SCRATCH,
        compiler_params=params(),
        cost_estimate=cost(30),
    )(ids, ridge, own, other, u, inv1, inv2)


def swap_cores(x):
    return lax.ppermute(x, "outer", [(0, 1), (1, 0)])


def along(axis, x, distance):
    stride = {"x": 1, "y": 4, "z": 16}[axis]
    pairs = []
    for source in range(64):
        digit = source // stride % 4
        pairs.append((source, source + ((digit + distance) % 4 - digit) * stride))
    return lax.ppermute(x, "inner", pairs)


def exchange(axis, parts):
    return [parts[0]] + [along(axis, parts[step], step) for step in (1, 3, 2)]


def in_order(parts):
    return [parts[0], parts[1], parts[3], parts[2]]


def shared(axis, x):
    return in_order(exchange(axis, [x] * 4))


def scattered(axis, parts):
    return in_order(exchange(axis, parts))


def total(parts):
    return (parts[0] + parts[2]) + (parts[1] + parts[3])


def plane_exchange(x):
    return lax.all_to_all(x, "inner", 0, 0, axis_index_groups=PLANES, tiled=True)


def copies(piece):
    return jnp.broadcast_to(piece[None], (16,) + piece.shape)


def local(matrix, sign_flip, keep_list, ridge_weights):
    core, inner = lax.axis_index("outer"), lax.axis_index("inner")
    ids = jnp.stack([core, core * 64 + inner, inner & 3, (inner >> 2) & 3, inner >> 4]).astype(jnp.int32)
    keep_here = lax.dynamic_index_in_dim(keep_list.reshape(2, 4, 16, 2), inner >> 4, 1, False)
    keep_rows = jnp.repeat(keep_here.reshape(32, 2), 4, axis=0)
    table, signs = jnp.asarray(local_table()), sign_flip.reshape(1, -1)
    ridge = ridge_weights.reshape(1, FEAT)

    along1 = scattered("z", local_mix(ids, table, signs, matrix, 0))
    mixed2 = local_mix(ids, table, signs, matrix, 1)
    along1, mixed2 = lax.optimization_barrier((along1, mixed2))
    along2 = scattered("z", mixed2)
    mine1 = select_rows(ids, keep_rows, along1).reshape(256, HALF)
    theirs1 = swap_cores(mine1)
    by_y = sum_split(ids, scattered("x", first_gram(ids, mine1, theirs1)))
    piece1 = total(scattered("y", by_y))
    piece1 = total(shared("z", piece1))
    row1 = jnp.concatenate(shared("y", piece1), axis=0)
    own1 = jnp.concatenate(shared("x", row1), axis=0)
    other1 = swap_cores(own1)

    mine2 = select_rows(ids, keep_rows, along2).reshape(256, HALF)
    theirs2 = swap_cores(mine2)
    gram2, to_send = second_gram(ids, mine1, theirs1, mine2, theirs2)
    piece2 = jnp.sum(plane_exchange(gram2.reshape(16, 104, 128)), axis=0)
    piece2 = total(shared("z", piece2))
    own2 = plane_exchange(copies(piece2)).reshape(13 * NB, NB)

    u, inv1 = first_factor(ids, ridge[:, :HALF], own1, other1)
    u, inv2 = middle_factor(u)
    other2 = swap_cores(own2)
    to_send, own2, other2 = lax.optimization_barrier((to_send, own2, other2))
    received = plane_exchange(to_send)
    factor = last_factor(ids, ridge[:, HALF:], own2, other2, u, inv1, inv2)
    sketch = final_mix(ids, received.reshape(256, FEAT))
    return sketch, factor


def solution(mesh):
    return jax.shard_map(
        local,
        mesh=mesh,
        in_specs=(P(("outer", "inner"), None), P(("outer", "inner")), P(), P()),
        out_specs=(P(("outer", "inner"), None), P(("outer", "inner"), None)),
        check_vma=False,
    )
```

time: 162 us -> 160 us (0.988)
  starting transfers between devices: 17.7 us -> 63.5 us
  blocking collectives: 45 us -> 0 us
  waiting for transfers between devices: 32.4 us -> 30.1 us
    all_to_all x2 -> x0, blocking collectives: 45 us -> none  [plane_exchange(): lax.all_to_all(x, 'inner', 0, 0, axis_index_groups=PLANES, tiled=True)]
    ppermute x3 -> x24, starting transfers between devices: 3.04 us -> 37.3 us  [along(): return lax.ppermute(x, 'inner', pairs)]
    all_to_all x1 -> x0, waiting for transfers between devices: 25.2 us -> none  [local(): lax.all_to_all(mixed.reshape(4, 128, FEAT), 'inner', 0, 0, axis_index_gro...]
    ppermute x3 -> x24, waiting for transfers between devices: 2.53 us -> 26.7 us  [along(): return lax.ppermute(x, 'inner', pairs)]
    all_to_all x1 -> x3, starting transfers between devices: 3.66 us -> 16.1 us  [plane_exchange(): lax.all_to_all(x, 'inner', 0, 0, axis_index_groups=PLANES, tiled=True)]
    all_to_all x1 -> x0, starting transfers between devices: 5.99 us -> none  [local(): lax.all_to_all(mixed.reshape(4, 128, FEAT), 'inner', 0, 0, axis_index_gro...]
    ppermute x2 -> x4, starting transfers between devices: 4.99 us -> 10.1 us  [swap_cores(): return lax.ppermute(x, 'outer', [(0, 1), (1, 0)])]
    ppermute x2 -> x4, waiting for transfers between devices: 4.69 us -> 0.01 us  [swap_cores(): return lax.ppermute(x, 'outer', [(0, 1), (1, 0)])]
  transfers between devices with their start and end apart: 7 -> 31, of which waited for: 5 -> 11; matrix products, arithmetic and copies ran while one was open for 0% -> 1% of each run, Pallas kernels for 29% -> 30%
where the time goes in v2:
time: 160 us
  starting transfers between devices  63.5 us (40%)
  Pallas kernels  53.8 us (34%)
  waiting for transfers between devices  30.1 us (19%)
  local copies, waits for them, and re-layouts  11.2 us (7%)
    ppermute x24, starting transfers between devices, along(): return lax.ppermute(x, 'inner', pairs)  37.3 us
    ppermute x24, waiting for transfers between devices, along(): return lax.ppermute(x, 'inner', pairs)  26.7 us
    pallas_call x1, Pallas kernels, last_factor(): pl.pallas_call(last_factor_kernel, out_shape=jax.ShapeDtypeStruct((8, FEA...  22.1 us
    all_to_all x3, starting transfers between devices, plane_exchange(): lax.all_to_all(x, 'inner', 0, 0, axis_index_groups=PLANES, tiled=True)  16.1 us
    ppermute x4, starting transfers between devices, swap_cores(): return lax.ppermute(x, 'outer', [(0, 1), (1, 0)])  10.1 us
    unnamed x37, local copies, waits for them, and re-layouts  9.89 us
    pallas_call x1, Pallas kernels, first_factor(): pl.pallas_call(first_factor_kernel, out_shape=(SQUARE, INVERSES), in_spec...  9.39 us
    pallas_call x1, Pallas kernels, middle_factor(): pl.pallas_call(middle_factor_kernel, out_shape=(SQUARE, INVERSES), in_spe...  7.83 us
  transfers between devices with their start and end apart: 31, of which 11 were waited for; matrix products, arithmetic and copies ran while one was open for 1% of the time, Pallas kernels for 30%

profile of v2, /device:TPU:1, one launch (start us, length us, event | category | flops | bytes accessed | tf_op | source)
XLA Modules:
  0.0 159.6 jit_solution(881230844281181151)
XLA Ops:
  6.5 2.5 %collective-permute-start = (f32[128,512]{1,0:T(8,128)}, f32[128,512]{1,0:T(8,128)S(1)}, u32[]{:S(2)}, u32[]{:S(2)}) collective-permute-start(f32[128,512]{1,0:T(8,128)} %get-tuple-element.36), channel_id=1, source_target_pairs={{0,16},{1,17},{2,18},{3,19},{4,20},{5,21},{6,22},{7,23},{8,24},{9,... | collective-permute-start | bytes 786440 | tf_op jit(solution)/shard_map/ppermute | solution.py:491
  8.9 3.3 %collective-permute-start.1 = (f32[128,512]{1,0:T(8,128)}, f32[128,512]{1,0:T(8,128)}, u32[]{:S(2)}, u32[]{:S(2)}) collective-permute-start(f32[128,512]{1,0:T(8,128)} %get-tuple-element.37), channel_id=1, source_target_pairs={{0,32},{1,33},{2,34},{3,35},{4,36},{5,37},{6,38},{7,39},{8,40},{9,... | collective-permute-start | bytes 786440 | tf_op jit(solution)/shard_map/ppermute | solution.py:491
  17.3 6.6 %collective-permute-done.1.y2_ref = f32[128,512]{1,0:T(8,128)} collective-permute-done((f32[128,512]{1,0:T(8,128)}, f32[128,512]{1,0:T(8,128)}, u32[]{:S(2)}, u32[]{:S(2)}) %collective-permute-start.1) | collective-permute-done | bytes 262176 | tf_op jit(solution)/shard_map/ppermute | solution.py:491
  33.7 2.4 %collective-permute-start.13 = (f32[160,128]{1,0:T(8,128)S(1)}, f32[160,128]{1,0:T(8,128)S(1)}, u32[]{:S(2)}, u32[]{:S(2)}) collective-permute-start(f32[160,128]{1,0:T(8,128)S(1)} %get-tuple-element.58), channel_id=1, source_target_pairs={{0,2},{1,3},{2,0},{3,1},{4,6},{5,7},{6,4},{7,5},{8,10},{9,11},{10,... | collective-permute-start | bytes 245768 | tf_op jit(solution)/shard_map/ppermute | solution.py:491
  36.4 2.5 %collective-permute-start.14 = (f32[160,128]{1,0:T(8,128)S(1)}, f32[160,128]{1,0:T(8,128)S(1)}, u32[]{:S(2)}, u32[]{:S(2)}) collective-permute-start(f32[160,128]{1,0:T(8,128)S(1)} %get-tuple-element.59), channel_id=1, source_target_pairs={{0,3},{1,0},{2,1},{3,2},{4,7},{5,4},{6,5},{7,6},{8,11},{9,8},{10,9... | collective-permute-start | bytes 245768 | tf_op jit(solution)/shard_map/ppermute | solution.py:491
  38.9 3.4 %collective-permute-done.5.y2_ref = f32[128,512]{1,0:T(8,128)S(1)} collective-permute-done((f32[128,512]{1,0:T(8,128)}, f32[128,512]{1,0:T(8,128)S(1)}, u32[]{:S(2)}, u32[]{:S(2)}) %collective-permute-start.5) | collective-permute-done | bytes 262176 | tf_op jit(solution)/shard_map/ppermute | solution.py:491
  45.3 3.0 %collective-permute-start.15 = (f32[40,128]{1,0:T(8,128)S(1)}, f32[40,128]{1,0:T(8,128)S(1)}, u32[]{:S(2)}, u32[]{:S(2)}) collective-permute-start(f32[40,128]{1,0:T(8,128)S(1)} %get-tuple-element.61), channel_id=1, source_target_pairs={{0,8},{1,9},{2,10},{3,11},{4,12},{5,13},{6,14},{7,15},{8,0},{9,1},... | collective-permute-start | bytes 61448 | tf_op jit(solution)/shard_map/ppermute | solution.py:491
  55.8 2.6 %collective-permute-done.19 = f32[40,128]{1,0:T(8,128)S(1)} collective-permute-done((f32[40,128]{1,0:T(8,128)S(1)}, f32[40,128]{1,0:T(8,128)S(1)}, u32[]{:S(2)}, u32[]{:S(2)}) %collective-permute-start.19) | collective-permute-done | bytes 20512 | tf_op jit(solution)/shard_map/ppermute | solution.py:491
  58.7 2.7 %collective-permute-start.23 = (f32[40,128]{1,0:T(8,128)S(1)}, f32[40,128]{1,0:T(8,128)S(1)}, u32[]{:S(2)}, u32[]{:S(2)}) collective-permute-start(f32[40,128]{1,0:T(8,128)S(1)} %get-tuple-element.69), channel_id=1, source_target_pairs={{0,12},{1,13},{2,14},{3,15},{4,0},{5,1},{6,2},{7,3},{8,4},{9,5},{1... | collective-permute-start | bytes 61448 | tf_op jit(solution)/shard_map/ppermute | solution.py:491
  62.1 3.1 %shard_map.81 = (f32[1664,128]{1,0:T(8,128)}, f32[16,2,8,1024]{3,2,1,0:T(8,128)}) custom-call(s32[5]{0:T(128)S(1)} %stack.23.ids_ref, f32[256,512]{1,0:T(8,128)S(1)} %bitcast.19, f32[256,512]{1,0:T(8,128)S(1)} %collective-permute-done.3.w1_ref.w_ref, f32[256,512]{1,0:T(8,128)S(1)} %bitcast.22, f32[256,512]{1,0:T(8,128)S(1)} %collective-permute-done.7.w2_ref), custom_call_target="tpu_custom_call" | custom-call | tf_op jit(solution)/shard_map/pallas_call | solution.py:212
  65.3 6.3 %all-to-all-start = ((f32[16,104,128]{2,1,0:T(8,128)}), f32[16,104,128]{2,1,0:T(8,128)S(1)}, u32[]{:S(2)}, u32[]{:S(2)}) async-start(f32[16,104,128]{2,1,0:T(8,128)} %bitcast.10), calls=%async_computation | async-start | bytes 1703936 | tf_op jit(solution)/shard_map/all_to_all | solution.py:515
  71.6 2.6 %collective-permute-start.26 = (f32[160,128]{1,0:T(8,128)S(1)}, f32[160,128]{1,0:T(8,128)S(1)}, u32[]{:S(2)}, u32[]{:S(2)}) collective-permute-start(f32[160,128]{1,0:T(8,128)S(1)} %pad_maximum_fusion), channel_id=1, source_target_pairs={{0,3},{1,0},{2,1},{3,2},{4,7},{5,4},{6,5},{7,6},{8,11},{9,8},{10,9... | collective-permute-start | bytes 245768 | tf_op jit(solution)/shard_map/ppermute | solution.py:491
  75.4 8.6 %collective-permute-done.24 = f32[160,128]{1,0:T(8,128)S(1)} collective-permute-done((f32[160,128]{1,0:T(8,128)S(1)}, f32[160,128]{1,0:T(8,128)S(1)}, u32[]{:S(2)}, u32[]{:S(2)}) %collective-permute-start.24) | collective-permute-done | bytes 81952 | tf_op jit(solution)/shard_map/ppermute | solution.py:491
  84.0 4.7 %collective-permute-start.27 = (f32[640,128]{1,0:T(8,128)S(1)}, f32[640,128]{1,0:T(8,128)S(1)}, u32[]{:S(2)}, u32[]{:S(2)}) collective-permute-start(f32[640,128]{1,0:T(8,128)S(1)} %constant_dynamic-update-slice_fusion.own_rel), channel_id=1, source_target_pairs={{0,64},{64,0},{1,65},{65,1},{2,66},{66,2},{3,67},{67,3},{4,68},{68... | collective-permute-start | bytes 983048 | tf_op jit(solution)/shard_map/ppermute | solution.py:482
  88.8 2.7 %collective-permute-start.10 = (f32[104,128]{1,0:T(8,128)S(1)}, f32[104,128]{1,0:T(8,128)S(1)}, u32[]{:S(2)}, u32[]{:S(2)}) collective-permute-start(f32[104,128]{1,0:T(8,128)S(1)} %reduce_sum.9), channel_id=1, source_target_pairs={{0,48},{1,49},{2,50},{3,51},{4,52},{5,53},{6,54},{7,55},{8,56},{9,... | collective-permute-start | bytes 159752 | tf_op jit(solution)/shard_map/ppermute | solution.py:491
  92.8 3.2 %collective-permute-done.9 = f32[104,128]{1,0:T(8,128)S(1)} collective-permute-done((f32[104,128]{1,0:T(8,128)S(1)}, f32[104,128]{1,0:T(8,128)S(1)}, u32[]{:S(2)}, u32[]{:S(2)}) %collective-permute-start.9) | collective-permute-done | bytes 53280 | tf_op jit(solution)/shard_map/ppermute | solution.py:491
  97.3 6.2 %all-to-all-start.1 = ((f32[16,104,128]{2,1,0:T(8,128)}), f32[16,104,128]{2,1,0:T(8,128)S(1)}, u32[]{:S(2)}, u32[]{:S(2)}) async-start(f32[16,104,128]{2,1,0:T(8,128)} %broadcast_in_dim.10), calls=%async_computation.1 | async-start | bytes 1703936 | tf_op jit(solution)/shard_map/all_to_all | solution.py:515
  103.6 9.4 %shard_map.85 = (f32[512,512]{1,0:T(8,128)S(1)}, f32[2,128,128]{2,1,0:T(8,128)S(1)}) custom-call(s32[5]{0:T(128)S(1)} %stack.23.ids_ref, f32[1,512]{1,0:T(1,128)S(1)} %get-tuple-element.70.ridge_ref, f32[640,128]{1,0:T(8,128)S(1)} %constant_dynamic-update-slice_fusion.own_rel, f32[640,128]{1,0:T(8,128)S(1)} %collective-permute-done.27.other_rel), custom_call_target="tpu_custom_call" | custom-call | flops 12000000000 | bytes 2097152 | tf_op jit(solution)/shard_map/pallas_call | solution.py:446
  114.0 3.4 %all-to-all-done.1 = f32[16,104,128]{2,1,0:T(8,128)S(1)} async-done(((f32[16,104,128]{2,1,0:T(8,128)}), f32[16,104,128]{2,1,0:T(8,128)S(1)}, u32[]{:S(2)}, u32[]{:S(2)}) %all-to-all-start.1) | async-done | bytes 852000 | tf_op jit(solution)/shard_map/all_to_all | solution.py:515
  117.3 2.4 %collective-permute-start.11 = (f32[1664,128]{1,0:T(8,128)S(1)}, f32[1664,128]{1,0:T(8,128)S(1)}, u32[]{:S(2)}, u32[]{:S(2)}) collective-permute-start(f32[1664,128]{1,0:T(8,128)S(1)} %bitcast.23), channel_id=1, source_target_pairs={{0,64},{64,0},{1,65},{65,1},{2,66},{66,2},{3,67},{67,3},{4,68},{68... | collective-permute-start | bytes 2555912 | tf_op jit(solution)/shard_map/ppermute | solution.py:482
  121.0 7.8 %shard_map.86 = (f32[512,512]{1,0:T(8,128)S(1)}, f32[2,128,128]{2,1,0:T(8,128)S(1)}) custom-call(f32[512,512]{1,0:T(8,128)S(1)} %copy-done.13), custom_call_target="tpu_custom_call" | custom-call | flops 12000000000 | bytes 2097152 | tf_op jit(solution)/shard_map/pallas_call | solution.py:458
  129.8 3.7 %all-to-all-start.2 = ((f32[16,2,8,1024]{3,2,1,0:T(8,128)}), f32[16,2,8,1024]{3,2,1,0:T(8,128)S(1)}, u32[]{:S(2)}, u32[]{:S(2)}) async-start(f32[16,2,8,1024]{3,2,1,0:T(8,128)} %get-tuple-element.53), calls=%async_computation.2 | async-start | bytes 2097152 | tf_op jit(solution)/shard_map/all_to_all | solution.py:515
  134.7 22.1 %shard_map.87 = f32[8,1024]{1,0:T(8,128)} custom-call(s32[5]{0:T(128)S(1)} %stack.23.ids_ref, f32[1,512]{1,0:T(1,128)S(1)} %get-tuple-element.71.ridge_ref, f32[1664,128]{1,0:T(8,128)S(1)} %bitcast.24, f32[1664,128]{1,0:T(8,128)S(1)} %collective-permute-done.11.other_ref, f32[512,512]{1,0:T(8,128)S(1)} %copy-done.11, ...), custom_call_target="tpu_custom_call" | custom-call | flops 30000001024 | bytes 2097152 | tf_op jit(solution)/shard_map/pallas_call | solution.py:470
  156.9 2.7 %shard_map.82 = f32[256,1024]{1,0:T(8,128)} custom-call(s32[5]{0:T(128)S(1)} %stack.23.ids_ref, bf16[256,256]{1,0:T(8,128)(2,1)S(1)} %copy-done.4, f32[256,1024]{1,0:T(8,128)S(1)} %bitcast.20), custom_call_target="tpu_custom_call" | custom-call | tf_op jit(solution)/shard_map/pallas_call | solution.py:236
  (99 shorter events, 40.7 us)
Async XLA Ops:
  6.5 10.8 %collective-permute-start = (f32[128,512]{1,0:T(8,128)}, f32[128,512]{1,0:T(8,128)S(1)}, u32[]{:S(2)}, u32[]{:S(2)}) collective-permute-start(f32[128,512]{1,0:T(8,128)} %get-tuple-element.36), channel_id=1, source_target_pairs={{0,16},{1,17},{2,18},{3,19},{4,20},{5,21},{6,22},{7,23},{8,24},{9,... | collective-permute-start | bytes 786440 | tf_op jit(solution)/shard_map/ppermute | solution.py:491
  8.9 14.9 %collective-permute-start.1 = (f32[128,512]{1,0:T(8,128)}, f32[128,512]{1,0:T(8,128)}, u32[]{:S(2)}, u32[]{:S(2)}) collective-permute-start(f32[128,512]{1,0:T(8,128)} %get-tuple-element.37), channel_id=1, source_target_pairs={{0,32},{1,33},{2,34},{3,35},{4,36},{5,37},{6,38},{7,39},{8,40},{9,... | collective-permute-start | bytes 786440 | tf_op jit(solution)/shard_map/ppermute | solution.py:491
  12.2 11.6 %collective-permute-start.2 = (f32[128,512]{1,0:T(8,128)}, f32[128,512]{1,0:T(8,128)}, u32[]{:S(2)}, u32[]{:S(2)}) collective-permute-start(f32[128,512]{1,0:T(8,128)} %get-tuple-element.38), channel_id=1, source_target_pairs={{0,48},{1,49},{2,50},{3,51},{4,52},{5,53},{6,54},{7,55},{8,56},{9,... | collective-permute-start | bytes 786440 | tf_op jit(solution)/shard_map/ppermute | solution.py:491
  25.5 5.7 %collective-permute-start.3 = (f32[256,512]{1,0:T(8,128)S(1)}, f32[256,512]{1,0:T(8,128)S(1)}, u32[]{:S(2)}, u32[]{:S(2)}) collective-permute-start(f32[256,512]{1,0:T(8,128)S(1)} %bitcast.17), channel_id=1, source_target_pairs={{0,64},{64,0},{1,65},{65,1},{2,66},{66,2},{3,67},{67,3},{4,68},{68... | collective-permute-start | bytes 1572872 | tf_op jit(solution)/shard_map/ppermute | solution.py:482
  27.1 9.3 %collective-permute-start.4 = (f32[128,512]{1,0:T(8,128)}, f32[128,512]{1,0:T(8,128)S(1)}, u32[]{:S(2)}, u32[]{:S(2)}) collective-permute-start(f32[128,512]{1,0:T(8,128)} %copy-done.9), channel_id=1, source_target_pairs={{0,16},{1,17},{2,18},{3,19},{4,20},{5,21},{6,22},{7,23},{8,24},{9,... | collective-permute-start | bytes 786440 | tf_op jit(solution)/shard_map/ppermute | solution.py:491
  28.0 14.3 %collective-permute-start.5 = (f32[128,512]{1,0:T(8,128)}, f32[128,512]{1,0:T(8,128)S(1)}, u32[]{:S(2)}, u32[]{:S(2)}) collective-permute-start(f32[128,512]{1,0:T(8,128)} %copy-done.8), channel_id=1, source_target_pairs={{0,32},{1,33},{2,34},{3,35},{4,36},{5,37},{6,38},{7,39},{8,40},{9,... | collective-permute-start | bytes 786440 | tf_op jit(solution)/shard_map/ppermute | solution.py:491
  30.1 12.2 %collective-permute-start.6 = (f32[128,512]{1,0:T(8,128)}, f32[128,512]{1,0:T(8,128)S(1)}, u32[]{:S(2)}, u32[]{:S(2)}) collective-permute-start(f32[128,512]{1,0:T(8,128)} %copy-done.7), channel_id=1, source_target_pairs={{0,48},{1,49},{2,50},{3,51},{4,52},{5,53},{6,54},{7,55},{8,56},{9,... | collective-permute-start | bytes 786440 | tf_op jit(solution)/shard_map/ppermute | solution.py:491
  32.4 12.3 %collective-permute-start.12 = (f32[160,128]{1,0:T(8,128)S(1)}, f32[160,128]{1,0:T(8,128)S(1)}, u32[]{:S(2)}, u32[]{:S(2)}) collective-permute-start(f32[160,128]{1,0:T(8,128)S(1)} %get-tuple-element.57), channel_id=1, source_target_pairs={{0,1},{1,2},{2,3},{3,0},{4,5},{5,6},{6,7},{7,4},{8,9},{9,10},{10,1... | collective-permute-start | bytes 245768 | tf_op jit(solution)/shard_map/ppermute | solution.py:491
  33.7 11.0 %collective-permute-start.13 = (f32[160,128]{1,0:T(8,128)S(1)}, f32[160,128]{1,0:T(8,128)S(1)}, u32[]{:S(2)}, u32[]{:S(2)}) collective-permute-start(f32[160,128]{1,0:T(8,128)S(1)} %get-tuple-element.58), channel_id=1, source_target_pairs={{0,2},{1,3},{2,0},{3,1},{4,6},{5,7},{6,4},{7,5},{8,10},{9,11},{10,... | collective-permute-start | bytes 245768 | tf_op jit(solution)/shard_map/ppermute | solution.py:491
  36.4 8.3 %collective-permute-start.14 = (f32[160,128]{1,0:T(8,128)S(1)}, f32[160,128]{1,0:T(8,128)S(1)}, u32[]{:S(2)}, u32[]{:S(2)}) collective-permute-start(f32[160,128]{1,0:T(8,128)S(1)} %get-tuple-element.59), channel_id=1, source_target_pairs={{0,3},{1,0},{2,1},{3,2},{4,7},{5,4},{6,5},{7,6},{8,11},{9,8},{10,9... | collective-permute-start | bytes 245768 | tf_op jit(solution)/shard_map/ppermute | solution.py:491
  43.4 18.7 %collective-permute-start.7 = (f32[256,512]{1,0:T(8,128)S(1)}, f32[256,512]{1,0:T(8,128)S(1)}, u32[]{:S(2)}, u32[]{:S(2)}) collective-permute-start(f32[256,512]{1,0:T(8,128)S(1)} %bitcast.21), channel_id=1, source_target_pairs={{0,64},{64,0},{1,65},{65,1},{2,66},{66,2},{3,67},{67,3},{4,68},{68... | collective-permute-start | bytes 1572872 | tf_op jit(solution)/shard_map/ppermute | solution.py:482
  45.3 5.7 %collective-permute-start.15 = (f32[40,128]{1,0:T(8,128)S(1)}, f32[40,128]{1,0:T(8,128)S(1)}, u32[]{:S(2)}, u32[]{:S(2)}) collective-permute-start(f32[40,128]{1,0:T(8,128)S(1)} %get-tuple-element.61), channel_id=1, source_target_pairs={{0,8},{1,9},{2,10},{3,11},{4,12},{5,13},{6,14},{7,15},{8,0},{9,1},... | collective-permute-start | bytes 61448 | tf_op jit(solution)/shard_map/ppermute | solution.py:491
  58.7 12.8 %collective-permute-start.23 = (f32[40,128]{1,0:T(8,128)S(1)}, f32[40,128]{1,0:T(8,128)S(1)}, u32[]{:S(2)}, u32[]{:S(2)}) collective-permute-start(f32[40,128]{1,0:T(8,128)S(1)} %get-tuple-element.69), channel_id=1, source_target_pairs={{0,12},{1,13},{2,14},{3,15},{4,0},{5,1},{6,2},{7,3},{8,4},{9,5},{1... | collective-permute-start | bytes 61448 | tf_op jit(solution)/shard_map/ppermute | solution.py:491
  61.5 10.1 %collective-permute-start.22 = (f32[40,128]{1,0:T(8,128)S(1)}, f32[40,128]{1,0:T(8,128)S(1)}, u32[]{:S(2)}, u32[]{:S(2)}) collective-permute-start(f32[40,128]{1,0:T(8,128)S(1)} %get-tuple-element.69), channel_id=1, source_target_pairs={{0,8},{1,9},{2,10},{3,11},{4,12},{5,13},{6,14},{7,15},{8,0},{9,1},... | collective-permute-start | bytes 61448 | tf_op jit(solution)/shard_map/ppermute | solution.py:491
  61.5 10.1 %collective-permute-start.21 = (f32[40,128]{1,0:T(8,128)S(1)}, f32[40,128]{1,0:T(8,128)S(1)}, u32[]{:S(2)}, u32[]{:S(2)}) collective-permute-start(f32[40,128]{1,0:T(8,128)S(1)} %get-tuple-element.69), channel_id=1, source_target_pairs={{0,4},{1,5},{2,6},{3,7},{4,8},{5,9},{6,10},{7,11},{8,12},{9,13},{1... | collective-permute-start | bytes 61448 | tf_op jit(solution)/shard_map/ppermute | solution.py:491
  65.3 23.5 %all-to-all-start = ((f32[16,104,128]{2,1,0:T(8,128)}), f32[16,104,128]{2,1,0:T(8,128)S(1)}, u32[]{:S(2)}, u32[]{:S(2)}) async-start(f32[16,104,128]{2,1,0:T(8,128)} %bitcast.10), calls=%async_computation | async-start | bytes 1703936 | tf_op jit(solution)/shard_map/all_to_all | solution.py:515
  71.6 12.4 %collective-permute-start.26 = (f32[160,128]{1,0:T(8,128)S(1)}, f32[160,128]{1,0:T(8,128)S(1)}, u32[]{:S(2)}, u32[]{:S(2)}) collective-permute-start(f32[160,128]{1,0:T(8,128)S(1)} %pad_maximum_fusion), channel_id=1, source_target_pairs={{0,3},{1,0},{2,1},{3,2},{4,7},{5,4},{6,5},{7,6},{8,11},{9,8},{10,9... | collective-permute-start | bytes 245768 | tf_op jit(solution)/shard_map/ppermute | solution.py:491
  74.2 9.7 %collective-permute-start.25 = (f32[160,128]{1,0:T(8,128)S(1)}, f32[160,128]{1,0:T(8,128)S(1)}, u32[]{:S(2)}, u32[]{:S(2)}) collective-permute-start(f32[160,128]{1,0:T(8,128)S(1)} %pad_maximum_fusion), channel_id=1, source_target_pairs={{0,2},{1,3},{2,0},{3,1},{4,6},{5,7},{6,4},{7,5},{8,10},{9,11},{10,... | collective-permute-start | bytes 245768 | tf_op jit(solution)/shard_map/ppermute | solution.py:491
  74.8 9.1 %collective-permute-start.24 = (f32[160,128]{1,0:T(8,128)S(1)}, f32[160,128]{1,0:T(8,128)S(1)}, u32[]{:S(2)}, u32[]{:S(2)}) collective-permute-start(f32[160,128]{1,0:T(8,128)S(1)} %pad_maximum_fusion), channel_id=1, source_target_pairs={{0,1},{1,2},{2,3},{3,0},{4,5},{5,6},{6,7},{7,4},{8,9},{9,10},{10,1... | collective-permute-start | bytes 245768 | tf_op jit(solution)/shard_map/ppermute | solution.py:491
  84.0 19.5 %collective-permute-start.27 = (f32[640,128]{1,0:T(8,128)S(1)}, f32[640,128]{1,0:T(8,128)S(1)}, u32[]{:S(2)}, u32[]{:S(2)}) collective-permute-start(f32[640,128]{1,0:T(8,128)S(1)} %constant_dynamic-update-slice_fusion.own_rel), channel_id=1, source_target_pairs={{0,64},{64,0},{1,65},{65,1},{2,66},{66,2},{3,67},{67,3},{4,68},{68... | collective-permute-start | bytes 983048 | tf_op jit(solution)/shard_map/ppermute | solution.py:482
  91.5 4.8 %collective-permute-start.8 = (f32[104,128]{1,0:T(8,128)S(1)}, f32[104,128]{1,0:T(8,128)S(1)}, u32[]{:S(2)}, u32[]{:S(2)}) collective-permute-start(f32[104,128]{1,0:T(8,128)S(1)} %reduce_sum.9), channel_id=1, source_target_pairs={{0,32},{1,33},{2,34},{3,35},{4,36},{5,37},{6,38},{7,39},{8,40},{9,... | collective-permute-start | bytes 159752 | tf_op jit(solution)/shard_map/ppermute | solution.py:491
  97.3 20.0 %all-to-all-start.1 = ((f32[16,104,128]{2,1,0:T(8,128)}), f32[16,104,128]{2,1,0:T(8,128)S(1)}, u32[]{:S(2)}, u32[]{:S(2)}) async-start(f32[16,104,128]{2,1,0:T(8,128)} %broadcast_in_dim.10), calls=%async_computation.1 | async-start | bytes 1703936 | tf_op jit(solution)/shard_map/all_to_all | solution.py:515
  117.3 12.5 %collective-permute-start.11 = (f32[1664,128]{1,0:T(8,128)S(1)}, f32[1664,128]{1,0:T(8,128)S(1)}, u32[]{:S(2)}, u32[]{:S(2)}) collective-permute-start(f32[1664,128]{1,0:T(8,128)S(1)} %bitcast.23), channel_id=1, source_target_pairs={{0,64},{64,0},{1,65},{65,1},{2,66},{66,2},{3,67},{67,3},{4,68},{68... | collective-permute-start | bytes 2555912 | tf_op jit(solution)/shard_map/ppermute | solution.py:482
  129.8 27.0 %all-to-all-start.2 = ((f32[16,2,8,1024]{3,2,1,0:T(8,128)}), f32[16,2,8,1024]{3,2,1,0:T(8,128)S(1)}, u32[]{:S(2)}, u32[]{:S(2)}) async-start(f32[16,2,8,1024]{3,2,1,0:T(8,128)} %get-tuple-element.53), calls=%async_computation.2 | async-start | bytes 2097152 | tf_op jit(solution)/shard_map/all_to_all | solution.py:515
  (23 other events, 129.9 us)

commit v3 on v2

--- a/solution.py
+++ b/solution.py
@@ -19,7 +19,7 @@
 PLANES = [[16 * j + i for i in range(16)] for j in range(4)]
 
 
-def params(mib=48):
+def params(mib=60):
     return pltpu.CompilerParams(vmem_limit_bytes=mib << 20)
 
 
@@ -57,56 +57,46 @@
     return lax.dot_general(a, b, (((0,), (0,)), ((), ())), preferred_element_type=f32)
 
 
-def turn(index, step):
-    return (index + step) & 3
-
-
-def local_mix_kernel(ids_ref, table_ref, sign_ref, x_ref, *rest):
-    outs, signed = rest[:4], rest[4]
-
+def local_mix_kernel(table_ref, sign_ref, x_ref, o_ref, signed):
     @pl.when(pl.program_id(0) == 0)
     def _():
         signed[...] = (table_ref[...].astype(f32) * (sign_ref[...].astype(f32) * 2.0**-13)).astype(bf16)
 
     high, low = halves(x_ref[...])
-    for step in range(4):
-        rows = signed[pl.ds(pl.multiple_of(turn(ids_ref[4], step) * 128, 128), 128), :]
-        outs[step][...] = mm(rows, high) + mm(rows, low)
-
-
-def local_mix(ids, table, signs, matrix, half):
-    rows = matrix.shape[0]
+    o_ref[...] = mm(signed[...], high) + mm(signed[...], low)
+
+
+def local_mix(matrix, sign_flip):
+    rows, features = matrix.shape
     cols = 256
     return pl.pallas_call(
         local_mix_kernel,
-        grid=(HALF // cols,),
-        out_shape=(jax.ShapeDtypeStruct((128, HALF), f32),) * 4,
+        grid=(features // cols,),
+        out_shape=jax.ShapeDtypeStruct((rows, features), f32),
         in_specs=[
-            SMEM,
             pl.BlockSpec((rows, rows), lambda g: (0, 0)),
             pl.BlockSpec((1, rows), lambda g: (0, 0)),
-            pl.BlockSpec((rows, cols), lambda g: (0, g + half * (HALF // cols))),
+            pl.BlockSpec((rows, cols), lambda g: (0, g)),
         ],
-        out_specs=(pl.BlockSpec((128, cols), lambda g: (0, g)),) * 4,
+        out_specs=pl.BlockSpec((rows, cols), lambda g: (0, g)),
         scratch_shapes=[pltpu.VMEM((rows, rows), bf16)],
-        compiler_params=params(),
-    )(ids, table, signs, matrix)
-
-
-def select_kernel(ids_ref, keep_ref, y0_ref, y1_ref, y2_ref, y3_ref, v_ref):
-    parts = [ref[...] for ref in (y0_ref, y1_ref, y2_ref, y3_ref)]
-    shape = parts[0].shape
+        compiler_params=params(60),
+    )(jnp.asarray(local_table()), sign_flip.reshape(1, rows), matrix)
+
+
+def select_kernel(keep_ref, y_ref, v_ref):
+    y0, y1, y2, y3 = (y_ref[z] for z in range(4))
+    s, d, s2, d2 = y0 + y1, y0 - y1, y2 + y3, y2 - y3
 
     def combo(which):
-        total = None
-        for step, part in enumerate(parts):
-            common = which & turn(ids_ref[4], 4 - step)
-            sign = (1 - 2 * ((common ^ (common >> 1)) & 1)).astype(f32)
-            term = part * jnp.broadcast_to(sign, shape)
-            total = term if total is None else total + term
-        return total
-
-    v0, v1 = combo(keep_ref[:, 0:1]), combo(keep_ref[:, 1:2])
+        low = (which & 1) == 1
+        first = jnp.where(low, d, s)
+        second = jnp.where(low, d2, s2)
+        return first + jnp.where((which & 2) == 2, -second, second)
+
+    shape = s.shape
+    v0 = combo(jnp.broadcast_to(keep_ref[:, 0:1], shape))
+    v1 = combo(jnp.broadcast_to(keep_ref[:, 1:2], shape))
     upper = (lax.broadcasted_iota(jnp.int32, shape, 0) & 7) < 4
     even = jnp.where(upper, v0, pltpu.roll(v1, 4, axis=0))
     odd = jnp.where(upper, pltpu.roll(v0, shape[0] - 4, axis=0), v1)
@@ -114,112 +104,73 @@
     v_ref[:, 1] = odd.reshape(16, 8, shape[1])
 
 
-def select_rows(ids, keep_rows, parts):
+def select_rows(keep_rows, y):
     cols = 256
-    features = parts[0].shape[1]
+    features = y.shape[2]
     return pl.pallas_call(
         select_kernel,
         grid=(features // cols,),
         out_shape=jax.ShapeDtypeStruct((16, 2, 8, features), f32),
-        in_specs=[SMEM, pl.BlockSpec((128, 2), lambda g: (0, 0))]
-        + [pl.BlockSpec((128, cols), lambda g: (0, g))] * 4,
+        in_specs=[
+            pl.BlockSpec((128, 2), lambda g: (0, 0)),
+            pl.BlockSpec((4, 128, cols), lambda g: (0, 0, g)),
+        ],
         out_specs=pl.BlockSpec((16, 2, 8, cols), lambda g: (0, 0, 0, g)),
-        compiler_params=params(),
-    )(ids, keep_rows, *parts)
-
-
-def load_halves(mine_ref, theirs_ref, high, low):
-    for part, ref in enumerate((mine_ref, theirs_ref)):
+        compiler_params=params(60),
+    )(keep_rows, y)
+
+
+def gram_kernel(ids_ref, v_ref, w_ref, g_ref, s_ref, high, low, first, second):
+    own = pl.ds(pl.multiple_of(ids_ref[0] * 128, 128), 128)
+    for part, ref in enumerate((v_ref, w_ref)):
         h, l = halves(ref[...])
         high[256 * part : 256 * part + 256, :] = h
         low[256 * part : 256 * part + 256, :] = l
-
-
-def strip_blocks(left, right, at, start, g_ref, slot):
-    high, low = left
-    high_right, low_right = right
-    h, l = high[:, at : at + NB], low[:, at : at + NB]
-    total = tmm(h, high_right[:, start:]) + (tmm(h, low_right[:, start:]) + tmm(l, high_right[:, start:]))
-    for block in range((HALF - start) // NB):
-        row = NB * (slot + block)
-        g_ref[row : row + NB, :] = total[:, NB * block : NB * block + NB]
-    return slot + (HALF - start) // NB
-
-
-def first_gram_kernel(ids_ref, v_ref, w_ref, *rest):
-    outs, (high, low, blocks) = rest[:4], rest[4:]
-    load_halves(v_ref, w_ref, high, low)
+        s_ref[:, part] = ref[own, :].reshape(16, 8, FEAT)
+
+    def strip_sum(strip):
+        at = NB * strip
+        h, l = high[:, at : at + NB], low[:, at : at + NB]
+        return tmm(h, high[:, at:]) + (tmm(h, low[:, at:]) + tmm(l, high[:, at:]))
+
+    def store(target, slot, value):
+        for block in range(value.shape[1] // NB):
+            row = NB * (slot + block)
+            target[row : row + NB, :] = value[:, NB * block : NB * block + NB]
+        return slot + value.shape[1] // NB
+
     for which, strips in enumerate(PAIRS):
 
         @pl.when(ids_ref[0] == which)
         def _():
-            slot = 0
+            slot1 = slot2 = 0
             for strip in strips:
-                slot = strip_blocks((high, low), (high, low), NB * strip, NB * strip, blocks, slot)
-
-    for step in range(4):
-        outs[step][...] = blocks[pl.ds(pl.multiple_of(turn(ids_ref[2], step) * 160, 8), 160), :]
-
-
-def sum_split_kernel(ids_ref, *rest):
-    parts, outs, total = rest[:4], rest[4:8], rest[8]
-    total[...] = (parts[0][...] + parts[1][...]) + (parts[2][...] + parts[3][...])
-    for step in range(4):
-        outs[step][...] = total[pl.ds(pl.multiple_of(turn(ids_ref[3], step) * 40, 8), 40), :]
-
-
-def sum_split(ids, parts):
-    return pl.pallas_call(
-        sum_split_kernel,
-        out_shape=(jax.ShapeDtypeStruct((40, NB), f32),) * 4,
-        in_specs=[SMEM] + [VMEM] * 4,
-        out_specs=(VMEM,) * 4,
-        scratch_shapes=[pltpu.VMEM((160, NB), f32)],
-        compiler_params=params(),
-    )(ids, *parts)
-
-
-def second_gram_kernel(ids_ref, v1_ref, w1_ref, v2_ref, w2_ref, g_ref, s_ref, high1, low1, high2, low2):
-    load_halves(v1_ref, w1_ref, high1, low1)
-    load_halves(v2_ref, w2_ref, high2, low2)
-    own = pl.ds(pl.multiple_of(ids_ref[0] * 128, 128), 128)
-    for half, refs in enumerate(((v1_ref, w1_ref), (v2_ref, w2_ref))):
-        for part, ref in enumerate(refs):
-            s_ref[:, part, :, half * HALF : half * HALF + HALF] = ref[own, :].reshape(16, 8, HALF)
-    for which, strips in enumerate(PAIRS):
-
-        @pl.when(ids_ref[0] == which)
-        def _():
-            slot = 0
+                value = strip_sum(strip)
+                edge = HALF - NB * strip
+                slot1 = store(first, slot1, value[:, :edge])
+                slot2 = store(second, slot2, value[:, edge:])
             for strip in strips:
-                slot = strip_blocks((high1, low1), (high2, low2), NB * strip, 0, g_ref, slot)
-            for strip in strips:
-                slot = strip_blocks((high2, low2), (high2, low2), NB * strip, NB * strip, g_ref, slot)
-
-
-def first_gram(ids, mine, theirs):
-    return pl.pallas_call(
-        first_gram_kernel,
-        out_shape=(jax.ShapeDtypeStruct((160, NB), f32),) * 4,
+                slot2 = store(second, slot2, strip_sum(strip + 4))
+
+    for piece in range(16):
+        g_ref[piece, :40] = first[40 * piece : 40 * piece + 40, :]
+        g_ref[piece, 40:] = second[104 * piece : 104 * piece + 104, :]
+
+
+def gram_half(ids, mine, theirs):
+    rows = mine.shape[0]
+    return pl.pallas_call(
+        gram_kernel,
+        out_shape=(
+            jax.ShapeDtypeStruct((16, 144, NB), f32),
+            jax.ShapeDtypeStruct((16, 2, 8, FEAT), f32),
+        ),
         in_specs=[SMEM, VMEM, VMEM],
-        out_specs=(VMEM,) * 4,
-        scratch_shapes=[pltpu.VMEM((512, HALF), bf16)] * 2 + [pltpu.VMEM((5 * NB, NB), f32)],
+        out_specs=(VMEM, VMEM),
+        scratch_shapes=[pltpu.VMEM((2 * rows, FEAT), bf16)] * 2
+        + [pltpu.VMEM((5 * NB, NB), f32), pltpu.VMEM((13 * NB, NB), f32)],
         compiler_params=params(),
     )(ids, mine, theirs)
-
-
-def second_gram(ids, mine1, theirs1, mine2, theirs2):
-    return pl.pallas_call(
-        second_gram_kernel,
-        out_shape=(
-            jax.ShapeDtypeStruct((13 * NB, NB), f32),
-            jax.ShapeDtypeStruct((16, 2, 8, FEAT), f32),
-        ),
-        in_specs=[SMEM] + [VMEM] * 4,
-        out_specs=(VMEM, VMEM),
-        scratch_shapes=[pltpu.VMEM((512, HALF), bf16)] * 4,
-        compiler_params=params(),
-    )(ids, mine1, theirs1, mine2, theirs2)
 
 
 def final_kernel(ids_ref, table_ref, r_ref, o_ref):
@@ -362,14 +313,7 @@
     lax.fori_loop(first, last, body, 0)
 
 
-def first_factor_kernel(ids_ref, ridge_ref, own_rel, other_rel, a, inv_ref, own_ref, other_ref, w, upper, inverse):
-    for back_x in range(4):
-        for back_y in range(4):
-            source = 160 * back_x + 40 * back_y
-            row = turn(ids_ref[2], 4 - back_x) * 160 + turn(ids_ref[3], 4 - back_y) * 40
-            target = pl.ds(pl.multiple_of(row, 8), 40)
-            own_ref[target, :] = own_rel[source : source + 40, :]
-            other_ref[target, :] = other_rel[source : source + 40, :]
+def first_factor_kernel(ids_ref, ridge_ref, own_ref, other_ref, a, inv_ref, w, upper, inverse):
     for which in range(2):
 
         @pl.when(ids_ref[0] == which)
@@ -448,7 +392,7 @@
         out_shape=(SQUARE, INVERSES),
         in_specs=[SMEM, VMEM, VMEM, VMEM],
         out_specs=(VMEM, VMEM),
-        scratch_shapes=[pltpu.VMEM((5 * NB, NB), f32)] * 2 + BLOCK_SCRATCH,
+        scratch_shapes=BLOCK_SCRATCH,
         compiler_params=params(),
         cost_estimate=cost(12),
     )(ids, ridge, own, other)
@@ -482,33 +426,8 @@
     return lax.ppermute(x, "outer", [(0, 1), (1, 0)])
 
 
-def along(axis, x, distance):
-    stride = {"x": 1, "y": 4, "z": 16}[axis]
-    pairs = []
-    for source in range(64):
-        digit = source // stride % 4
-        pairs.append((source, source + ((digit + distance) % 4 - digit) * stride))
-    return lax.ppermute(x, "inner", pairs)
-
-
-def exchange(axis, parts):
-    return [parts[0]] + [along(axis, parts[step], step) for step in (1, 3, 2)]
-
-
-def in_order(parts):
-    return [parts[0], parts[1], parts[3], parts[2]]
-
-
-def shared(axis, x):
-    return in_order(exchange(axis, [x] * 4))
-
-
-def scattered(axis, parts):
-    return in_order(exchange(axis, parts))
-
-
-def total(parts):
-    return (parts[0] + parts[2]) + (parts[1] + parts[3])
+def along_z(x, distance):
+    return lax.ppermute(x, "inner", [(i, (i + 16 * distance) % 64) for i in range(64)])
 
 
 def plane_exchange(x):
@@ -521,32 +440,25 @@
 
 def local(matrix, sign_flip, keep_list, ridge_weights):
     core, inner = lax.axis_index("outer"), lax.axis_index("inner")
-    ids = jnp.stack([core, core * 64 + inner, inner & 3, (inner >> 2) & 3, inner >> 4]).astype(jnp.int32)
+    ids = jnp.stack([core, core * 64 + inner]).astype(jnp.int32)
     keep_here = lax.dynamic_index_in_dim(keep_list.reshape(2, 4, 16, 2), inner >> 4, 1, False)
     keep_rows = jnp.repeat(keep_here.reshape(32, 2), 4, axis=0)
-    table, signs = jnp.asarray(local_table()), sign_flip.reshape(1, -1)
     ridge = ridge_weights.reshape(1, FEAT)
 
-    along1 = scattered("z", local_mix(ids, table, signs, matrix, 0))
-    mixed2 = local_mix(ids, table, signs, matrix, 1)
-    along1, mixed2 = lax.optimization_barrier((along1, mixed2))
-    along2 = scattered("z", mixed2)
-    mine1 = select_rows(ids, keep_rows, along1).reshape(256, HALF)
-    theirs1 = swap_cores(mine1)
-    by_y = sum_split(ids, scattered("x", first_gram(ids, mine1, theirs1)))
-    piece1 = total(scattered("y", by_y))
-    piece1 = total(shared("z", piece1))
-    row1 = jnp.concatenate(shared("y", piece1), axis=0)
-    own1 = jnp.concatenate(shared("x", row1), axis=0)
+    mixed = local_mix(matrix, sign_flip)
+    along = lax.all_to_all(
+        mixed.reshape(4, 128, FEAT), "inner", 0, 0, axis_index_groups=Z_GROUPS, tiled=True
+    )
+    mine = select_rows(keep_rows, along).reshape(256, FEAT)
+    theirs = swap_cores(mine)
+    gram, to_send = gram_half(ids, mine, theirs)
+    piece = jnp.sum(plane_exchange(gram), axis=0)
+    piece = (piece + along_z(piece, 2)) + (along_z(piece, 1) + along_z(piece, 3))
+    own1 = plane_exchange(copies(piece[:40]))
+    later, own1 = lax.optimization_barrier((copies(piece[40:]), own1))
+    own1 = own1.reshape(5 * NB, NB)
+    own2 = plane_exchange(later).reshape(13 * NB, NB)
     other1 = swap_cores(own1)
-
-    mine2 = select_rows(ids, keep_rows, along2).reshape(256, HALF)
-    theirs2 = swap_cores(mine2)
-    gram2, to_send = second_gram(ids, mine1, theirs1, mine2, theirs2)
-    piece2 = jnp.sum(plane_exchange(gram2.reshape(16, 104, 128)), axis=0)
-    piece2 = total(shared("z", piece2))
-    own2 = plane_exchange(copies(piece2)).reshape(13 * NB, NB)
-
     u, inv1 = first_factor(ids, ridge[:, :HALF], own1, other1)
     u, inv2 = middle_factor(u)
     other2 = swap_cores(own2)

time: 160 us -> 163 us (1.019)
  starting transfers between devices: 63.5 us -> 26.2 us
  blocking collectives: 0 us -> 24.8 us
  waiting for transfers between devices: 30.1 us -> 41.8 us
  Pallas kernels: 53.8 us -> 61.3 us
  local copies, waits for them, and re-layouts: 11.2 us -> 6.6 us
    ppermute x24 -> x3, starting transfers between devices: 37.3 us -> 3.04 us  [along_z(): lax.ppermute(x, 'inner', [(i, (i + 16 * distance) % 64) for i in range(64)])]
    all_to_all x0 -> x1, waiting for transfers between devices: none -> 25.2 us  [local(): lax.all_to_all(mixed.reshape(4, 128, FEAT), 'inner', 0, 0, axis_index_gro...]
    all_to_all x0 -> x1, blocking collectives: none -> 24.8 us  [plane_exchange(): lax.all_to_all(x, 'inner', 0, 0, axis_index_groups=PLANES, tiled=True)]
    ppermute x24 -> x3, waiting for transfers between devices: 26.7 us -> 2.53 us  [along_z(): lax.ppermute(x, 'inner', [(i, (i + 16 * distance) % 64) for i in range(64)])]
    all_to_all x3, waiting for transfers between devices: 3.38 us -> 12.2 us  [plane_exchange(): lax.all_to_all(x, 'inner', 0, 0, axis_index_groups=PLANES, tiled=True)]
    unnamed x37 -> x18, local copies, waits for them, and re-layouts: 9.89 us -> 3.38 us
    all_to_all x0 -> x1, starting transfers between devices: none -> 5.98 us  [local(): lax.all_to_all(mixed.reshape(4, 128, FEAT), 'inner', 0, 0, axis_index_gro...]
    all_to_all x3, starting transfers between devices: 16.1 us -> 11 us  [plane_exchange(): lax.all_to_all(x, 'inner', 0, 0, axis_index_groups=PLANES, tiled=True)]
  transfers between devices with their start and end apart: 31 -> 10, of which waited for: 11 -> 6; matrix products, arithmetic and copies ran while one was open for 1% -> 1% of each run, Pallas kernels for 30% -> 27%
where the time goes in v3:
time: 163 us; the launch traced here: 162 us
  Pallas kernels  61.3 us (38%)
  waiting for transfers between devices  41.8 us (26%)
  starting transfers between devices  26.2 us (16%)
  blocking collectives  24.8 us (15%)
  local copies, waits for them, and re-layouts  6.6 us (4%)
    all_to_all x1, waiting for transfers between devices, local(): lax.all_to_all(mixed.reshape(4, 128, FEAT), 'inner', 0, 0, axis_index_gro...  25.2 us
    all_to_all x1, blocking collectives, plane_exchange(): lax.all_to_all(x, 'inner', 0, 0, axis_index_groups=PLANES, tiled=True)  24.8 us
    pallas_call x1, Pallas kernels, last_factor(): pl.pallas_call(last_factor_kernel, out_shape=jax.ShapeDtypeStruct((8, FEA...  23.1 us
    all_to_all x3, waiting for transfers between devices, plane_exchange(): lax.all_to_all(x, 'inner', 0, 0, axis_index_groups=PLANES, tiled=True)  12.2 us
    all_to_all x3, starting transfers between devices, plane_exchange(): lax.all_to_all(x, 'inner', 0, 0, axis_index_groups=PLANES, tiled=True)  11 us
    pallas_call x1, Pallas kernels, first_factor(): pl.pallas_call(first_factor_kernel, out_shape=(SQUARE, INVERSES), in_spec...  10.9 us
    pallas_call x1, Pallas kernels, middle_factor(): pl.pallas_call(middle_factor_kernel, out_shape=(SQUARE, INVERSES), in_spe...  10.1 us
    ppermute x3, starting transfers between devices, swap_cores(): return lax.ppermute(x, 'outer', [(0, 1), (1, 0)])  6.21 us
  transfers between devices with their start and end apart: 10, of which 6 were waited for; matrix products, arithmetic and copies ran while one was open for 1% of the time, Pallas kernels for 27%

profile of v3, /device:TPU:1, one launch (start us, length us, event | category | flops | bytes accessed | tf_op | source)
XLA Modules:
  0.0 162.2 jit_solution(14268640132029660960)
XLA Ops:
  0.6 5.0 %shard_map.77 = f32[512,1024]{1,0:T(8,128)} custom-call(bf16[512,512]{1,0:T(8,128)(2,1)} %constant.24.clone.table_ref, s32[1,512]{1,0:T(1,128)} %bitcast.26, f32[512,1024]{1,0:T(8,128)} %x_ref.1), custom_call_target="tpu_custom_call" | custom-call | tf_op jit(solution)/shard_map/pallas_call | solution.py:72
  5.6 6.0 %all-to-all-start = ((f32[4,128,1024]{2,1,0:T(8,128)}), f32[4,128,1024]{2,1,0:T(8,128)S(1)}, u32[]{:S(2)}, u32[]{:S(2)}) async-start(f32[4,128,1024]{2,1,0:T(8,128)} %bitcast.14), calls=%async_computation | async-start | bytes 4194304 | tf_op jit(solution)/shard_map/all_to_all | solution.py:449
  11.8 25.2 %all-to-all-done.y_ref = f32[4,128,1024]{2,1,0:T(8,128)S(1)} async-done(((f32[4,128,1024]{2,1,0:T(8,128)}), f32[4,128,1024]{2,1,0:T(8,128)S(1)}, u32[]{:S(2)}, u32[]{:S(2)}) %all-to-all-start) | async-done | bytes 2097184 | tf_op jit(solution)/shard_map/all_to_all | solution.py:449
  38.4 3.8 %shard_map.78 = f32[16,2,8,1024]{3,2,1,0:T(8,128)} custom-call(s32[128,2]{1,0:T(8,128)} %bitcast.22, f32[4,128,1024]{2,1,0:T(8,128)} %copy-done), custom_call_target="tpu_custom_call" | custom-call | tf_op jit(solution)/shard_map/pallas_call | solution.py:110
  42.2 1.9 %collective-permute-start = (f32[256,1024]{1,0:T(8,128)}, f32[256,1024]{1,0:T(8,128)S(1)}, u32[]{:S(2)}, u32[]{:S(2)}) collective-permute-start(f32[256,1024]{1,0:T(8,128)} %bitcast.15), channel_id=1, source_target_pairs={{0,64},{64,0},{1,65},{65,1},{2,66},{66,2},{3,67},{67,3},{4,68},{68... | collective-permute-start | bytes 3145736 | tf_op jit(solution)/shard_map/ppermute | solution.py:426
  44.7 1.8 %collective-permute-done.w_ref = f32[256,1024]{1,0:T(8,128)S(1)} collective-permute-done((f32[256,1024]{1,0:T(8,128)}, f32[256,1024]{1,0:T(8,128)S(1)}, u32[]{:S(2)}, u32[]{:S(2)}) %collective-permute-start) | collective-permute-done | bytes 1048608 | tf_op jit(solution)/shard_map/ppermute | solution.py:426
  46.6 1.0 copy-done.2
  47.6 4.5 %shard_map.79 = (f32[16,144,128]{2,1,0:T(8,128)}, f32[16,2,8,1024]{3,2,1,0:T(8,128)}) custom-call(s32[2]{0:T(128)} %pad_add_fusion.ids_ref, f32[256,1024]{1,0:T(8,128)} %bitcast.16, f32[256,1024]{1,0:T(8,128)} %copy-done.2), custom_call_target="tpu_custom_call" | custom-call | tf_op jit(solution)/shard_map/pallas_call | solution.py:162
  52.1 24.8 %all_to_all.25 = f32[16,144,128]{2,1,0:T(8,128)S(1)} all-to-all(f32[16,144,128]{2,1,0:T(8,128)} %get-tuple-element.14), channel_id=1, replica_groups={{0,1,2,3,4,5,6,7,8,9,10,11,12,13,14,15},{16,17,18,19,20,21,22,23,24,25,..., dimensions={0} | all-to-all | bytes 2359296 | tf_op jit(solution)/shard_map/all_to_all | solution.py:434
  77.3 1.2 collective-permute-start.2
  78.5 1.5 collective-permute-start.3
  80.0 1.9 %collective-permute-done.1 = f32[144,128]{1,0:T(8,128)S(1)} collective-permute-done((f32[144,128]{1,0:T(8,128)S(1)}, f32[144,128]{1,0:T(8,128)S(1)}, u32[]{:S(2)}, u32[]{:S(2)}) %collective-permute-start.1) | collective-permute-done | bytes 73760 | tf_op jit(solution)/shard_map/ppermute | solution.py:430
  83.3 3.7 %all-to-all-start.2 = ((f32[16,40,128]{2,1,0:T(8,128)}), f32[16,40,128]{2,1,0:T(8,128)S(1)}, u32[]{:S(2)}, u32[]{:S(2)}) async-start(f32[16,40,128]{2,1,0:T(8,128)} %broadcast_in_dim.8), calls=%async_computation.2 | async-start | bytes 655360 | tf_op jit(solution)/shard_map/all_to_all | solution.py:434
  87.1 7.9 %all-to-all-done.2 = f32[16,40,128]{2,1,0:T(8,128)S(1)} async-done(((f32[16,40,128]{2,1,0:T(8,128)}), f32[16,40,128]{2,1,0:T(8,128)S(1)}, u32[]{:S(2)}, u32[]{:S(2)}) %all-to-all-start.2) | async-done | bytes 327712 | tf_op jit(solution)/shard_map/all_to_all | solution.py:434
  94.9 1.0 broadcast_in_dim.7
  96.0 3.6 %collective-permute-start.5 = (f32[640,128]{1,0:T(8,128)S(1)}, f32[640,128]{1,0:T(8,128)S(1)}, u32[]{:S(2)}, u32[]{:S(2)}) collective-permute-start(f32[640,128]{1,0:T(8,128)S(1)} %bitcast.20), channel_id=1, source_target_pairs={{0,64},{64,0},{1,65},{65,1},{2,66},{66,2},{3,67},{67,3},{4,68},{68... | collective-permute-start | bytes 983048 | tf_op jit(solution)/shard_map/ppermute | solution.py:426
  100.1 3.6 %all-to-all-start.3 = ((f32[16,104,128]{2,1,0:T(8,128)}), f32[16,104,128]{2,1,0:T(8,128)S(1)}, u32[]{:S(2)}, u32[]{:S(2)}) async-start(f32[16,104,128]{2,1,0:T(8,128)} %broadcast_in_dim.7), calls=%async_computation.3 | async-start | bytes 1703936 | tf_op jit(solution)/shard_map/all_to_all | solution.py:434
  104.5 10.9 %shard_map.81 = (f32[512,512]{1,0:T(8,128)}, f32[2,128,128]{2,1,0:T(8,128)}) custom-call(s32[2]{0:T(128)} %pad_add_fusion.ids_ref, f32[1,512]{1,0:T(1,128)} %get-tuple-element.24.ridge_ref, f32[640,128]{1,0:T(8,128)} %bitcast.21, f32[640,128]{1,0:T(8,128)} %copy-done.8), custom_call_target="tpu_custom_call" | custom-call | flops 12000000000 | bytes 2097152 | tf_op jit(solution)/shard_map/pallas_call | solution.py:390
  115.4 4.3 %all-to-all-done.3 = f32[16,104,128]{2,1,0:T(8,128)S(1)} async-done(((f32[16,104,128]{2,1,0:T(8,128)}), f32[16,104,128]{2,1,0:T(8,128)S(1)}, u32[]{:S(2)}, u32[]{:S(2)}) %all-to-all-start.3) | async-done | bytes 852000 | tf_op jit(solution)/shard_map/all_to_all | solution.py:434
  120.5 10.1 %shard_map.82 = (f32[512,512]{1,0:T(8,128)}, f32[2,128,128]{2,1,0:T(8,128)}) custom-call(f32[512,512]{1,0:T(8,128)} %get-tuple-element.20.given_ref), custom_call_target="tpu_custom_call" | custom-call | flops 12000000000 | bytes 2097152 | tf_op jit(solution)/shard_map/pallas_call | solution.py:402
  130.6 3.7 %all-to-all-start.4 = ((f32[16,2,8,1024]{3,2,1,0:T(8,128)}), f32[16,2,8,1024]{3,2,1,0:T(8,128)S(1)}, u32[]{:S(2)}, u32[]{:S(2)}) async-start(f32[16,2,8,1024]{3,2,1,0:T(8,128)} %get-tuple-element.16), calls=%async_computation.4 | async-start | bytes 2097152 | tf_op jit(solution)/shard_map/all_to_all | solution.py:434
  134.2 23.1 %shard_map.83 = f32[8,1024]{1,0:T(8,128)} custom-call(s32[2]{0:T(128)} %pad_add_fusion.ids_ref, f32[1,512]{1,0:T(1,128)} %get-tuple-element.25.ridge_ref, f32[1664,128]{1,0:T(8,128)} %bitcast.19, f32[1664,128]{1,0:T(8,128)} %copy-done.7, f32[512,512]{1,0:T(8,128)} %get-tuple-element.21.u_ref, f32[2,128,128]{2,1,0:T(8,128)} %get-tuple-element.22.inv1_ref, ...), custom_call_target="tpu_custom_call" | custom-call | flops 30000001024 | bytes 2097152 | tf_op jit(solution)/shard_map/pallas_call | solution.py:414
  157.4 1.0 copy-done.1
  158.4 3.8 %shard_map.80 = f32[256,1024]{1,0:T(8,128)} custom-call(s32[2]{0:T(128)} %pad_add_fusion.ids_ref, bf16[256,256]{1,0:T(8,128)(2,1)} %constant.25.clone.table_ref, f32[256,1024]{1,0:T(8,128)} %bitcast.17), custom_call_target="tpu_custom_call" | custom-call | tf_op jit(solution)/shard_map/pallas_call | solution.py:187
  (34 shorter events, 6.2 us)
Async XLA Ops:
  5.6 6.0 %copy-start.6 = (s32[128,2]{0,1:T(2,128)S(1)}, s32[128,2]{0,1:T(2,128)}, u32[]{:S(2)}) copy-start(s32[128,2]{0,1:T(2,128)} %param.8) | copy-start | bytes 3076
  5.6 31.4 %all-to-all-start = ((f32[4,128,1024]{2,1,0:T(8,128)}), f32[4,128,1024]{2,1,0:T(8,128)S(1)}, u32[]{:S(2)}, u32[]{:S(2)}) async-start(f32[4,128,1024]{2,1,0:T(8,128)} %bitcast.14), calls=%async_computation | async-start | bytes 4194304 | tf_op jit(solution)/shard_map/all_to_all | solution.py:449
  37.0 1.4 copy-start
  42.2 4.4 %collective-permute-start = (f32[256,1024]{1,0:T(8,128)}, f32[256,1024]{1,0:T(8,128)S(1)}, u32[]{:S(2)}, u32[]{:S(2)}) collective-permute-start(f32[256,1024]{1,0:T(8,128)} %bitcast.15), channel_id=1, source_target_pairs={{0,64},{64,0},{1,65},{65,1},{2,66},{66,2},{3,67},{67,3},{4,68},{68... | collective-permute-start | bytes 3145736 | tf_op jit(solution)/shard_map/ppermute | solution.py:426
  46.6 1.0 copy-start.2
  76.9 22.6 %copy-start.5 = (f32[1024]{0:T(1024)S(1)}, f32[1024]{0:T(1024)}, u32[]{:S(2)}) copy-start(f32[1024]{0:T(1024)} %param.9) | copy-start | bytes 12292
  77.0 4.9 %collective-permute-start.1 = (f32[144,128]{1,0:T(8,128)S(1)}, f32[144,128]{1,0:T(8,128)S(1)}, u32[]{:S(2)}, u32[]{:S(2)}) collective-permute-start(f32[144,128]{1,0:T(8,128)S(1)} %reduce_sum.9), channel_id=1, source_target_pairs={{0,32},{1,33},{2,34},{3,35},{4,36},{5,37},{6,38},{7,39},{8,40},{9,... | collective-permute-start | bytes 221192 | tf_op jit(solution)/shard_map/ppermute | solution.py:430
  77.3 5.2 %collective-permute-start.2 = (f32[144,128]{1,0:T(8,128)S(1)}, f32[144,128]{1,0:T(8,128)S(1)}, u32[]{:S(2)}, u32[]{:S(2)}) collective-permute-start(f32[144,128]{1,0:T(8,128)S(1)} %reduce_sum.9), channel_id=1, source_target_pairs={{0,16},{1,17},{2,18},{3,19},{4,20},{5,21},{6,22},{7,23},{8,24},{9,... | collective-permute-start | bytes 221192 | tf_op jit(solution)/shard_map/ppermute | solution.py:430
  78.5 4.0 %collective-permute-start.3 = (f32[144,128]{1,0:T(8,128)S(1)}, f32[144,128]{1,0:T(8,128)S(1)}, u32[]{:S(2)}, u32[]{:S(2)}) collective-permute-start(f32[144,128]{1,0:T(8,128)S(1)} %reduce_sum.9), channel_id=1, source_target_pairs={{0,48},{1,49},{2,50},{3,51},{4,52},{5,53},{6,54},{7,55},{8,56},{9,... | collective-permute-start | bytes 221192 | tf_op jit(solution)/shard_map/ppermute | solution.py:430
  83.3 11.6 %all-to-all-start.2 = ((f32[16,40,128]{2,1,0:T(8,128)}), f32[16,40,128]{2,1,0:T(8,128)S(1)}, u32[]{:S(2)}, u32[]{:S(2)}) async-start(f32[16,40,128]{2,1,0:T(8,128)} %broadcast_in_dim.8), calls=%async_computation.2 | async-start | bytes 655360 | tf_op jit(solution)/shard_map/all_to_all | solution.py:434
  94.9 8.8 %copy-start.4 = (f32[16,40,128]{2,1,0:T(8,128)}, f32[16,40,128]{2,1,0:T(8,128)S(1)}, u32[]{:S(2)}) copy-start(f32[16,40,128]{2,1,0:T(8,128)S(1)} %all-to-all-done.2) | copy-start | bytes 983044
  96.0 7.8 %collective-permute-start.5 = (f32[640,128]{1,0:T(8,128)S(1)}, f32[640,128]{1,0:T(8,128)S(1)}, u32[]{:S(2)}, u32[]{:S(2)}) collective-permute-start(f32[640,128]{1,0:T(8,128)S(1)} %bitcast.20), channel_id=1, source_target_pairs={{0,64},{64,0},{1,65},{65,1},{2,66},{66,2},{3,67},{67,3},{4,68},{68... | collective-permute-start | bytes 983048 | tf_op jit(solution)/shard_map/ppermute | solution.py:426
  100.1 19.6 %all-to-all-start.3 = ((f32[16,104,128]{2,1,0:T(8,128)}), f32[16,104,128]{2,1,0:T(8,128)S(1)}, u32[]{:S(2)}, u32[]{:S(2)}) async-start(f32[16,104,128]{2,1,0:T(8,128)} %broadcast_in_dim.7), calls=%async_computation.3 | async-start | bytes 1703936 | tf_op jit(solution)/shard_map/all_to_all | solution.py:434
  103.7 0.7 copy-start.8
  119.7 10.9 %copy-start.3 = (f32[16,104,128]{2,1,0:T(8,128)}, f32[16,104,128]{2,1,0:T(8,128)S(1)}, u32[]{:S(2)}) copy-start(f32[16,104,128]{2,1,0:T(8,128)S(1)} %all-to-all-done.3) | copy-start | bytes 2555908
  119.7 10.9 %collective-permute-start.4 = (f32[1664,128]{1,0:T(8,128)S(1)}, f32[1664,128]{1,0:T(8,128)S(1)}, u32[]{:S(2)}, u32[]{:S(2)}) collective-permute-start(f32[1664,128]{1,0:T(8,128)S(1)} %bitcast.18), channel_id=1, source_target_pairs={{0,64},{64,0},{1,65},{65,1},{2,66},{66,2},{3,67},{67,3},{4,68},{68... | collective-permute-start | bytes 2555912 | tf_op jit(solution)/shard_map/ppermute | solution.py:426
  130.6 3.7 %copy-start.7 = (f32[1664,128]{1,0:T(8,128)}, f32[1664,128]{1,0:T(8,128)S(1)}, u32[]{:S(2)}) copy-start(f32[1664,128]{1,0:T(8,128)S(1)} %collective-permute-done.4.other_ref) | copy-start | bytes 2555908
  130.6 26.8 %all-to-all-start.4 = ((f32[16,2,8,1024]{3,2,1,0:T(8,128)}), f32[16,2,8,1024]{3,2,1,0:T(8,128)S(1)}, u32[]{:S(2)}, u32[]{:S(2)}) async-start(f32[16,2,8,1024]{3,2,1,0:T(8,128)} %get-tuple-element.16), calls=%async_computation.4 | async-start | bytes 2097152 | tf_op jit(solution)/shard_map/all_to_all | solution.py:434
  157.4 1.0 copy-start.1

commit v4 on v1

--- a/solution.py
+++ b/solution.py
@@ -1,5 +1,3 @@
-import functools
-
 import jax
 import jax.numpy as jnp
 import numpy as np
@@ -8,7 +6,6 @@
 from jax.experimental.pallas import tpu as pltpu
 from jax.sharding import PartitionSpec as P
 
-precise = lax.Precision.HIGHEST
 f32 = jnp.float32
 bf16 = jnp.bfloat16
 VMEM = pl.BlockSpec(memory_space=pltpu.VMEM)
@@ -17,12 +14,14 @@
 NB = 128
 PANELS = FEAT // NB
 STRIPS = ((0, 3, 4, 7), (1, 2, 5, 6))
-HALF_BLOCKS = 18
+GRAM_ROWS = 144
+LEFT = (0, 0, 0, 1, 1, 2)
+RIGHT = (0, 1, 2, 0, 1, 0)
 Z_GROUPS = [[i + 16 * j for j in range(4)] for i in range(16)]
 PLANES = [[16 * j + i for i in range(16)] for j in range(4)]
 
 
-def params(mib=48):
+def params(mib=32):
     return pltpu.CompilerParams(vmem_limit_bytes=mib << 20)
 
 
@@ -42,7 +41,7 @@
 
 def final_table():
     j, i, o, e = (v.reshape(-1, 1) for v in np.meshgrid(range(2), range(16), range(2), range(4), indexing="ij"))
-    ip, op, jp, ep = (v.reshape(1, -1) for v in np.meshgrid(range(16), range(2), range(2), range(4), indexing="ij"))
+    op, ip, jp, ep = (v.reshape(1, -1) for v in np.meshgrid(range(2), range(16), range(2), range(4), indexing="ij"))
     table = parity_sign(i, ip) * parity_sign(o, op) * (j == jp) * (e == ep)
     return table.astype(np.float32).astype(bf16)
 
@@ -83,7 +82,7 @@
         ],
         out_specs=pl.BlockSpec((rows, cols), lambda g: (0, g)),
         scratch_shapes=[pltpu.VMEM((rows, rows), bf16)],
-        compiler_params=params(),
+        compiler_params=params(60),
     )(jnp.asarray(local_table()), sign_flip.reshape(1, rows), matrix)
 
 
@@ -123,71 +122,99 @@
     )(keep_rows, y)
 
 
-def gram_kernel(ids_ref, v_ref, w_ref, g_ref, s_ref, high, low):
+def gram_kernel(ids_ref, v_ref, w_ref, g_ref, high, low, flat):
     core = ids_ref[0]
+    own = pl.ds(pl.multiple_of(core * 128, 128), 128)
     for part, ref in enumerate((v_ref, w_ref)):
         h, l = halves(ref[...])
         high[256 * part : 256 * part + 256, :] = h
         low[256 * part : 256 * part + 256, :] = l
-        own = ref[pl.ds(pl.multiple_of(core * 128, 128), 128), :]
-        s_ref[:, part] = own.reshape(16, 8, FEAT)
+        rows = ref[own, :].reshape(16, 8, FEAT)
+        for block in range(PANELS):
+            at = GRAM_ROWS + 8 * (PANELS * part + block)
+            g_ref[:, at : at + 8] = rows[:, :, NB * block : NB * block + NB]
     for which, strips in enumerate(STRIPS):
 
         @pl.when(core == which)
         def _():
-            slot = 0
+            row = 0
             for strip in strips:
                 at = NB * strip
                 h, l = high[:, at : at + NB], low[:, at : at + NB]
-                right, right_low = high[:, at:], low[:, at:]
-                total = tmm(h, right) + (tmm(h, right_low) + tmm(l, right))
+                total = tmm(h, high[:, at:]) + (tmm(h, low[:, at:]) + tmm(l, high[:, at:]))
                 for block in range(PANELS - strip):
-                    g_ref[slot] = total[:, NB * block : NB * block + NB]
-                    slot += 1
+                    flat[row : row + NB, :] = total[:, NB * block : NB * block + NB]
+                    row += NB
+
+    for piece in range(16):
+        g_ref[piece, :GRAM_ROWS] = flat[GRAM_ROWS * piece : GRAM_ROWS * (piece + 1), :]
 
 
 def gram_half(ids, mine, theirs):
     rows = mine.shape[0]
     return pl.pallas_call(
         gram_kernel,
-        out_shape=(
-            jax.ShapeDtypeStruct((HALF_BLOCKS, NB, NB), f32),
-            jax.ShapeDtypeStruct((16, 2, 8, FEAT), f32),
-        ),
+        out_shape=jax.ShapeDtypeStruct((16, GRAM_ROWS + 128, NB), f32),
         in_specs=[SMEM, VMEM, VMEM],
-        out_specs=(VMEM, VMEM),
-        scratch_shapes=[pltpu.VMEM((2 * rows, FEAT), bf16)] * 2,
+        out_specs=VMEM,
+        scratch_shapes=[pltpu.VMEM((2 * rows, FEAT), bf16)] * 2 + [pltpu.VMEM((16 * GRAM_ROWS, NB), f32)],
         compiler_params=params(),
     )(ids, mine, theirs)
 
 
-def final_kernel(ids_ref, table_ref, r_ref, o_ref):
-    high, low = halves(r_ref[...])
-    total = mm(table_ref[...], high) + mm(table_ref[...], low)
+def final_kernel(ids_ref, table_ref, r_ref, o_ref, high, low):
+    for part in range(2):
+        for block in range(PANELS):
+            at = GRAM_ROWS + 8 * (PANELS * part + block)
+            h, l = halves(r_ref[:, at : at + 8].reshape(128, NB))
+            high[128 * part : 128 * part + 128, NB * block : NB * block + NB] = h
+            low[128 * part : 128 * part + 128, NB * block : NB * block + NB] = l
+    total = mm(table_ref[...], high[...]) + mm(table_ref[...], low[...])
     odd = (lax.broadcasted_iota(jnp.int32, total.shape, 0) >> 2) & 1
     flip = (odd * ids_ref[0]) == 1
     o_ref[...] = total * jnp.where(flip, -32.0, 32.0)
 
 
 def final_mix(ids, received):
-    rows, features = received.shape
-    cols = 256
+    rows = 256
     return pl.pallas_call(
         final_kernel,
-        grid=(features // cols,),
-        out_shape=jax.ShapeDtypeStruct((rows, features), f32),
-        in_specs=[
-            SMEM,
-            pl.BlockSpec((rows, rows), lambda g: (0, 0)),
-            pl.BlockSpec((rows, cols), lambda g: (0, g)),
-        ],
-        out_specs=pl.BlockSpec((rows, cols), lambda g: (0, g)),
+        out_shape=jax.ShapeDtypeStruct((rows, FEAT), f32),
+        in_specs=[SMEM, VMEM, VMEM],
+        out_specs=VMEM,
+        scratch_shapes=[pltpu.VMEM((rows, FEAT), bf16)] * 2,
         compiler_params=params(),
+        cost_estimate=pl.CostEstimate(flops=2_000_000_000, bytes_accessed=4 << 20, transcendentals=0),
     )(ids, jnp.asarray(final_table()), received)
 
 
 def lane_splat(x, lane):
     return jnp.broadcast_to(x[:, lane : lane + 1], (8, NB))
+
+
+def thirds(x):
+    high = x.astype(bf16).astype(f32)
+    rest = x - high
+    middle = rest.astype(bf16).astype(f32)
+    return high, middle, rest - middle
+
+
+def pieces3(x):
+    return tuple(part.astype(bf16) for part in thirds(x))
+
+
+def outer_sum(left, right):
+    lh, lm, ll = thirds(left)
+    rh, rm, rl = thirds(right)
+    stacked_left = jnp.concatenate([lh, lh, lh, lm, lm, ll], axis=0).astype(bf16)
+    stacked_right = jnp.concatenate([rh, rm, rl, rh, rm, rh], axis=0).astype(bf16)
+    return tmm(stacked_left, stacked_right)
+
+
+def tree_sum(terms):
+    while len(terms) > 1:
+        terms = [x + y for x, y in zip(terms[::2], terms[1::2])]
+    return terms[0]
 
 
 def factor_block(w, upper, inverse):
@@ -204,9 +231,6 @@
         base = 8 * step
         inside = (lane >= base) & (lane < base + 8)
         aug = [jnp.where(inside, jnp.where(lane == base + b, 1.0, 0.0), rho[b]) for b in range(8)]
-        if step < 15:
-            coming = [jnp.where(inside, 0.0, row_splat(base + 8 + a)) for a in range(8)]
-            start = {(a, b): lane_splat(coming[a], base + 8 + b) for a, b in pairs}
         u, t = [None] * 8, [None] * 8
         for b in range(8):
             r = lax.rsqrt(e[b, b])
@@ -218,38 +242,29 @@
             for a in range(b + 1, 8):
                 rho[a] = rho[a] - c[a] * u[b]
                 aug[a] = aug[a] - c[a] * t[b]
-        for b in range(8):
-            upper[base + b : base + b + 1, :] = jnp.where(lane >= base + b, u[b], 0.0)[0:1]
-            inverse[base + b : base + b + 1, :] = jnp.where(lane <= base + b, t[b], 0.0)[0:1]
-        if step < 15:
-            c = {(b, a): lane_splat(u[b], base + 8 + a) for b in range(8) for a in range(8)}
-            e = {}
-            for a, a2 in pairs:
-                total = c[0, a] * c[0, a2]
-                for b in range(1, 8):
-                    total = total + c[b, a] * c[b, a2]
-                e[a, a2] = start[a, a2] - total
-            for a in range(8):
-                total = c[0, a] * t[0]
-                for b in range(1, 8):
-                    total = total + c[b, a] * t[b]
-                coming[a] = coming[a] - total
-            rho = coming
+        left, right = u[0], t[0]
+        for b in range(1, 8):
+            left = jnp.where(sub == b, u[b], left)
+            right = jnp.where(sub == b, t[b], right)
+        upper[base : base + 8, :] = jnp.where(lane >= base + sub, left, 0.0)
+        inverse[base : base + 8, :] = jnp.where(lane <= base + sub, right, 0.0)
+        if step == 15:
+            break
+        if step < 14:
+            update = outer_sum(left, right)
+        coming = [jnp.where(inside, 0.0, row_splat(base + 8 + a)) for a in range(8)]
+        c = {(b, a): lane_splat(u[b], base + 8 + a) for b in range(8) for a in range(8)}
+        e = {(a, a2): lane_splat(coming[a], base + 8 + a2) for a, a2 in pairs}
+        e = {(a, a2): e[a, a2] - tree_sum([c[b, a] * c[b, a2] for b in range(8)]) for a, a2 in pairs}
+        rho = [coming[a] - tree_sum([c[b, a] * t[b] for b in range(8)]) for a in range(8)]
         if step < 14:
             after = base + 16
-            left, right = u[0], t[0]
-            for b in range(1, 8):
-                left = jnp.where(sub == b, u[b], left)
-                right = jnp.where(sub == b, t[b], right)
-            update = lax.dot_general(
-                left, right, (((0,), (0,)), ((), ())), precision=precise, preferred_element_type=f32
-            )
             rest = lax.broadcasted_iota(jnp.int32, (NB - after, NB), 1)
             cleared = jnp.where((rest >= base) & (rest < base + 8), 0.0, w[after:, :])
             w[after:, :] = cleared - update[after:, :]
 
 
-def factor_kernel(ids_ref, ridge_ref, own_ref, other_ref, o_ref, a, w, upper, inverse):
+def factor_kernel(ids_ref, ridge_ref, own_ref, other_ref, o_ref, a, w, upper, inverse, stack1, stack2):
     core, position = ids_ref[0], ids_ref[1]
     eye = lax.broadcasted_iota(jnp.int32, (NB, NB), 0) == lax.broadcasted_iota(jnp.int32, (NB, NB), 1)
     for which in range(2):
@@ -260,7 +275,7 @@
                 slot = 0
                 for strip in strips:
                     for block in range(strip, PANELS):
-                        piece = ref[slot]
+                        piece = ref[NB * slot : NB * slot + NB, :]
                         if block == strip:
                             ridge = ridge_ref[0:1, NB * strip : NB * strip + NB]
                             piece = piece + jnp.where(eye, ridge, 0.0)
@@ -278,17 +293,21 @@
                 s0, s1 = NB * fixed, NB * fixed + NB
                 a[s0:s1, s0:s1] = upper[...]
                 if fixed < PANELS - 1:
-                    rows = jnp.dot(inverse[...], a[s0:s1, s1:], precision=precise, preferred_element_type=f32)
+                    inv, rest = pieces3(inverse[...]), pieces3(a[s0:s1, s1:])
+                    rows = mm(
+                        jnp.concatenate([inv[k] for k in LEFT], axis=1),
+                        jnp.concatenate([rest[k] for k in RIGHT], axis=0),
+                    )
                     a[s0:s1, s1:] = rows
+                    width = FEAT - s1
+                    parts = pieces3(rows)
+                    for k in range(6):
+                        stack1[NB * k : NB * k + NB, :width] = parts[LEFT[k]]
+                        stack2[NB * k : NB * k + NB, :width] = parts[RIGHT[k]]
                     for strip in range(fixed + 1, PANELS):
                         b0, t0 = NB * (strip - fixed - 1), NB * strip
-                        a[t0 : t0 + NB, t0:] = a[t0 : t0 + NB, t0:] - lax.dot_general(
-                            rows[:, b0 : b0 + NB],
-                            rows[:, b0:],
-                            (((0,), (0,)), ((), ())),
-                            precision=precise,
-                            preferred_element_type=f32,
-                        )
+                        update = tmm(stack1[:, b0 : b0 + NB], stack2[:, b0:width])
+                        a[t0 : t0 + NB, t0:] = a[t0 : t0 + NB, t0:] - update
 
         return carry
 
@@ -304,7 +323,8 @@
         out_shape=jax.ShapeDtypeStruct((8, FEAT), f32),
         in_specs=[SMEM, VMEM, VMEM, VMEM],
         out_specs=VMEM,
-        scratch_shapes=[pltpu.VMEM((FEAT, FEAT), f32)] + [pltpu.VMEM((NB, NB), f32)] * 3,
+        scratch_shapes=[pltpu.VMEM((FEAT, FEAT), f32)] + [pltpu.VMEM((NB, NB), f32)] * 3
+        + [pltpu.VMEM((6 * NB, FEAT), bf16)] * 2,
         compiler_params=params(),
         cost_estimate=pl.CostEstimate(flops=40_000_000_000, bytes_accessed=2 << 20, transcendentals=0),
     )(ids, ridge, own, other)
@@ -333,16 +353,13 @@
     )
     mine = select_rows(keep_rows, along).reshape(256, FEAT)
     theirs = swap_cores(mine)
-    gram, to_send = gram_half(ids, mine, theirs)
-    pieces = plane_exchange(gram.reshape(16, 144, 128))
-    piece = jnp.sum(pieces, axis=0)
+    received = plane_exchange(gram_half(ids, mine, theirs))
+    piece = jnp.sum(received[:, :GRAM_ROWS], axis=0)
     piece = (piece + along_z(piece, 2)) + (along_z(piece, 1) + along_z(piece, 3))
-    own = plane_exchange(jnp.broadcast_to(piece[None], (16, 144, 128))).reshape(HALF_BLOCKS, NB, NB)
+    own = plane_exchange(jnp.broadcast_to(piece[None], (16, GRAM_ROWS, NB))).reshape(16 * GRAM_ROWS, NB)
+    sketch = final_mix(ids, received)
     other = swap_cores(own)
-    to_send, own, other = lax.optimization_barrier((to_send, own, other))
-    received = plane_exchange(to_send)
     factor = factor_rows(ids, ridge_weights.reshape(1, FEAT), own, other)
-    sketch = final_mix(ids, received.reshape(256, FEAT))
     return sketch, factor
 
 

time: 162 us -> 150 us (0.926)
  local copies, waits for them, and re-layouts: 10.4 us -> 0.29 us
  blocking collectives: 45 us -> 54.3 us
  Pallas kernels: 55 us -> 48.3 us
  starting transfers between devices: 17.7 us -> 14.1 us
    unnamed x24 -> x6, local copies, waits for them, and re-layouts: 10.1 us -> 0.01 us
    all_to_all x2, blocking collectives: 45 us -> 54.3 us  [plane_exchange(): lax.all_to_all(x, 'inner', 0, 0, axis_index_groups=PLANES, tiled=True)]
    pallas_call x1, Pallas kernels: 47 us -> 38 us  [factor_rows(): pl.pallas_call(factor_kernel, out_shape=jax.ShapeDtypeStruct((8, FEAT), f...]
    all_to_all x1 -> x0, starting transfers between devices: 3.66 us -> none  [plane_exchange(): lax.all_to_all(x, 'inner', 0, 0, axis_index_groups=PLANES, tiled=True)]
    pallas_call x1, Pallas kernels: 2.19 us -> 5.01 us  [local_mix(): pl.pallas_call(local_mix_kernel, grid=(features // cols,), out_shape=jax....]
    ppermute x2, waiting for transfers between devices: 4.69 us -> 2.58 us  [swap_cores(): return lax.ppermute(x, 'outer', [(0, 1), (1, 0)])]
    ppermute x3, waiting for transfers between devices: 2.53 us -> 4.43 us  [along_z(): lax.ppermute(x, 'inner', [(i, (i + 16 * distance) % 64) for i in range(64)])]
  transfers between devices with their start and end apart: 7 -> 6, of which waited for: 5 -> 6; matrix products, arithmetic and copies ran while one was open for 0% -> 0% of each run, Pallas kernels for 29% -> 1%
where the time goes in v4:
time: 150 us
  blocking collectives  54.3 us (36%)
  Pallas kernels  48.3 us (32%)
  waiting for transfers between devices  32.2 us (21%)
  starting transfers between devices  14.1 us (9%)
    all_to_all x2, blocking collectives, plane_exchange(): lax.all_to_all(x, 'inner', 0, 0, axis_index_groups=PLANES, tiled=True)  54.3 us
    pallas_call x1, Pallas kernels, factor_rows(): pl.pallas_call(factor_kernel, out_shape=jax.ShapeDtypeStruct((8, FEAT), f...  38 us
    all_to_all x1, waiting for transfers between devices, local(): lax.all_to_all(mixed.reshape(4, 128, FEAT), 'inner', 0, 0, axis_index_gro...  25.2 us
    all_to_all x1, starting transfers between devices, local(): lax.all_to_all(mixed.reshape(4, 128, FEAT), 'inner', 0, 0, axis_index_gro...  5.99 us
    ppermute x2, starting transfers between devices, swap_cores(): return lax.ppermute(x, 'outer', [(0, 1), (1, 0)])  5.86 us
    pallas_call x1, Pallas kernels, local_mix(): pl.pallas_call(local_mix_kernel, grid=(features // cols,), out_shape=jax....  5.01 us
    ppermute x3, waiting for transfers between devices, along_z(): lax.ppermute(x, 'inner', [(i, (i + 16 * distance) % 64) for i in range(64)])  4.43 us
  transfers between devices with their start and end apart: 6, of which 6 were waited for; matrix products, arithmetic and copies ran while one was open for 0% of the time, Pallas kernels for 1%

profile of v4, /device:TPU:1, one launch (start us, length us, event | category | flops | bytes accessed | tf_op | source)
XLA Modules:
  0.0 150.1 jit_solution(5797020543857614407)
XLA Ops:
  0.6 5.0 %shard_map.77 = f32[512,1024]{1,0:T(8,128)} custom-call(bf16[512,512]{1,0:T(8,128)(2,1)} %constant.37.clone.table_ref, s32[1,512]{1,0:T(1,128)} %bitcast.21, f32[512,1024]{1,0:T(8,128)} %x_ref.1), custom_call_target="tpu_custom_call" | custom-call | tf_op jit(solution)/shard_map/pallas_call | solution.py:74
  5.6 6.0 %all-to-all-start = ((f32[4,128,1024]{2,1,0:T(8,128)}), f32[4,128,1024]{2,1,0:T(8,128)S(1)}, u32[]{:S(2)}, u32[]{:S(2)}) async-start(f32[4,128,1024]{2,1,0:T(8,128)} %bitcast.18), calls=%async_computation | async-start | bytes 4194304 | tf_op jit(solution)/shard_map/all_to_all | solution.py:351
  11.6 0.1 reshape.30
  11.7 0.1 copy.10
  11.8 25.2 %all-to-all-done.y_ref = f32[4,128,1024]{2,1,0:T(8,128)S(1)} async-done(((f32[4,128,1024]{2,1,0:T(8,128)}), f32[4,128,1024]{2,1,0:T(8,128)S(1)}, u32[]{:S(2)}, u32[]{:S(2)}) %all-to-all-start) | async-done | bytes 2097184 | tf_op jit(solution)/shard_map/all_to_all | solution.py:351
  37.1 0.9 shard_map.78
  38.0 1.9 %collective-permute-start = (f32[256,1024]{1,0:T(8,128)S(1)}, f32[256,1024]{1,0:T(8,128)S(1)}, u32[]{:S(2)}, u32[]{:S(2)}) collective-permute-start(f32[256,1024]{1,0:T(8,128)S(1)} %bitcast.12), channel_id=1, source_target_pairs={{0,64},{64,0},{1,65},{65,1},{2,66},{66,2},{3,67},{67,3},{4,68},{68... | collective-permute-start | bytes 3145736 | tf_op jit(solution)/shard_map/ppermute | solution.py:334
  40.0 0.1 pad_add_fusion.ids_ref
  40.0 2.2 %collective-permute-done.w_ref = f32[256,1024]{1,0:T(8,128)S(1)} collective-permute-done((f32[256,1024]{1,0:T(8,128)S(1)}, f32[256,1024]{1,0:T(8,128)S(1)}, u32[]{:S(2)}, u32[]{:S(2)}) %collective-permute-start) | collective-permute-done | bytes 1048608 | tf_op jit(solution)/shard_map/ppermute | solution.py:334
  42.2 2.2 %shard_map.79 = f32[16,272,128]{2,1,0:T(8,128)S(1)} custom-call(s32[2]{0:T(128)S(1)} %pad_add_fusion.ids_ref, f32[256,1024]{1,0:T(8,128)S(1)} %bitcast.13, f32[256,1024]{1,0:T(8,128)S(1)} %collective-permute-done.w_ref), custom_call_target="tpu_custom_call" | custom-call | tf_op jit(solution)/shard_map/pallas_call | solution.py:155
  44.5 35.9 %all_to_all.15.r_ref = f32[16,272,128]{2,1,0:T(8,128)S(1)} all-to-all(f32[16,272,128]{2,1,0:T(8,128)S(1)} %shard_map.79), channel_id=1, replica_groups={{0,1,2,3,4,5,6,7,8,9,10,11,12,13,14,15},{16,17,18,19,20,21,22,23,24,25,..., dimensions={0} | all-to-all | bytes 4456448 | tf_op jit(solution)/shard_map/all_to_all | solution.py:342
  80.3 0.1 slice_reduce_fusion
  80.4 1.0 collective-permute-start.3
  81.4 0.6 collective-permute-start.2
  81.9 0.7 collective-permute-start.1
  82.6 1.1 collective-permute-done.3
  83.7 2.1 %collective-permute-done.2 = f32[144,128]{1,0:T(8,128)S(1)} collective-permute-done((f32[144,128]{1,0:T(8,128)S(1)}, f32[144,128]{1,0:T(8,128)S(1)}, u32[]{:S(2)}, u32[]{:S(2)}) %collective-permute-start.2) | collective-permute-done | bytes 73760 | tf_op jit(solution)/shard_map/ppermute | solution.py:338
  85.8 1.3 collective-permute-done.1
  87.1 0.1 broadcast_in_dim.10
  87.2 18.5 %all_to_all.16 = f32[16,144,128]{2,1,0:T(8,128)S(1)} all-to-all(f32[16,144,128]{2,1,0:T(8,128)S(1)} %broadcast_in_dim.10), channel_id=1, replica_groups={{0,1,2,3,4,5,6,7,8,9,10,11,12,13,14,15},{16,17,18,19,20,21,22,23,24,25,..., dimensions={0} | all-to-all | bytes 2359296 | tf_op jit(solution)/shard_map/all_to_all | solution.py:342
  105.6 3.9 %collective-permute-start.4 = (f32[2304,128]{1,0:T(8,128)S(1)}, f32[2304,128]{1,0:T(8,128)S(1)}, u32[]{:S(2)}, u32[]{:S(2)}) collective-permute-start(f32[2304,128]{1,0:T(8,128)S(1)} %bitcast.14), channel_id=1, source_target_pairs={{0,64},{64,0},{1,65},{65,1},{2,66},{66,2},{3,67},{67,3},{4,68},{68... | collective-permute-start | bytes 3538952 | tf_op jit(solution)/shard_map/ppermute | solution.py:334
  109.6 2.1 %shard_map.80 = f32[256,1024]{1,0:T(8,128)} custom-call(s32[2]{0:T(128)S(1)} %pad_add_fusion.ids_ref, bf16[256,256]{1,0:T(8,128)(2,1)S(1)} %copy-done.1, f32[16,272,128]{2,1,0:T(8,128)S(1)} %all_to_all.15.r_ref), custom_call_target="tpu_custom_call" | custom-call | flops 2000000000 | bytes 4194304 | tf_op jit(solution)/shard_map/pallas_call | solution.py:180
  111.7 0.4 collective-permute-done.4.other_ref
  112.0 38.0 %shard_map.81 = f32[8,1024]{1,0:T(8,128)} custom-call(s32[2]{0:T(128)S(1)} %pad_add_fusion.ids_ref, f32[1,1024]{1,0:T(1,128)S(1)} %bitcast.17, f32[2304,128]{1,0:T(8,128)S(1)} %bitcast.15, f32[2304,128]{1,0:T(8,128)S(1)} %collective-permute-done.4.other_ref), custom_call_target="tpu_custom_call" | custom-call | flops 40000000000 | bytes 2097152 | tf_op jit(solution)/shard_map/pallas_call | solution.py:321
  (9 shorter events, 0.1 us)
Async XLA Ops:
  5.6 6.0 %copy-start.2 = (s32[128,2]{0,1:T(2,128)S(1)}, s32[128,2]{0,1:T(2,128)}, u32[]{:S(2)}) copy-start(s32[128,2]{0,1:T(2,128)} %param.8) | copy-start | bytes 3076
  5.6 31.4 %all-to-all-start = ((f32[4,128,1024]{2,1,0:T(8,128)}), f32[4,128,1024]{2,1,0:T(8,128)S(1)}, u32[]{:S(2)}, u32[]{:S(2)}) async-start(f32[4,128,1024]{2,1,0:T(8,128)} %bitcast.18), calls=%async_computation | async-start | bytes 4194304 | tf_op jit(solution)/shard_map/all_to_all | solution.py:351
  38.0 4.2 %collective-permute-start = (f32[256,1024]{1,0:T(8,128)S(1)}, f32[256,1024]{1,0:T(8,128)S(1)}, u32[]{:S(2)}, u32[]{:S(2)}) collective-permute-start(f32[256,1024]{1,0:T(8,128)S(1)} %bitcast.12), channel_id=1, source_target_pairs={{0,64},{64,0},{1,65},{65,1},{2,66},{66,2},{3,67},{67,3},{4,68},{68... | collective-permute-start | bytes 3145736 | tf_op jit(solution)/shard_map/ppermute | solution.py:334
  80.4 29.2 %copy-start.1 = (bf16[256,256]{1,0:T(8,128)(2,1)S(1)}, bf16[256,256]{1,0:T(8,128)(2,1)}, u32[]{:S(2)}) copy-start(bf16[256,256]{1,0:T(8,128)(2,1)} %constant.38.clone.table_ref) | copy-start | bytes 393220
  80.4 3.3 %collective-permute-start.3 = (f32[144,128]{1,0:T(8,128)S(1)}, f32[144,128]{1,0:T(8,128)S(1)}, u32[]{:S(2)}, u32[]{:S(2)}) collective-permute-start(f32[144,128]{1,0:T(8,128)S(1)} %slice_reduce_fusion), channel_id=1, source_target_pairs={{0,48},{1,49},{2,50},{3,51},{4,52},{5,53},{6,54},{7,55},{8,56},{9,... | collective-permute-start | bytes 221192 | tf_op jit(solution)/shard_map/ppermute | solution.py:338
  81.4 4.4 %collective-permute-start.2 = (f32[144,128]{1,0:T(8,128)S(1)}, f32[144,128]{1,0:T(8,128)S(1)}, u32[]{:S(2)}, u32[]{:S(2)}) collective-permute-start(f32[144,128]{1,0:T(8,128)S(1)} %slice_reduce_fusion), channel_id=1, source_target_pairs={{0,16},{1,17},{2,18},{3,19},{4,20},{5,21},{6,22},{7,23},{8,24},{9,... | collective-permute-start | bytes 221192 | tf_op jit(solution)/shard_map/ppermute | solution.py:338
  81.9 5.1 %collective-permute-start.1 = (f32[144,128]{1,0:T(8,128)S(1)}, f32[144,128]{1,0:T(8,128)S(1)}, u32[]{:S(2)}, u32[]{:S(2)}) collective-permute-start(f32[144,128]{1,0:T(8,128)S(1)} %slice_reduce_fusion), channel_id=1, source_target_pairs={{0,32},{1,33},{2,34},{3,35},{4,36},{5,37},{6,38},{7,39},{8,40},{9,... | collective-permute-start | bytes 221192 | tf_op jit(solution)/shard_map/ppermute | solution.py:338
  105.6 6.4 %copy-start = (f32[1024]{0:T(1024)S(1)}, f32[1024]{0:T(1024)}, u32[]{:S(2)}) copy-start(f32[1024]{0:T(1024)} %param.9) | copy-start | bytes 12292
  105.6 6.4 %collective-permute-start.4 = (f32[2304,128]{1,0:T(8,128)S(1)}, f32[2304,128]{1,0:T(8,128)S(1)}, u32[]{:S(2)}, u32[]{:S(2)}) collective-permute-start(f32[2304,128]{1,0:T(8,128)S(1)} %bitcast.14), channel_id=1, source_target_pairs={{0,64},{64,0},{1,65},{65,1},{2,66},{66,2},{3,67},{67,3},{4,68},{68... | collective-permute-start | bytes 3538952 | tf_op jit(solution)/shard_map/ppermute | solution.py:334

commit v5 on v4

--- a/solution.py
+++ b/solution.py
@@ -41,7 +41,7 @@
 
 def final_table():
     j, i, o, e = (v.reshape(-1, 1) for v in np.meshgrid(range(2), range(16), range(2), range(4), indexing="ij"))
-    op, ip, jp, ep = (v.reshape(1, -1) for v in np.meshgrid(range(2), range(16), range(2), range(4), indexing="ij"))
+    ip, op, jp, ep = (v.reshape(1, -1) for v in np.meshgrid(range(16), range(2), range(2), range(4), indexing="ij"))
     table = parity_sign(i, ip) * parity_sign(o, op) * (j == jp) * (e == ep)
     return table.astype(np.float32).astype(bf16)
 
@@ -122,17 +122,14 @@
     )(keep_rows, y)
 
 
-def gram_kernel(ids_ref, v_ref, w_ref, g_ref, high, low, flat):
+def gram_kernel(ids_ref, v_ref, w_ref, g_ref, s_ref, high, low, flat):
     core = ids_ref[0]
     own = pl.ds(pl.multiple_of(core * 128, 128), 128)
     for part, ref in enumerate((v_ref, w_ref)):
         h, l = halves(ref[...])
         high[256 * part : 256 * part + 256, :] = h
         low[256 * part : 256 * part + 256, :] = l
-        rows = ref[own, :].reshape(16, 8, FEAT)
-        for block in range(PANELS):
-            at = GRAM_ROWS + 8 * (PANELS * part + block)
-            g_ref[:, at : at + 8] = rows[:, :, NB * block : NB * block + NB]
+        s_ref[:, part] = ref[own, :].reshape(16, 8, FEAT)
     for which, strips in enumerate(STRIPS):
 
         @pl.when(core == which)
@@ -147,44 +144,39 @@
                     row += NB
 
     for piece in range(16):
-        g_ref[piece, :GRAM_ROWS] = flat[GRAM_ROWS * piece : GRAM_ROWS * (piece + 1), :]
+        g_ref[piece] = flat[GRAM_ROWS * piece : GRAM_ROWS * (piece + 1), :]
 
 
 def gram_half(ids, mine, theirs):
     rows = mine.shape[0]
     return pl.pallas_call(
         gram_kernel,
-        out_shape=jax.ShapeDtypeStruct((16, GRAM_ROWS + 128, NB), f32),
+        out_shape=(
+            jax.ShapeDtypeStruct((16, GRAM_ROWS, NB), f32),
+            jax.ShapeDtypeStruct((16, 2, 8, FEAT), f32),
+        ),
         in_specs=[SMEM, VMEM, VMEM],
-        out_specs=VMEM,
+        out_specs=(VMEM, VMEM),
         scratch_shapes=[pltpu.VMEM((2 * rows, FEAT), bf16)] * 2 + [pltpu.VMEM((16 * GRAM_ROWS, NB), f32)],
         compiler_params=params(),
     )(ids, mine, theirs)
 
 
-def final_kernel(ids_ref, table_ref, r_ref, o_ref, high, low):
-    for part in range(2):
-        for block in range(PANELS):
-            at = GRAM_ROWS + 8 * (PANELS * part + block)
-            h, l = halves(r_ref[:, at : at + 8].reshape(128, NB))
-            high[128 * part : 128 * part + 128, NB * block : NB * block + NB] = h
-            low[128 * part : 128 * part + 128, NB * block : NB * block + NB] = l
-    total = mm(table_ref[...], high[...]) + mm(table_ref[...], low[...])
+def final_kernel(ids_ref, table_ref, r_ref, o_ref):
+    high, low = halves(r_ref[...])
+    total = mm(table_ref[...], high) + mm(table_ref[...], low)
     odd = (lax.broadcasted_iota(jnp.int32, total.shape, 0) >> 2) & 1
     flip = (odd * ids_ref[0]) == 1
     o_ref[...] = total * jnp.where(flip, -32.0, 32.0)
 
 
 def final_mix(ids, received):
-    rows = 256
     return pl.pallas_call(
         final_kernel,
-        out_shape=jax.ShapeDtypeStruct((rows, FEAT), f32),
+        out_shape=jax.ShapeDtypeStruct(received.shape, f32),
         in_specs=[SMEM, VMEM, VMEM],
         out_specs=VMEM,
-        scratch_shapes=[pltpu.VMEM((rows, FEAT), bf16)] * 2,
         compiler_params=params(),
-        cost_estimate=pl.CostEstimate(flops=2_000_000_000, bytes_accessed=4 << 20, transcendentals=0),
     )(ids, jnp.asarray(final_table()), received)
 
 
@@ -217,46 +209,53 @@
     return terms[0]
 
 
+def row_splat(x, row):
+    return jnp.broadcast_to(x[row : row + 1, :], (8, NB))
+
+
+def by_row(sub, values):
+    a = [jnp.where((sub & 1) == 0, values[k], values[k + 1]) for k in (0, 2, 4, 6)]
+    b = [jnp.where((sub & 2) == 0, a[k], a[k + 1]) for k in (0, 2)]
+    return jnp.where(sub < 4, b[0], b[1])
+
+
 def factor_block(w, upper, inverse):
     lane = lax.broadcasted_iota(jnp.int32, (8, NB), 1)
     sub = lax.broadcasted_iota(jnp.int32, (8, NB), 0)
-    pairs = [(a, b) for a in range(8) for b in range(a, 8)]
-
-    def row_splat(row):
-        return jnp.broadcast_to(w[row : row + 1, :], (8, NB))
-
-    rho = [row_splat(b) for b in range(8)]
-    e = {(a, b): lane_splat(rho[a], b) for a, b in pairs}
+    rows = w[0:8, :]
+    e = [lane_splat(rows, a) for a in range(8)]
     for step in range(16):
         base = 8 * step
         inside = (lane >= base) & (lane < base + 8)
-        aug = [jnp.where(inside, jnp.where(lane == base + b, 1.0, 0.0), rho[b]) for b in range(8)]
-        u, t = [None] * 8, [None] * 8
+        aug = jnp.where(inside, jnp.where(lane == base + sub, 1.0, 0.0), rows)
+        scales, finished = [], []
         for b in range(8):
-            r = lax.rsqrt(e[b, b])
-            u[b], t[b] = rho[b] * r, aug[b] * r
-            c = {a: e[b, a] * r for a in range(b + 1, 8)}
-            for a in range(b + 1, 8):
-                for a2 in range(a, 8):
-                    e[a, a2] = e[a, a2] - c[a] * c[a2]
-            for a in range(b + 1, 8):
-                rho[a] = rho[a] - c[a] * u[b]
-                aug[a] = aug[a] - c[a] * t[b]
-        left, right = u[0], t[0]
-        for b in range(1, 8):
-            left = jnp.where(sub == b, u[b], left)
-            right = jnp.where(sub == b, t[b], right)
+            r = lax.rsqrt(row_splat(e[b], b))
+            scales.append(r)
+            multiplier = jnp.where(sub > b, e[b] * r, 0.0)
+            scaled = row_splat(aug, b) * r
+            finished.append(scaled)
+            if b < 7:
+                for a in range(b + 1, 8):
+                    e[a] = e[a] - multiplier * (row_splat(e[a], b) * r)
+                rows = rows - multiplier * (row_splat(rows, b) * r)
+                aug = aug - multiplier * scaled
+        scale = by_row(sub, scales)
+        if step < 15:
+            columns = [lane_splat(rows, base + 8 + a) * scale for a in range(8)]
+        left, right = rows * scale, aug * scale
         upper[base : base + 8, :] = jnp.where(lane >= base + sub, left, 0.0)
         inverse[base : base + 8, :] = jnp.where(lane <= base + sub, right, 0.0)
         if step == 15:
             break
         if step < 14:
             update = outer_sum(left, right)
-        coming = [jnp.where(inside, 0.0, row_splat(base + 8 + a)) for a in range(8)]
-        c = {(b, a): lane_splat(u[b], base + 8 + a) for b in range(8) for a in range(8)}
-        e = {(a, a2): lane_splat(coming[a], base + 8 + a2) for a, a2 in pairs}
-        e = {(a, a2): e[a, a2] - tree_sum([c[b, a] * c[b, a2] for b in range(8)]) for a, a2 in pairs}
-        rho = [coming[a] - tree_sum([c[b, a] * t[b] for b in range(8)]) for a in range(8)]
+        coming = jnp.where(inside, 0.0, w[base + 8 : base + 16, :])
+        start = [lane_splat(coming, base + 8 + a) for a in range(8)]
+        c = {(b, a): row_splat(columns[a], b) for b in range(8) for a in range(8)}
+        turned = [by_row(sub, [c[b, a] for a in range(8)]) for b in range(8)]
+        e = [start[a] - tree_sum([turned[b] * c[b, a] for b in range(8)]) for a in range(8)]
+        rows = coming - tree_sum([turned[b] * finished[b] for b in range(8)])
         if step < 14:
             after = base + 16
             rest = lax.broadcasted_iota(jnp.int32, (NB - after, NB), 1)
@@ -353,13 +352,15 @@
     )
     mine = select_rows(keep_rows, along).reshape(256, FEAT)
     theirs = swap_cores(mine)
-    received = plane_exchange(gram_half(ids, mine, theirs))
-    piece = jnp.sum(received[:, :GRAM_ROWS], axis=0)
+    gram, to_send = gram_half(ids, mine, theirs)
+    piece = jnp.sum(plane_exchange(gram), axis=0)
     piece = (piece + along_z(piece, 2)) + (along_z(piece, 1) + along_z(piece, 3))
     own = plane_exchange(jnp.broadcast_to(piece[None], (16, GRAM_ROWS, NB))).reshape(16 * GRAM_ROWS, NB)
-    sketch = final_mix(ids, received)
+    to_send, own = lax.optimization_barrier((to_send, own))
+    received = plane_exchange(to_send)
     other = swap_cores(own)
     factor = factor_rows(ids, ridge_weights.reshape(1, FEAT), own, other)
+    sketch = final_mix(ids, received.reshape(256, FEAT))
     return sketch, factor
 
 

time: 150 us -> 155 us (1.033)
  blocking collectives: 54.3 us -> 62.6 us
  Pallas kernels: 48.3 us -> 43.2 us
    all_to_all x2 -> x3, blocking collectives: 54.3 us -> 62.6 us  [plane_exchange(): lax.all_to_all(x, 'inner', 0, 0, axis_index_groups=PLANES, tiled=True)]
    pallas_call x1, Pallas kernels: 38 us -> 33.1 us  [factor_rows(): pl.pallas_call(factor_kernel, out_shape=jax.ShapeDtypeStruct((8, FEAT), f...]
  transfers between devices with their start and end apart: 6 -> 6, of which waited for: 6 -> 5; matrix products, arithmetic and copies ran while one was open for 0% -> 0% of each run, Pallas kernels for 1% -> 1%
where the time goes in v5:
time: 155 us; the launch traced here: 154 us
  blocking collectives  62.6 us (40%)
  Pallas kernels  43.2 us (28%)
  waiting for transfers between devices  31.9 us (21%)
  starting transfers between devices  14.1 us (9%)
    all_to_all x3, blocking collectives, plane_exchange(): lax.all_to_all(x, 'inner', 0, 0, axis_index_groups=PLANES, tiled=True)  62.6 us
    pallas_call x1, Pallas kernels, factor_rows(): pl.pallas_call(factor_kernel, out_shape=jax.ShapeDtypeStruct((8, FEAT), f...  33.1 us
    all_to_all x1, waiting for transfers between devices, local(): lax.all_to_all(mixed.reshape(4, 128, FEAT), 'inner', 0, 0, axis_index_gro...  25.2 us
    all_to_all x1, starting transfers between devices, local(): lax.all_to_all(mixed.reshape(4, 128, FEAT), 'inner', 0, 0, axis_index_gro...  5.99 us
    ppermute x2, starting transfers between devices, swap_cores(): return lax.ppermute(x, 'outer', [(0, 1), (1, 0)])  5.86 us
    pallas_call x1, Pallas kernels, local_mix(): pl.pallas_call(local_mix_kernel, grid=(features // cols,), out_shape=jax....  4.94 us
    ppermute x3, waiting for transfers between devices, along_z(): lax.ppermute(x, 'inner', [(i, (i + 16 * distance) % 64) for i in range(64)])  4.43 us
  transfers between devices with their start and end apart: 6, of which 5 were waited for; matrix products, arithmetic and copies ran while one was open for 0% of the time, Pallas kernels for 1%

profile of v5, /device:TPU:1, one launch (start us, length us, event | category | flops | bytes accessed | tf_op | source)
XLA Modules:
  0.0 154.1 jit_solution(2345811599237782733)
XLA Ops:
  0.6 4.9 %shard_map.77 = f32[512,1024]{1,0:T(8,128)} custom-call(bf16[512,512]{1,0:T(8,128)(2,1)} %constant.37.clone.table_ref, s32[1,512]{1,0:T(1,128)} %bitcast.23, f32[512,1024]{1,0:T(8,128)} %x_ref.1), custom_call_target="tpu_custom_call" | custom-call | tf_op jit(solution)/shard_map/pallas_call | solution.py:74
  5.6 6.0 %all-to-all-start = ((f32[4,128,1024]{2,1,0:T(8,128)}), f32[4,128,1024]{2,1,0:T(8,128)S(1)}, u32[]{:S(2)}, u32[]{:S(2)}) async-start(f32[4,128,1024]{2,1,0:T(8,128)} %bitcast.20), calls=%async_computation | async-start | bytes 4194304 | tf_op jit(solution)/shard_map/all_to_all | solution.py:350
  11.6 0.1 reshape.33
  11.7 0.1 copy.10
  11.8 25.2 %all-to-all-done.y_ref = f32[4,128,1024]{2,1,0:T(8,128)S(1)} async-done(((f32[4,128,1024]{2,1,0:T(8,128)}), f32[4,128,1024]{2,1,0:T(8,128)S(1)}, u32[]{:S(2)}, u32[]{:S(2)}) %all-to-all-start) | async-done | bytes 2097184 | tf_op jit(solution)/shard_map/all_to_all | solution.py:350
  37.0 0.9 shard_map.78
  37.9 1.9 %collective-permute-start = (f32[256,1024]{1,0:T(8,128)S(1)}, f32[256,1024]{1,0:T(8,128)S(1)}, u32[]{:S(2)}, u32[]{:S(2)}) collective-permute-start(f32[256,1024]{1,0:T(8,128)S(1)} %bitcast.13), channel_id=1, source_target_pairs={{0,64},{64,0},{1,65},{65,1},{2,66},{66,2},{3,67},{67,3},{4,68},{68... | collective-permute-start | bytes 3145736 | tf_op jit(solution)/shard_map/ppermute | solution.py:333
  39.9 0.1 pad_add_fusion.ids_ref
  40.0 2.2 %collective-permute-done.w_ref = f32[256,1024]{1,0:T(8,128)S(1)} collective-permute-done((f32[256,1024]{1,0:T(8,128)S(1)}, f32[256,1024]{1,0:T(8,128)S(1)}, u32[]{:S(2)}, u32[]{:S(2)}) %collective-permute-start) | collective-permute-done | bytes 1048608 | tf_op jit(solution)/shard_map/ppermute | solution.py:333
  42.2 2.2 %shard_map.79 = (f32[16,144,128]{2,1,0:T(8,128)S(1)}, f32[16,2,8,1024]{3,2,1,0:T(8,128)S(1)}) custom-call(s32[2]{0:T(128)S(1)} %pad_add_fusion.ids_ref, f32[256,1024]{1,0:T(8,128)S(1)} %bitcast.14, f32[256,1024]{1,0:T(8,128)S(1)} %collective-permute-done.w_ref), custom_call_target="tpu_custom_call" | custom-call | tf_op jit(solution)/shard_map/pallas_call | solution.py:152
  44.4 24.7 %all_to_all.20 = f32[16,144,128]{2,1,0:T(8,128)} all-to-all(f32[16,144,128]{2,1,0:T(8,128)S(1)} %get-tuple-element.7), channel_id=1, replica_groups={{0,1,2,3,4,5,6,7,8,9,10,11,12,13,14,15},{16,17,18,19,20,21,22,23,24,25,..., dimensions={0} | all-to-all | bytes 2359296 | tf_op jit(solution)/shard_map/all_to_all | solution.py:341
  69.1 1.3 reduce_sum.9
  70.5 1.0 collective-permute-start.3
  71.4 0.6 collective-permute-start.2
  72.0 0.7 collective-permute-start.1
  72.7 1.0 collective-permute-done.3
  73.7 2.1 %collective-permute-done.2 = f32[144,128]{1,0:T(8,128)S(1)} collective-permute-done((f32[144,128]{1,0:T(8,128)S(1)}, f32[144,128]{1,0:T(8,128)S(1)}, u32[]{:S(2)}, u32[]{:S(2)}) %collective-permute-start.2) | collective-permute-done | bytes 73760 | tf_op jit(solution)/shard_map/ppermute | solution.py:337
  75.8 1.3 collective-permute-done.1
  77.1 0.1 broadcast_in_dim.10
  77.2 18.5 %all_to_all.21 = f32[16,144,128]{2,1,0:T(8,128)S(1)} all-to-all(f32[16,144,128]{2,1,0:T(8,128)S(1)} %broadcast_in_dim.10), channel_id=1, replica_groups={{0,1,2,3,4,5,6,7,8,9,10,11,12,13,14,15},{16,17,18,19,20,21,22,23,24,25,..., dimensions={0} | all-to-all | bytes 2359296 | tf_op jit(solution)/shard_map/all_to_all | solution.py:341
  95.7 3.9 %collective-permute-start.4 = (f32[2304,128]{1,0:T(8,128)S(1)}, f32[2304,128]{1,0:T(8,128)S(1)}, u32[]{:S(2)}, u32[]{:S(2)}) collective-permute-start(f32[2304,128]{1,0:T(8,128)S(1)} %bitcast.16), channel_id=1, source_target_pairs={{0,64},{64,0},{1,65},{65,1},{2,66},{66,2},{3,67},{67,3},{4,68},{68... | collective-permute-start | bytes 3538952 | tf_op jit(solution)/shard_map/ppermute | solution.py:333
  99.6 19.4 %all_to_all.22 = f32[16,2,8,1024]{3,2,1,0:T(8,128)S(1)} all-to-all(f32[16,2,8,1024]{3,2,1,0:T(8,128)S(1)} %get-tuple-element.8), channel_id=1, replica_groups={{0,1,2,3,4,5,6,7,8,9,10,11,12,13,14,15},{16,17,18,19,20,21,22,23,24,25,..., dimensions={0} | all-to-all | bytes 2097152 | tf_op jit(solution)/shard_map/all_to_all | solution.py:341
  119.0 2.0 %shard_map.80 = f32[256,1024]{1,0:T(8,128)} custom-call(s32[2]{0:T(128)S(1)} %pad_add_fusion.ids_ref, bf16[256,256]{1,0:T(8,128)(2,1)S(1)} %copy-done, f32[256,1024]{1,0:T(8,128)S(1)} %bitcast.15), custom_call_target="tpu_custom_call" | custom-call | tf_op jit(solution)/shard_map/pallas_call | solution.py:174
  121.0 33.1 %shard_map.81 = f32[8,1024]{1,0:T(8,128)} custom-call(s32[2]{0:T(128)S(1)} %pad_add_fusion.ids_ref, f32[1,1024]{1,0:T(1,128)S(1)} %bitcast.19, f32[2304,128]{1,0:T(8,128)S(1)} %bitcast.17, f32[2304,128]{1,0:T(8,128)S(1)} %collective-permute-done.4.other_ref), custom_call_target="tpu_custom_call" | custom-call | flops 40000000000 | bytes 2097152 | tf_op jit(solution)/shard_map/pallas_call | solution.py:320
  (10 shorter events, 0.1 us)
Async XLA Ops:
  5.6 6.0 %copy-start.2 = (s32[128,2]{0,1:T(2,128)S(1)}, s32[128,2]{0,1:T(2,128)}, u32[]{:S(2)}) copy-start(s32[128,2]{0,1:T(2,128)} %param.8) | copy-start | bytes 3076
  5.6 31.4 %all-to-all-start = ((f32[4,128,1024]{2,1,0:T(8,128)}), f32[4,128,1024]{2,1,0:T(8,128)S(1)}, u32[]{:S(2)}, u32[]{:S(2)}) async-start(f32[4,128,1024]{2,1,0:T(8,128)} %bitcast.20), calls=%async_computation | async-start | bytes 4194304 | tf_op jit(solution)/shard_map/all_to_all | solution.py:350
  37.9 4.2 %collective-permute-start = (f32[256,1024]{1,0:T(8,128)S(1)}, f32[256,1024]{1,0:T(8,128)S(1)}, u32[]{:S(2)}, u32[]{:S(2)}) collective-permute-start(f32[256,1024]{1,0:T(8,128)S(1)} %bitcast.13), channel_id=1, source_target_pairs={{0,64},{64,0},{1,65},{65,1},{2,66},{66,2},{3,67},{67,3},{4,68},{68... | collective-permute-start | bytes 3145736 | tf_op jit(solution)/shard_map/ppermute | solution.py:333
  70.5 3.3 %collective-permute-start.3 = (f32[144,128]{1,0:T(8,128)S(1)}, f32[144,128]{1,0:T(8,128)S(1)}, u32[]{:S(2)}, u32[]{:S(2)}) collective-permute-start(f32[144,128]{1,0:T(8,128)S(1)} %reduce_sum.9), channel_id=1, source_target_pairs={{0,48},{1,49},{2,50},{3,51},{4,52},{5,53},{6,54},{7,55},{8,56},{9,... | collective-permute-start | bytes 221192 | tf_op jit(solution)/shard_map/ppermute | solution.py:337
  71.4 4.4 %collective-permute-start.2 = (f32[144,128]{1,0:T(8,128)S(1)}, f32[144,128]{1,0:T(8,128)S(1)}, u32[]{:S(2)}, u32[]{:S(2)}) collective-permute-start(f32[144,128]{1,0:T(8,128)S(1)} %reduce_sum.9), channel_id=1, source_target_pairs={{0,16},{1,17},{2,18},{3,19},{4,20},{5,21},{6,22},{7,23},{8,24},{9,... | collective-permute-start | bytes 221192 | tf_op jit(solution)/shard_map/ppermute | solution.py:337
  72.0 5.1 %collective-permute-start.1 = (f32[144,128]{1,0:T(8,128)S(1)}, f32[144,128]{1,0:T(8,128)S(1)}, u32[]{:S(2)}, u32[]{:S(2)}) collective-permute-start(f32[144,128]{1,0:T(8,128)S(1)} %reduce_sum.9), channel_id=1, source_target_pairs={{0,32},{1,33},{2,34},{3,35},{4,36},{5,37},{6,38},{7,39},{8,40},{9,... | collective-permute-start | bytes 221192 | tf_op jit(solution)/shard_map/ppermute | solution.py:337
  95.7 23.3 %copy-start = (bf16[256,256]{1,0:T(8,128)(2,1)S(1)}, bf16[256,256]{1,0:T(8,128)(2,1)}, u32[]{:S(2)}) copy-start(bf16[256,256]{1,0:T(8,128)(2,1)} %constant.38.clone.table_ref) | copy-start | bytes 393220
  95.7 25.3 %collective-permute-start.4 = (f32[2304,128]{1,0:T(8,128)S(1)}, f32[2304,128]{1,0:T(8,128)S(1)}, u32[]{:S(2)}, u32[]{:S(2)}) collective-permute-start(f32[2304,128]{1,0:T(8,128)S(1)} %bitcast.16), channel_id=1, source_target_pairs={{0,64},{64,0},{1,65},{65,1},{2,66},{66,2},{3,67},{67,3},{4,68},{68... | collective-permute-start | bytes 3538952 | tf_op jit(solution)/shard_map/ppermute | solution.py:333
  119.0 2.0 %copy-start.1 = (f32[1024]{0:T(1024)S(1)}, f32[1024]{0:T(1024)}, u32[]{:S(2)}) copy-start(f32[1024]{0:T(1024)} %param.9) | copy-start | bytes 12292

commit v6 on v5

--- a/solution.py
+++ b/solution.py
@@ -356,9 +356,9 @@
     piece = jnp.sum(plane_exchange(gram), axis=0)
     piece = (piece + along_z(piece, 2)) + (along_z(piece, 1) + along_z(piece, 3))
     own = plane_exchange(jnp.broadcast_to(piece[None], (16, GRAM_ROWS, NB))).reshape(16 * GRAM_ROWS, NB)
-    to_send, own = lax.optimization_barrier((to_send, own))
+    other = swap_cores(own)
+    to_send, own, other = lax.optimization_barrier((to_send, own, other))
     received = plane_exchange(to_send)
-    other = swap_cores(own)
     factor = factor_rows(ids, ridge_weights.reshape(1, FEAT), own, other)
     sketch = final_mix(ids, received.reshape(256, FEAT))
     return sketch, factor

time: 155 us -> 143 us (0.923)
  blocking collectives: 62.6 us -> 45 us
  starting transfers between devices: 14.1 us -> 17.7 us
  local copies, waits for them, and re-layouts: 0.29 us -> 2.58 us
    all_to_all x3 -> x2, blocking collectives: 62.6 us -> 45 us  [plane_exchange(): lax.all_to_all(x, 'inner', 0, 0, axis_index_groups=PLANES, tiled=True)]
    all_to_all x0 -> x1, starting transfers between devices: none -> 3.66 us  [plane_exchange(): lax.all_to_all(x, 'inner', 0, 0, axis_index_groups=PLANES, tiled=True)]
    ppermute x2, waiting for transfers between devices: 2.21 us -> 4.69 us  [swap_cores(): return lax.ppermute(x, 'outer', [(0, 1), (1, 0)])]
    unnamed x6 -> x10, local copies, waits for them, and re-layouts: 0.01 us -> 2.3 us
    ppermute x3, waiting for transfers between devices: 4.43 us -> 2.53 us  [along_z(): lax.ppermute(x, 'inner', [(i, (i + 16 * distance) % 64) for i in range(64)])]
  transfers between devices with their start and end apart: 6 -> 7, of which waited for: 5 -> 5; matrix products, arithmetic and copies ran while one was open for 0% -> 0% of each run, Pallas kernels for 1% -> 23%
where the time goes in v6:
time: 143 us
  blocking collectives  45 us (31%)
  Pallas kernels  44.1 us (31%)
  waiting for transfers between devices  32.4 us (23%)
  starting transfers between devices  17.7 us (12%)
  local copies, waits for them, and re-layouts  2.58 us (2%)
    all_to_all x2, blocking collectives, plane_exchange(): lax.all_to_all(x, 'inner', 0, 0, axis_index_groups=PLANES, tiled=True)  45 us
    pallas_call x1, Pallas kernels, factor_rows(): pl.pallas_call(factor_kernel, out_shape=jax.ShapeDtypeStruct((8, FEAT), f...  33.1 us
    all_to_all x1, waiting for transfers between devices, local(): lax.all_to_all(mixed.reshape(4, 128, FEAT), 'inner', 0, 0, axis_index_gro...  25.2 us
    all_to_all x1, starting transfers between devices, local(): lax.all_to_all(mixed.reshape(4, 128, FEAT), 'inner', 0, 0, axis_index_gro...  5.99 us
    ppermute x2, starting transfers between devices, swap_cores(): return lax.ppermute(x, 'outer', [(0, 1), (1, 0)])  4.99 us
    pallas_call x1, Pallas kernels, local_mix(): pl.pallas_call(local_mix_kernel, grid=(features // cols,), out_shape=jax....  4.95 us
    ppermute x2, waiting for transfers between devices, swap_cores(): return lax.ppermute(x, 'outer', [(0, 1), (1, 0)])  4.69 us
    all_to_all x1, starting transfers between devices, plane_exchange(): lax.all_to_all(x, 'inner', 0, 0, axis_index_groups=PLANES, tiled=True)  3.66 us
  transfers between devices with their start and end apart: 7, of which 5 were waited for; matrix products, arithmetic and copies ran while one was open for 0% of the time, Pallas kernels for 23%

profile of v6, /device:TPU:1, one launch (start us, length us, event | category | flops | bytes accessed | tf_op | source)
XLA Modules:
  0.0 142.7 jit_solution(8024263162514350231)
XLA Ops:
  0.6 4.9 %shard_map.77 = f32[512,1024]{1,0:T(8,128)} custom-call(bf16[512,512]{1,0:T(8,128)(2,1)} %constant.37.clone.table_ref, s32[1,512]{1,0:T(1,128)} %bitcast.23, f32[512,1024]{1,0:T(8,128)} %x_ref.1), custom_call_target="tpu_custom_call" | custom-call | tf_op jit(solution)/shard_map/pallas_call | solution.py:74
  5.6 6.0 %all-to-all-start = ((f32[4,128,1024]{2,1,0:T(8,128)}), f32[4,128,1024]{2,1,0:T(8,128)S(1)}, u32[]{:S(2)}, u32[]{:S(2)}) async-start(f32[4,128,1024]{2,1,0:T(8,128)} %bitcast.20), calls=%async_computation | async-start | bytes 4194304 | tf_op jit(solution)/shard_map/all_to_all | solution.py:350
  11.6 0.1 reshape.33
  11.7 0.1 copy.10
  11.8 25.2 %all-to-all-done.y_ref = f32[4,128,1024]{2,1,0:T(8,128)S(1)} async-done(((f32[4,128,1024]{2,1,0:T(8,128)}), f32[4,128,1024]{2,1,0:T(8,128)S(1)}, u32[]{:S(2)}, u32[]{:S(2)}) %all-to-all-start) | async-done | bytes 2097184 | tf_op jit(solution)/shard_map/all_to_all | solution.py:350
  37.0 0.9 shard_map.78
  37.9 1.9 %collective-permute-start = (f32[256,1024]{1,0:T(8,128)S(1)}, f32[256,1024]{1,0:T(8,128)S(1)}, u32[]{:S(2)}, u32[]{:S(2)}) collective-permute-start(f32[256,1024]{1,0:T(8,128)S(1)} %bitcast.13), channel_id=1, source_target_pairs={{0,64},{64,0},{1,65},{65,1},{2,66},{66,2},{3,67},{67,3},{4,68},{68... | collective-permute-start | bytes 3145736 | tf_op jit(solution)/shard_map/ppermute | solution.py:333
  40.0 2.2 %collective-permute-done.w_ref = f32[256,1024]{1,0:T(8,128)S(1)} collective-permute-done((f32[256,1024]{1,0:T(8,128)S(1)}, f32[256,1024]{1,0:T(8,128)S(1)}, u32[]{:S(2)}, u32[]{:S(2)}) %collective-permute-start) | collective-permute-done | bytes 1048608 | tf_op jit(solution)/shard_map/ppermute | solution.py:333
  42.2 3.1 %shard_map.79 = (f32[16,144,128]{2,1,0:T(8,128)S(1)}, f32[16,2,8,1024]{3,2,1,0:T(8,128)}) custom-call(s32[2]{0:T(128)S(1)} %pad_add_fusion.ids_ref, f32[256,1024]{1,0:T(8,128)S(1)} %bitcast.14, f32[256,1024]{1,0:T(8,128)S(1)} %collective-permute-done.w_ref), custom_call_target="tpu_custom_call" | custom-call | tf_op jit(solution)/shard_map/pallas_call | solution.py:152
  45.3 24.6 %all_to_all.20 = f32[16,144,128]{2,1,0:T(8,128)S(1)} all-to-all(f32[16,144,128]{2,1,0:T(8,128)S(1)} %get-tuple-element.8), channel_id=1, replica_groups={{0,1,2,3,4,5,6,7,8,9,10,11,12,13,14,15},{16,17,18,19,20,21,22,23,24,25,..., dimensions={0} | all-to-all | bytes 2359296 | tf_op jit(solution)/shard_map/all_to_all | solution.py:341
  70.0 0.4 collective-permute-start.1
  70.3 1.2 collective-permute-start.2
  71.5 1.5 %collective-permute-start.3 = (f32[144,128]{1,0:T(8,128)S(1)}, f32[144,128]{1,0:T(8,128)S(1)}, u32[]{:S(2)}, u32[]{:S(2)}) collective-permute-start(f32[144,128]{1,0:T(8,128)S(1)} %reduce_sum.9), channel_id=1, source_target_pairs={{0,48},{1,49},{2,50},{3,51},{4,52},{5,53},{6,54},{7,55},{8,56},{9,... | collective-permute-start | bytes 221192 | tf_op jit(solution)/shard_map/ppermute | solution.py:337
  73.0 1.9 %collective-permute-done.1 = f32[144,128]{1,0:T(8,128)S(1)} collective-permute-done((f32[144,128]{1,0:T(8,128)S(1)}, f32[144,128]{1,0:T(8,128)S(1)}, u32[]{:S(2)}, u32[]{:S(2)}) %collective-permute-start.1) | collective-permute-done | bytes 73760 | tf_op jit(solution)/shard_map/ppermute | solution.py:337
  74.9 0.7 collective-permute-done.2
  75.6 0.1 broadcast_in_dim.10
  75.7 20.4 %all_to_all.21 = f32[16,144,128]{2,1,0:T(8,128)S(1)} all-to-all(f32[16,144,128]{2,1,0:T(8,128)S(1)} %broadcast_in_dim.10), channel_id=1, replica_groups={{0,1,2,3,4,5,6,7,8,9,10,11,12,13,14,15},{16,17,18,19,20,21,22,23,24,25,..., dimensions={0} | all-to-all | bytes 2359296 | tf_op jit(solution)/shard_map/all_to_all | solution.py:341
  96.1 3.0 %collective-permute-start.4 = (f32[2304,128]{1,0:T(8,128)S(1)}, f32[2304,128]{1,0:T(8,128)S(1)}, u32[]{:S(2)}, u32[]{:S(2)}) collective-permute-start(f32[2304,128]{1,0:T(8,128)S(1)} %bitcast.16), channel_id=1, source_target_pairs={{0,64},{64,0},{1,65},{65,1},{2,66},{66,2},{3,67},{67,3},{4,68},{68... | collective-permute-start | bytes 3538952 | tf_op jit(solution)/shard_map/ppermute | solution.py:333
  99.1 2.5 %collective-permute-done.4.other_ref = f32[2304,128]{1,0:T(8,128)S(1)} collective-permute-done((f32[2304,128]{1,0:T(8,128)S(1)}, f32[2304,128]{1,0:T(8,128)S(1)}, u32[]{:S(2)}, u32[]{:S(2)}) %collective-permute-start.4) | collective-permute-done | bytes 1179680 | tf_op jit(solution)/shard_map/ppermute | solution.py:333
  101.6 1.0 copy-done.1
  102.6 3.7 %all-to-all-start.3 = ((f32[16,2,8,1024]{3,2,1,0:T(8,128)}), f32[16,2,8,1024]{3,2,1,0:T(8,128)S(1)}, u32[]{:S(2)}, u32[]{:S(2)}) async-start(f32[16,2,8,1024]{3,2,1,0:T(8,128)} %get-tuple-element.9), calls=%async_computation.3 | async-start | bytes 2097152 | tf_op jit(solution)/shard_map/all_to_all | solution.py:341
  106.3 1.3 copy-done.2
  107.6 33.1 %shard_map.81 = f32[8,1024]{1,0:T(8,128)} custom-call(s32[2]{0:T(128)S(1)} %pad_add_fusion.ids_ref, f32[1,1024]{1,0:T(1,128)S(1)} %bitcast.19, f32[2304,128]{1,0:T(8,128)S(1)} %bitcast.17, f32[2304,128]{1,0:T(8,128)S(1)} %copy-done.2), custom_call_target="tpu_custom_call" | custom-call | flops 40000000000 | bytes 2097152 | tf_op jit(solution)/shard_map/pallas_call | solution.py:320
  140.7 2.0 %shard_map.80 = f32[256,1024]{1,0:T(8,128)} custom-call(s32[2]{0:T(128)S(1)} %pad_add_fusion.ids_ref, bf16[256,256]{1,0:T(8,128)(2,1)S(1)} %copy-done, f32[256,1024]{1,0:T(8,128)S(1)} %bitcast.15), custom_call_target="tpu_custom_call" | custom-call | tf_op jit(solution)/shard_map/pallas_call | solution.py:174
  (15 shorter events, 0.2 us)
Async XLA Ops:
  5.6 6.0 %copy-start.4 = (s32[128,2]{0,1:T(2,128)S(1)}, s32[128,2]{0,1:T(2,128)}, u32[]{:S(2)}) copy-start(s32[128,2]{0,1:T(2,128)} %param.8) | copy-start | bytes 3076
  5.6 31.4 %all-to-all-start = ((f32[4,128,1024]{2,1,0:T(8,128)}), f32[4,128,1024]{2,1,0:T(8,128)S(1)}, u32[]{:S(2)}, u32[]{:S(2)}) async-start(f32[4,128,1024]{2,1,0:T(8,128)} %bitcast.20), calls=%async_computation | async-start | bytes 4194304 | tf_op jit(solution)/shard_map/all_to_all | solution.py:350
  37.9 4.2 %collective-permute-start = (f32[256,1024]{1,0:T(8,128)S(1)}, f32[256,1024]{1,0:T(8,128)S(1)}, u32[]{:S(2)}, u32[]{:S(2)}) collective-permute-start(f32[256,1024]{1,0:T(8,128)S(1)} %bitcast.13), channel_id=1, source_target_pairs={{0,64},{64,0},{1,65},{65,1},{2,66},{66,2},{3,67},{67,3},{4,68},{68... | collective-permute-start | bytes 3145736 | tf_op jit(solution)/shard_map/ppermute | solution.py:333
  70.0 4.9 %collective-permute-start.1 = (f32[144,128]{1,0:T(8,128)S(1)}, f32[144,128]{1,0:T(8,128)S(1)}, u32[]{:S(2)}, u32[]{:S(2)}) collective-permute-start(f32[144,128]{1,0:T(8,128)S(1)} %reduce_sum.9), channel_id=1, source_target_pairs={{0,32},{1,33},{2,34},{3,35},{4,36},{5,37},{6,38},{7,39},{8,40},{9,... | collective-permute-start | bytes 221192 | tf_op jit(solution)/shard_map/ppermute | solution.py:337
  70.3 5.2 %collective-permute-start.2 = (f32[144,128]{1,0:T(8,128)S(1)}, f32[144,128]{1,0:T(8,128)S(1)}, u32[]{:S(2)}, u32[]{:S(2)}) collective-permute-start(f32[144,128]{1,0:T(8,128)S(1)} %reduce_sum.9), channel_id=1, source_target_pairs={{0,16},{1,17},{2,18},{3,19},{4,20},{5,21},{6,22},{7,23},{8,24},{9,... | collective-permute-start | bytes 221192 | tf_op jit(solution)/shard_map/ppermute | solution.py:337
  71.5 4.0 %collective-permute-start.3 = (f32[144,128]{1,0:T(8,128)S(1)}, f32[144,128]{1,0:T(8,128)S(1)}, u32[]{:S(2)}, u32[]{:S(2)}) collective-permute-start(f32[144,128]{1,0:T(8,128)S(1)} %reduce_sum.9), channel_id=1, source_target_pairs={{0,48},{1,49},{2,50},{3,51},{4,52},{5,53},{6,54},{7,55},{8,56},{9,... | collective-permute-start | bytes 221192 | tf_op jit(solution)/shard_map/ppermute | solution.py:337
  96.1 10.2 %copy-start.3 = (f32[1024]{0:T(1024)S(1)}, f32[1024]{0:T(1024)}, u32[]{:S(2)}) copy-start(f32[1024]{0:T(1024)} %param.9) | copy-start | bytes 12292
  96.1 5.5 %collective-permute-start.4 = (f32[2304,128]{1,0:T(8,128)S(1)}, f32[2304,128]{1,0:T(8,128)S(1)}, u32[]{:S(2)}, u32[]{:S(2)}) collective-permute-start(f32[2304,128]{1,0:T(8,128)S(1)} %bitcast.16), channel_id=1, source_target_pairs={{0,64},{64,0},{1,65},{65,1},{2,66},{66,2},{3,67},{67,3},{4,68},{68... | collective-permute-start | bytes 3538952 | tf_op jit(solution)/shard_map/ppermute | solution.py:333
  101.6 1.0 copy-start.1
  102.6 38.1 %all-to-all-start.3 = ((f32[16,2,8,1024]{3,2,1,0:T(8,128)}), f32[16,2,8,1024]{3,2,1,0:T(8,128)S(1)}, u32[]{:S(2)}, u32[]{:S(2)}) async-start(f32[16,2,8,1024]{3,2,1,0:T(8,128)} %get-tuple-element.9), calls=%async_computation.3 | async-start | bytes 2097152 | tf_op jit(solution)/shard_map/all_to_all | solution.py:341
  106.3 1.3 copy-start.2
  107.6 33.1 %copy-start = (bf16[256,256]{1,0:T(8,128)(2,1)S(1)}, bf16[256,256]{1,0:T(8,128)(2,1)}, u32[]{:S(2)}) copy-start(bf16[256,256]{1,0:T(8,128)(2,1)} %constant.38.clone.table_ref) | copy-start | bytes 393220

commit v7 on v5

--- a/solution.py
+++ b/solution.py
@@ -59,29 +59,54 @@
     return lax.dot_general(a, b, (((0,), (0,)), ((), ())), preferred_element_type=f32)
 
 
-def local_mix_kernel(table_ref, sign_ref, x_ref, o_ref, signed):
-    @pl.when(pl.program_id(0) == 0)
-    def _():
-        signed[...] = (table_ref[...].astype(f32) * (sign_ref[...].astype(f32) * 2.0**-13)).astype(bf16)
-
-    high, low = halves(x_ref[...])
-    o_ref[...] = mm(signed[...], high) + mm(signed[...], low)
+def local_mix_kernel(table_hbm, sign_hbm, x_hbm, o_hbm, table, sign, signed, x, out, sems):
+    chunks, _, cols = x.shape
+
+    def columns(ref, chunk):
+        return ref.at[:, cols * chunk : cols * chunk + cols]
+
+    def load(chunk):
+        return pltpu.make_async_copy(columns(x_hbm, chunk), x.at[chunk], sems.at[chunk])
+
+    def store(chunk):
+        return pltpu.make_async_copy(out.at[chunk], columns(o_hbm, chunk), sems.at[chunks + chunk])
+
+    get_table = pltpu.make_async_copy(table_hbm, table, sems.at[2 * chunks])
+    get_sign = pltpu.make_async_copy(sign_hbm, sign, sems.at[2 * chunks + 1])
+    get_sign.start()
+    get_table.start()
+    for chunk in range(chunks):
+        load(chunk).start()
+    get_sign.wait()
+    get_table.wait()
+    signed[...] = (table[...].astype(f32) * (sign[...].astype(f32) * 2.0**-13)).astype(bf16)
+    for chunk in range(chunks):
+        load(chunk).wait()
+        high, low = halves(x[chunk])
+        out[chunk] = mm(signed[...], high) + mm(signed[...], low)
+        store(chunk).start()
+    for chunk in range(chunks):
+        store(chunk).wait()
 
 
 def local_mix(matrix, sign_flip):
     rows, features = matrix.shape
-    cols = 256
+    chunks = 4
+    anywhere = pl.BlockSpec(memory_space=pl.ANY)
+    block = pltpu.VMEM((chunks, rows, features // chunks), f32)
     return pl.pallas_call(
         local_mix_kernel,
-        grid=(features // cols,),
         out_shape=jax.ShapeDtypeStruct((rows, features), f32),
-        in_specs=[
-            pl.BlockSpec((rows, rows), lambda g: (0, 0)),
-            pl.BlockSpec((1, rows), lambda g: (0, 0)),
-            pl.BlockSpec((rows, cols), lambda g: (0, g)),
+        in_specs=[anywhere] * 3,
+        out_specs=anywhere,
+        scratch_shapes=[
+            pltpu.VMEM((rows, rows), bf16),
+            pltpu.VMEM((1, rows), jnp.int32),
+            pltpu.VMEM((rows, rows), bf16),
+            block,
+            block,
+            pltpu.SemaphoreType.DMA((2 * chunks + 2,)),
         ],
-        out_specs=pl.BlockSpec((rows, cols), lambda g: (0, g)),
-        scratch_shapes=[pltpu.VMEM((rows, rows), bf16)],
         compiler_params=params(60),
     )(jnp.asarray(local_table()), sign_flip.reshape(1, rows), matrix)
 
@@ -162,7 +187,7 @@
     )(ids, mine, theirs)
 
 
-def final_kernel(ids_ref, table_ref, r_ref, o_ref):
+def final_kernel(ids_ref, table_ref, r_ref, factor_ref, o_ref):
     high, low = halves(r_ref[...])
     total = mm(table_ref[...], high) + mm(table_ref[...], low)
     odd = (lax.broadcasted_iota(jnp.int32, total.shape, 0) >> 2) & 1
@@ -170,14 +195,14 @@
     o_ref[...] = total * jnp.where(flip, -32.0, 32.0)
 
 
-def final_mix(ids, received):
+def final_mix(ids, received, factor):
     return pl.pallas_call(
         final_kernel,
         out_shape=jax.ShapeDtypeStruct(received.shape, f32),
-        in_specs=[SMEM, VMEM, VMEM],
+        in_specs=[SMEM, VMEM, VMEM, pl.BlockSpec(memory_space=pl.ANY)],
         out_specs=VMEM,
         compiler_params=params(),
-    )(ids, jnp.asarray(final_table()), received)
+    )(ids, jnp.asarray(final_table()), received, factor)
 
 
 def lane_splat(x, lane):
@@ -232,7 +257,7 @@
         for b in range(8):
             r = lax.rsqrt(row_splat(e[b], b))
             scales.append(r)
-            multiplier = jnp.where(sub > b, e[b] * r, 0.0)
+            multiplier = jnp.where(sub > b, e[b], 0.0) * r
             scaled = row_splat(aug, b) * r
             finished.append(scaled)
             if b < 7:
@@ -360,7 +385,7 @@
     received = plane_exchange(to_send)
     other = swap_cores(own)
     factor = factor_rows(ids, ridge_weights.reshape(1, FEAT), own, other)
-    sketch = final_mix(ids, received.reshape(256, FEAT))
+    sketch = final_mix(ids, received.reshape(256, FEAT), factor)
     return sketch, factor
 
 

time: 155 us -> 139 us (0.90)
  blocking collectives: 62.6 us -> 43.1 us
  starting transfers between devices: 14.1 us -> 17.6 us
    all_to_all x3 -> x2, blocking collectives: 62.6 us -> 43.1 us  [plane_exchange(): lax.all_to_all(x, 'inner', 0, 0, axis_index_groups=PLANES, tiled=True)]
    all_to_all x0 -> x1, starting transfers between devices: none -> 3.66 us  [plane_exchange(): lax.all_to_all(x, 'inner', 0, 0, axis_index_groups=PLANES, tiled=True)]
  transfers between devices with their start and end apart: 6 -> 7, of which waited for: 5 -> 5; matrix products, arithmetic and copies ran while one was open for 0% -> 0% of each run, Pallas kernels for 1% -> 24%
where the time goes in v7:
time: 139 us
  Pallas kernels  44.4 us (32%)
  blocking collectives  43.1 us (31%)
  waiting for transfers between devices  31.9 us (23%)
  starting transfers between devices  17.6 us (13%)
    all_to_all x2, blocking collectives, plane_exchange(): lax.all_to_all(x, 'inner', 0, 0, axis_index_groups=PLANES, tiled=True)  43.1 us
    pallas_call x1, Pallas kernels, factor_rows(): pl.pallas_call(factor_kernel, out_shape=jax.ShapeDtypeStruct((8, FEAT), f...  33.5 us
    all_to_all x1, waiting for transfers between devices, local(): lax.all_to_all(mixed.reshape(4, 128, FEAT), 'inner', 0, 0, axis_index_gro...  25.2 us
    ppermute x2, starting transfers between devices, swap_cores(): return lax.ppermute(x, 'outer', [(0, 1), (1, 0)])  5.87 us
    all_to_all x1, starting transfers between devices, local(): lax.all_to_all(mixed.reshape(4, 128, FEAT), 'inner', 0, 0, axis_index_gro...  5.87 us
    pallas_call x1, Pallas kernels, local_mix(): pl.pallas_call(local_mix_kernel, out_shape=jax.ShapeDtypeStruct((rows, fe...  4.94 us
    ppermute x3, waiting for transfers between devices, along_z(): lax.ppermute(x, 'inner', [(i, (i + 16 * distance) % 64) for i in range(64)])  4.43 us
    all_to_all x1, starting transfers between devices, plane_exchange(): lax.all_to_all(x, 'inner', 0, 0, axis_index_groups=PLANES, tiled=True)  3.66 us
  transfers between devices with their start and end apart: 7, of which 5 were waited for; matrix products, arithmetic and copies ran while one was open for 0% of the time, Pallas kernels for 24%

profile of v7, /device:TPU:1, one launch (start us, length us, event | category | flops | bytes accessed | tf_op | source)
XLA Modules:
  0.0 138.9 jit_solution(15940300832071899552)
XLA Ops:
  0.6 4.9 %shard_map.77 = f32[512,1024]{1,0:T(8,128)} custom-call(bf16[512,512]{1,0:T(8,128)(2,1)} %constant.37.clone.table_hbm, s32[1,512]{1,0:T(1,128)} %bitcast.23, f32[512,1024]{1,0:T(8,128)} %x_hbm.1), custom_call_target="tpu_custom_call" | custom-call | tf_op jit(solution)/shard_map/pallas_call | solution.py:97
  5.6 5.9 %all-to-all-start = ((f32[4,128,1024]{2,1,0:T(8,128)}), f32[4,128,1024]{2,1,0:T(8,128)S(1)}, u32[]{:S(2)}, u32[]{:S(2)}) async-start(f32[4,128,1024]{2,1,0:T(8,128)} %bitcast.20), calls=%async_computation | async-start | bytes 4194304 | tf_op jit(solution)/shard_map/all_to_all | solution.py:375
  11.5 0.1 reshape.33
  11.6 0.1 copy.10
  11.7 25.2 %all-to-all-done.y_ref = f32[4,128,1024]{2,1,0:T(8,128)S(1)} async-done(((f32[4,128,1024]{2,1,0:T(8,128)}), f32[4,128,1024]{2,1,0:T(8,128)S(1)}, u32[]{:S(2)}, u32[]{:S(2)}) %all-to-all-start) | async-done | bytes 2097184 | tf_op jit(solution)/shard_map/all_to_all | solution.py:375
  36.9 0.9 shard_map.78
  37.8 1.9 %collective-permute-start = (f32[256,1024]{1,0:T(8,128)S(1)}, f32[256,1024]{1,0:T(8,128)S(1)}, u32[]{:S(2)}, u32[]{:S(2)}) collective-permute-start(f32[256,1024]{1,0:T(8,128)S(1)} %bitcast.13), channel_id=1, source_target_pairs={{0,64},{64,0},{1,65},{65,1},{2,66},{66,2},{3,67},{67,3},{4,68},{68... | collective-permute-start | bytes 3145736 | tf_op jit(solution)/shard_map/ppermute | solution.py:358
  39.8 0.1 pad_add_fusion.ids_ref
  39.9 2.2 %collective-permute-done.w_ref = f32[256,1024]{1,0:T(8,128)S(1)} collective-permute-done((f32[256,1024]{1,0:T(8,128)S(1)}, f32[256,1024]{1,0:T(8,128)S(1)}, u32[]{:S(2)}, u32[]{:S(2)}) %collective-permute-start) | collective-permute-done | bytes 1048608 | tf_op jit(solution)/shard_map/ppermute | solution.py:358
  42.1 3.1 %shard_map.79 = (f32[16,144,128]{2,1,0:T(8,128)S(1)}, f32[16,2,8,1024]{3,2,1,0:T(8,128)}) custom-call(s32[2]{0:T(128)S(1)} %pad_add_fusion.ids_ref, f32[256,1024]{1,0:T(8,128)S(1)} %bitcast.14, f32[256,1024]{1,0:T(8,128)S(1)} %collective-permute-done.w_ref), custom_call_target="tpu_custom_call" | custom-call | tf_op jit(solution)/shard_map/pallas_call | solution.py:177
  45.2 24.6 %all_to_all.20 = f32[16,144,128]{2,1,0:T(8,128)S(1)} all-to-all(f32[16,144,128]{2,1,0:T(8,128)S(1)} %get-tuple-element.7), channel_id=1, replica_groups={{0,1,2,3,4,5,6,7,8,9,10,11,12,13,14,15},{16,17,18,19,20,21,22,23,24,25,..., dimensions={0} | all-to-all | bytes 2359296 | tf_op jit(solution)/shard_map/all_to_all | solution.py:366
  69.9 1.0 collective-permute-start.3
  70.8 0.6 collective-permute-start.2
  71.4 0.7 collective-permute-start.1
  72.1 1.0 collective-permute-done.3
  73.1 2.1 %collective-permute-done.2 = f32[144,128]{1,0:T(8,128)S(1)} collective-permute-done((f32[144,128]{1,0:T(8,128)S(1)}, f32[144,128]{1,0:T(8,128)S(1)}, u32[]{:S(2)}, u32[]{:S(2)}) %collective-permute-start.2) | collective-permute-done | bytes 73760 | tf_op jit(solution)/shard_map/ppermute | solution.py:362
  75.2 1.3 collective-permute-done.1
  76.6 0.1 broadcast_in_dim.10
  76.6 18.5 %all_to_all.21 = f32[16,144,128]{2,1,0:T(8,128)S(1)} all-to-all(f32[16,144,128]{2,1,0:T(8,128)S(1)} %broadcast_in_dim.10), channel_id=1, replica_groups={{0,1,2,3,4,5,6,7,8,9,10,11,12,13,14,15},{16,17,18,19,20,21,22,23,24,25,..., dimensions={0} | all-to-all | bytes 2359296 | tf_op jit(solution)/shard_map/all_to_all | solution.py:366
  95.1 3.9 %collective-permute-start.4 = (f32[2304,128]{1,0:T(8,128)S(1)}, f32[2304,128]{1,0:T(8,128)}, u32[]{:S(2)}, u32[]{:S(2)}) collective-permute-start(f32[2304,128]{1,0:T(8,128)S(1)} %bitcast.16), channel_id=1, source_target_pairs={{0,64},{64,0},{1,65},{65,1},{2,66},{66,2},{3,67},{67,3},{4,68},{68... | collective-permute-start | bytes 3538952 | tf_op jit(solution)/shard_map/ppermute | solution.py:358
  99.0 3.7 %all-to-all-start.3 = ((f32[16,2,8,1024]{3,2,1,0:T(8,128)}), f32[16,2,8,1024]{3,2,1,0:T(8,128)S(1)}, u32[]{:S(2)}, u32[]{:S(2)}) async-start(f32[16,2,8,1024]{3,2,1,0:T(8,128)} %get-tuple-element.8), calls=%async_computation.3 | async-start | bytes 2097152 | tf_op jit(solution)/shard_map/all_to_all | solution.py:366
  102.7 33.5 %shard_map.80.factor_ref = f32[8,1024]{1,0:T(8,128)} custom-call(s32[2]{0:T(128)S(1)} %pad_add_fusion.ids_ref, f32[1,1024]{1,0:T(1,128)S(1)} %bitcast.19, f32[2304,128]{1,0:T(8,128)S(1)} %bitcast.17, f32[2304,128]{1,0:T(8,128)} %collective-permute-done.4.other_ref), custom_call_target="tpu_custom_call" | custom-call | flops 40000000000 | bytes 2097152 | tf_op jit(solution)/shard_map/pallas_call | solution.py:345
  136.2 0.8 copy-done.1
  137.0 2.0 %shard_map.81 = f32[256,1024]{1,0:T(8,128)} custom-call(s32[2]{0:T(128)S(1)} %pad_add_fusion.ids_ref, bf16[256,256]{1,0:T(8,128)(2,1)S(1)} %copy-done, f32[256,1024]{1,0:T(8,128)S(1)} %bitcast.15, f32[8,1024]{1,0:T(8,128)S(1)} %copy-done.1), custom_call_target="tpu_custom_call" | custom-call | tf_op jit(solution)/shard_map/pallas_call | solution.py:199
  (13 shorter events, 0.1 us)
Async XLA Ops:
  5.6 5.9 %copy-start.3 = (s32[128,2]{0,1:T(2,128)S(1)}, s32[128,2]{0,1:T(2,128)}, u32[]{:S(2)}) copy-start(s32[128,2]{0,1:T(2,128)} %param.8) | copy-start | bytes 3076
  5.6 31.3 %all-to-all-start = ((f32[4,128,1024]{2,1,0:T(8,128)}), f32[4,128,1024]{2,1,0:T(8,128)S(1)}, u32[]{:S(2)}, u32[]{:S(2)}) async-start(f32[4,128,1024]{2,1,0:T(8,128)} %bitcast.20), calls=%async_computation | async-start | bytes 4194304 | tf_op jit(solution)/shard_map/all_to_all | solution.py:375
  37.8 4.2 %collective-permute-start = (f32[256,1024]{1,0:T(8,128)S(1)}, f32[256,1024]{1,0:T(8,128)S(1)}, u32[]{:S(2)}, u32[]{:S(2)}) collective-permute-start(f32[256,1024]{1,0:T(8,128)S(1)} %bitcast.13), channel_id=1, source_target_pairs={{0,64},{64,0},{1,65},{65,1},{2,66},{66,2},{3,67},{67,3},{4,68},{68... | collective-permute-start | bytes 3145736 | tf_op jit(solution)/shard_map/ppermute | solution.py:358
  69.9 3.3 %collective-permute-start.3 = (f32[144,128]{1,0:T(8,128)S(1)}, f32[144,128]{1,0:T(8,128)S(1)}, u32[]{:S(2)}, u32[]{:S(2)}) collective-permute-start(f32[144,128]{1,0:T(8,128)S(1)} %reduce_sum.9), channel_id=1, source_target_pairs={{0,48},{1,49},{2,50},{3,51},{4,52},{5,53},{6,54},{7,55},{8,56},{9,... | collective-permute-start | bytes 221192 | tf_op jit(solution)/shard_map/ppermute | solution.py:362
  70.8 4.4 %collective-permute-start.2 = (f32[144,128]{1,0:T(8,128)S(1)}, f32[144,128]{1,0:T(8,128)S(1)}, u32[]{:S(2)}, u32[]{:S(2)}) collective-permute-start(f32[144,128]{1,0:T(8,128)S(1)} %reduce_sum.9), channel_id=1, source_target_pairs={{0,16},{1,17},{2,18},{3,19},{4,20},{5,21},{6,22},{7,23},{8,24},{9,... | collective-permute-start | bytes 221192 | tf_op jit(solution)/shard_map/ppermute | solution.py:362
  71.4 5.1 %collective-permute-start.1 = (f32[144,128]{1,0:T(8,128)S(1)}, f32[144,128]{1,0:T(8,128)S(1)}, u32[]{:S(2)}, u32[]{:S(2)}) collective-permute-start(f32[144,128]{1,0:T(8,128)S(1)} %reduce_sum.9), channel_id=1, source_target_pairs={{0,32},{1,33},{2,34},{3,35},{4,36},{5,37},{6,38},{7,39},{8,40},{9,... | collective-permute-start | bytes 221192 | tf_op jit(solution)/shard_map/ppermute | solution.py:362
  95.1 7.6 %copy-start.2 = (f32[1024]{0:T(1024)S(1)}, f32[1024]{0:T(1024)}, u32[]{:S(2)}) copy-start(f32[1024]{0:T(1024)} %param.9) | copy-start | bytes 12292
  95.1 7.6 %collective-permute-start.4 = (f32[2304,128]{1,0:T(8,128)S(1)}, f32[2304,128]{1,0:T(8,128)}, u32[]{:S(2)}, u32[]{:S(2)}) collective-permute-start(f32[2304,128]{1,0:T(8,128)S(1)} %bitcast.16), channel_id=1, source_target_pairs={{0,64},{64,0},{1,65},{65,1},{2,66},{66,2},{3,67},{67,3},{4,68},{68... | collective-permute-start | bytes 3538952 | tf_op jit(solution)/shard_map/ppermute | solution.py:358
  99.0 37.2 %all-to-all-start.3 = ((f32[16,2,8,1024]{3,2,1,0:T(8,128)}), f32[16,2,8,1024]{3,2,1,0:T(8,128)S(1)}, u32[]{:S(2)}, u32[]{:S(2)}) async-start(f32[16,2,8,1024]{3,2,1,0:T(8,128)} %get-tuple-element.8), calls=%async_computation.3 | async-start | bytes 2097152 | tf_op jit(solution)/shard_map/all_to_all | solution.py:366
  102.7 33.5 %copy-start = (bf16[256,256]{1,0:T(8,128)(2,1)S(1)}, bf16[256,256]{1,0:T(8,128)(2,1)}, u32[]{:S(2)}) copy-start(bf16[256,256]{1,0:T(8,128)(2,1)} %constant.38.clone.table_ref) | copy-start | bytes 393220
  136.2 0.8 copy-start.1

commit v8 on v7

--- a/solution.py
+++ b/solution.py
@@ -15,6 +15,7 @@
 PANELS = FEAT // NB
 STRIPS = ((0, 3, 4, 7), (1, 2, 5, 6))
 GRAM_ROWS = 144
+DIRECT = 3
 LEFT = (0, 0, 0, 1, 1, 2)
 RIGHT = (0, 1, 2, 0, 1, 0)
 Z_GROUPS = [[i + 16 * j for j in range(4)] for i in range(16)]
@@ -187,7 +188,7 @@
     )(ids, mine, theirs)
 
 
-def final_kernel(ids_ref, table_ref, r_ref, factor_ref, o_ref):
+def final_kernel(ids_ref, table_ref, r_ref, o_ref):
     high, low = halves(r_ref[...])
     total = mm(table_ref[...], high) + mm(table_ref[...], low)
     odd = (lax.broadcasted_iota(jnp.int32, total.shape, 0) >> 2) & 1
@@ -195,14 +196,14 @@
     o_ref[...] = total * jnp.where(flip, -32.0, 32.0)
 
 
-def final_mix(ids, received, factor):
+def final_mix(ids, received):
     return pl.pallas_call(
         final_kernel,
         out_shape=jax.ShapeDtypeStruct(received.shape, f32),
-        in_specs=[SMEM, VMEM, VMEM, pl.BlockSpec(memory_space=pl.ANY)],
+        in_specs=[SMEM, VMEM, VMEM],
         out_specs=VMEM,
         compiler_params=params(),
-    )(ids, jnp.asarray(final_table()), received, factor)
+    )(ids, jnp.asarray(final_table()), received)
 
 
 def lane_splat(x, lane):
@@ -247,49 +248,65 @@
 def factor_block(w, upper, inverse):
     lane = lax.broadcasted_iota(jnp.int32, (8, NB), 1)
     sub = lax.broadcasted_iota(jnp.int32, (8, NB), 0)
+    groups = NB // 8
     rows = w[0:8, :]
     e = [lane_splat(rows, a) for a in range(8)]
-    for step in range(16):
+    held = {}
+    for step in range(groups):
         base = 8 * step
         inside = (lane >= base) & (lane < base + 8)
+        last = min(step + DIRECT, groups - 1)
+        near = range(step + 1, last + 1)
+        for group in near:
+            if group not in held:
+                held[group] = w[8 * group : 8 * group + 8, :]
+        columns = {group: [lane_splat(held[group], base + b) for b in range(8)] for group in near}
+        if near:
+            start = [lane_splat(held[step + 1], base + 8 + a) for a in range(8)]
         aug = jnp.where(inside, jnp.where(lane == base + sub, 1.0, 0.0), rows)
         scales, finished = [], []
+        multipliers = {group: [] for group in near}
         for b in range(8):
             r = lax.rsqrt(row_splat(e[b], b))
             scales.append(r)
             multiplier = jnp.where(sub > b, e[b], 0.0) * r
+            c = {a: row_splat(e[a], b) * r for a in range(b + 1, 8)}
             scaled = row_splat(aug, b) * r
             finished.append(scaled)
             if b < 7:
                 for a in range(b + 1, 8):
-                    e[a] = e[a] - multiplier * (row_splat(e[a], b) * r)
+                    e[a] = e[a] - multiplier * c[a]
                 rows = rows - multiplier * (row_splat(rows, b) * r)
                 aug = aug - multiplier * scaled
+            for group in near:
+                column = columns[group]
+                multipliers[group].append(column[b] * r)
+                for a in range(b + 1, 8):
+                    column[a] = column[a] - multipliers[group][b] * c[a]
         scale = by_row(sub, scales)
-        if step < 15:
-            columns = [lane_splat(rows, base + 8 + a) * scale for a in range(8)]
         left, right = rows * scale, aug * scale
         upper[base : base + 8, :] = jnp.where(lane >= base + sub, left, 0.0)
         inverse[base : base + 8, :] = jnp.where(lane <= base + sub, right, 0.0)
-        if step == 15:
+        if not near:
             break
-        if step < 14:
+        if last < groups - 1:
             update = outer_sum(left, right)
-        coming = jnp.where(inside, 0.0, w[base + 8 : base + 16, :])
-        start = [lane_splat(coming, base + 8 + a) for a in range(8)]
-        c = {(b, a): row_splat(columns[a], b) for b in range(8) for a in range(8)}
-        turned = [by_row(sub, [c[b, a] for a in range(8)]) for b in range(8)]
-        e = [start[a] - tree_sum([turned[b] * c[b, a] for b in range(8)]) for a in range(8)]
-        rows = coming - tree_sum([turned[b] * finished[b] for b in range(8)])
-        if step < 14:
-            after = base + 16
+        m = multipliers[step + 1]
+        e = [start[a] - tree_sum([m[b] * row_splat(m[b], a) for b in range(8)]) for a in range(8)]
+        for group in near:
+            terms = [multipliers[group][b] * finished[b] for b in range(8)]
+            held[group] = jnp.where(inside, 0.0, held[group]) - tree_sum(terms)
+        rows = held.pop(step + 1)
+        if last < groups - 1:
+            after = 8 * (last + 1)
             rest = lax.broadcasted_iota(jnp.int32, (NB - after, NB), 1)
             cleared = jnp.where((rest >= base) & (rest < base + 8), 0.0, w[after:, :])
             w[after:, :] = cleared - update[after:, :]
 
 
-def factor_kernel(ids_ref, ridge_ref, own_ref, other_ref, o_ref, a, w, upper, inverse, stack1, stack2):
+def factor_kernel(ids_ref, ridge_ref, own_ref, other_ref, o_ref, done_ref, a, w, upper, inverse, stack1, stack2):
     core, position = ids_ref[0], ids_ref[1]
+    done_ref[0], done_ref[1] = core, position
     eye = lax.broadcasted_iota(jnp.int32, (NB, NB), 0) == lax.broadcasted_iota(jnp.int32, (NB, NB), 1)
     for which in range(2):
 
@@ -344,9 +361,9 @@
 def factor_rows(ids, ridge, own, other):
     return pl.pallas_call(
         factor_kernel,
-        out_shape=jax.ShapeDtypeStruct((8, FEAT), f32),
+        out_shape=(jax.ShapeDtypeStruct((8, FEAT), f32), jax.ShapeDtypeStruct((2,), jnp.int32)),
         in_specs=[SMEM, VMEM, VMEM, VMEM],
-        out_specs=VMEM,
+        out_specs=(VMEM, SMEM),
         scratch_shapes=[pltpu.VMEM((FEAT, FEAT), f32)] + [pltpu.VMEM((NB, NB), f32)] * 3
         + [pltpu.VMEM((6 * NB, FEAT), bf16)] * 2,
         compiler_params=params(),
@@ -384,8 +401,8 @@
     to_send, own = lax.optimization_barrier((to_send, own))
     received = plane_exchange(to_send)
     other = swap_cores(own)
-    factor = factor_rows(ids, ridge_weights.reshape(1, FEAT), own, other)
-    sketch = final_mix(ids, received.reshape(256, FEAT), factor)
+    factor, done = factor_rows(ids, ridge_weights.reshape(1, FEAT), own, other)
+    sketch = final_mix(done, received.reshape(256, FEAT))
     return sketch, factor
 
 

time: 139 us -> 135 us (0.971)
  Pallas kernels: 44.4 us -> 40.4 us
    pallas_call x1, Pallas kernels: 33.5 us -> 29.5 us  [factor_rows(): pl.pallas_call(factor_kernel, out_shape=(jax.ShapeDtypeStruct((8, FEAT),...]
  transfers between devices with their start and end apart: 7 -> 7, of which waited for: 5 -> 5; matrix products, arithmetic and copies ran while one was open for 0% -> 0% of each run, Pallas kernels for 24% -> 22%
where the time goes in v8:
time: 135 us; the launch traced here: 134 us
  blocking collectives  43.1 us (32%)
  Pallas kernels  40.4 us (30%)
  waiting for transfers between devices  31.9 us (24%)
  starting transfers between devices  17.6 us (13%)
    all_to_all x2, blocking collectives, plane_exchange(): lax.all_to_all(x, 'inner', 0, 0, axis_index_groups=PLANES, tiled=True)  43.1 us
    pallas_call x1, Pallas kernels, factor_rows(): pl.pallas_call(factor_kernel, out_shape=(jax.ShapeDtypeStruct((8, FEAT),...  29.5 us
    all_to_all x1, waiting for transfers between devices, local(): lax.all_to_all(mixed.reshape(4, 128, FEAT), 'inner', 0, 0, axis_index_gro...  25.2 us
    ppermute x2, starting transfers between devices, swap_cores(): return lax.ppermute(x, 'outer', [(0, 1), (1, 0)])  5.87 us
    all_to_all x1, starting transfers between devices, local(): lax.all_to_all(mixed.reshape(4, 128, FEAT), 'inner', 0, 0, axis_index_gro...  5.87 us
    pallas_call x1, Pallas kernels, local_mix(): pl.pallas_call(local_mix_kernel, out_shape=jax.ShapeDtypeStruct((rows, fe...  4.94 us
    ppermute x3, waiting for transfers between devices, along_z(): lax.ppermute(x, 'inner', [(i, (i + 16 * distance) % 64) for i in range(64)])  4.43 us
    all_to_all x1, starting transfers between devices, plane_exchange(): lax.all_to_all(x, 'inner', 0, 0, axis_index_groups=PLANES, tiled=True)  3.66 us
  transfers between devices with their start and end apart: 7, of which 5 were waited for; matrix products, arithmetic and copies ran while one was open for 0% of the time, Pallas kernels for 22%

profile of v8, /device:TPU:1, one launch (start us, length us, event | category | flops | bytes accessed | tf_op | source)
XLA Modules:
  0.0 134.2 jit_solution(2239832198140735954)
XLA Ops:
  0.6 4.9 %shard_map.77 = f32[512,1024]{1,0:T(8,128)} custom-call(bf16[512,512]{1,0:T(8,128)(2,1)} %constant.37.clone.table_hbm, s32[1,512]{1,0:T(1,128)} %bitcast.23, f32[512,1024]{1,0:T(8,128)} %x_hbm.1), custom_call_target="tpu_custom_call" | custom-call | tf_op jit(solution)/shard_map/pallas_call | solution.py:98
  5.6 5.9 %all-to-all-start = ((f32[4,128,1024]{2,1,0:T(8,128)}), f32[4,128,1024]{2,1,0:T(8,128)S(1)}, u32[]{:S(2)}, u32[]{:S(2)}) async-start(f32[4,128,1024]{2,1,0:T(8,128)} %bitcast.20), calls=%async_computation | async-start | bytes 4194304 | tf_op jit(solution)/shard_map/all_to_all | solution.py:392
  11.5 0.1 reshape.34
  11.6 0.1 copy.10
  11.7 25.2 %all-to-all-done.y_ref = f32[4,128,1024]{2,1,0:T(8,128)S(1)} async-done(((f32[4,128,1024]{2,1,0:T(8,128)}), f32[4,128,1024]{2,1,0:T(8,128)S(1)}, u32[]{:S(2)}, u32[]{:S(2)}) %all-to-all-start) | async-done | bytes 2097184 | tf_op jit(solution)/shard_map/all_to_all | solution.py:392
  36.9 0.9 shard_map.78
  37.8 1.9 %collective-permute-start = (f32[256,1024]{1,0:T(8,128)S(1)}, f32[256,1024]{1,0:T(8,128)S(1)}, u32[]{:S(2)}, u32[]{:S(2)}) collective-permute-start(f32[256,1024]{1,0:T(8,128)S(1)} %bitcast.13), channel_id=1, source_target_pairs={{0,64},{64,0},{1,65},{65,1},{2,66},{66,2},{3,67},{67,3},{4,68},{68... | collective-permute-start | bytes 3145736 | tf_op jit(solution)/shard_map/ppermute | solution.py:375
  39.8 0.1 pad_add_fusion.ids_ref
  39.9 2.2 %collective-permute-done.w_ref = f32[256,1024]{1,0:T(8,128)S(1)} collective-permute-done((f32[256,1024]{1,0:T(8,128)S(1)}, f32[256,1024]{1,0:T(8,128)S(1)}, u32[]{:S(2)}, u32[]{:S(2)}) %collective-permute-start) | collective-permute-done | bytes 1048608 | tf_op jit(solution)/shard_map/ppermute | solution.py:375
  42.1 3.1 %shard_map.79 = (f32[16,144,128]{2,1,0:T(8,128)S(1)}, f32[16,2,8,1024]{3,2,1,0:T(8,128)}) custom-call(s32[2]{0:T(128)S(1)} %pad_add_fusion.ids_ref, f32[256,1024]{1,0:T(8,128)S(1)} %bitcast.14, f32[256,1024]{1,0:T(8,128)S(1)} %collective-permute-done.w_ref), custom_call_target="tpu_custom_call" | custom-call | tf_op jit(solution)/shard_map/pallas_call | solution.py:178
  45.2 24.6 %all_to_all.20 = f32[16,144,128]{2,1,0:T(8,128)S(1)} all-to-all(f32[16,144,128]{2,1,0:T(8,128)S(1)} %get-tuple-element.9), channel_id=1, replica_groups={{0,1,2,3,4,5,6,7,8,9,10,11,12,13,14,15},{16,17,18,19,20,21,22,23,24,25,..., dimensions={0} | all-to-all | bytes 2359296 | tf_op jit(solution)/shard_map/all_to_all | solution.py:383
  69.8 0.1 reduce_sum.9
  69.9 1.0 collective-permute-start.3
  70.8 0.6 collective-permute-start.2
  71.4 0.7 collective-permute-start.1
  72.1 1.0 collective-permute-done.3
  73.1 2.1 %collective-permute-done.2 = f32[144,128]{1,0:T(8,128)S(1)} collective-permute-done((f32[144,128]{1,0:T(8,128)S(1)}, f32[144,128]{1,0:T(8,128)S(1)}, u32[]{:S(2)}, u32[]{:S(2)}) %collective-permute-start.2) | collective-permute-done | bytes 73760 | tf_op jit(solution)/shard_map/ppermute | solution.py:379
  75.2 1.3 collective-permute-done.1
  76.6 0.1 broadcast_in_dim.10
  76.6 18.5 %all_to_all.21 = f32[16,144,128]{2,1,0:T(8,128)S(1)} all-to-all(f32[16,144,128]{2,1,0:T(8,128)S(1)} %broadcast_in_dim.10), channel_id=1, replica_groups={{0,1,2,3,4,5,6,7,8,9,10,11,12,13,14,15},{16,17,18,19,20,21,22,23,24,25,..., dimensions={0} | all-to-all | bytes 2359296 | tf_op jit(solution)/shard_map/all_to_all | solution.py:383
  95.1 3.9 %collective-permute-start.4 = (f32[2304,128]{1,0:T(8,128)S(1)}, f32[2304,128]{1,0:T(8,128)}, u32[]{:S(2)}, u32[]{:S(2)}) collective-permute-start(f32[2304,128]{1,0:T(8,128)S(1)} %bitcast.16), channel_id=1, source_target_pairs={{0,64},{64,0},{1,65},{65,1},{2,66},{66,2},{3,67},{67,3},{4,68},{68... | collective-permute-start | bytes 3538952 | tf_op jit(solution)/shard_map/ppermute | solution.py:375
  99.0 3.7 %all-to-all-start.3 = ((f32[16,2,8,1024]{3,2,1,0:T(8,128)}), f32[16,2,8,1024]{3,2,1,0:T(8,128)S(1)}, u32[]{:S(2)}, u32[]{:S(2)}) async-start(f32[16,2,8,1024]{3,2,1,0:T(8,128)} %get-tuple-element.12), calls=%async_computation.3 | async-start | bytes 2097152 | tf_op jit(solution)/shard_map/all_to_all | solution.py:383
  102.7 29.5 %shard_map.80 = (f32[8,1024]{1,0:T(8,128)}, s32[2]{0:T(128)S(1)}) custom-call(s32[2]{0:T(128)S(1)} %pad_add_fusion.ids_ref, f32[1,1024]{1,0:T(1,128)S(1)} %bitcast.19, f32[2304,128]{1,0:T(8,128)S(1)} %bitcast.17, f32[2304,128]{1,0:T(8,128)} %collective-permute-done.4.other_ref), custom_call_target="tpu_custom_call" | custom-call | flops 40000000000 | bytes 2097152 | tf_op jit(solution)/shard_map/pallas_call | solution.py:362
  132.2 2.0 %shard_map.81 = f32[256,1024]{1,0:T(8,128)} custom-call(s32[2]{0:T(128)S(1)} %get-tuple-element.11.ids_ref, bf16[256,256]{1,0:T(8,128)(2,1)S(1)} %copy-done, f32[256,1024]{1,0:T(8,128)S(1)} %bitcast.15), custom_call_target="tpu_custom_call" | custom-call | tf_op jit(solution)/shard_map/pallas_call | solution.py:200
  (11 shorter events, 0.1 us)
Async XLA Ops:
  5.6 5.9 %copy-start.2 = (s32[128,2]{0,1:T(2,128)S(1)}, s32[128,2]{0,1:T(2,128)}, u32[]{:S(2)}) copy-start(s32[128,2]{0,1:T(2,128)} %param.8) | copy-start | bytes 3076
  5.6 31.3 %all-to-all-start = ((f32[4,128,1024]{2,1,0:T(8,128)}), f32[4,128,1024]{2,1,0:T(8,128)S(1)}, u32[]{:S(2)}, u32[]{:S(2)}) async-start(f32[4,128,1024]{2,1,0:T(8,128)} %bitcast.20), calls=%async_computation | async-start | bytes 4194304 | tf_op jit(solution)/shard_map/all_to_all | solution.py:392
  37.8 4.2 %collective-permute-start = (f32[256,1024]{1,0:T(8,128)S(1)}, f32[256,1024]{1,0:T(8,128)S(1)}, u32[]{:S(2)}, u32[]{:S(2)}) collective-permute-start(f32[256,1024]{1,0:T(8,128)S(1)} %bitcast.13), channel_id=1, source_target_pairs={{0,64},{64,0},{1,65},{65,1},{2,66},{66,2},{3,67},{67,3},{4,68},{68... | collective-permute-start | bytes 3145736 | tf_op jit(solution)/shard_map/ppermute | solution.py:375
  69.9 3.3 %collective-permute-start.3 = (f32[144,128]{1,0:T(8,128)S(1)}, f32[144,128]{1,0:T(8,128)S(1)}, u32[]{:S(2)}, u32[]{:S(2)}) collective-permute-start(f32[144,128]{1,0:T(8,128)S(1)} %reduce_sum.9), channel_id=1, source_target_pairs={{0,48},{1,49},{2,50},{3,51},{4,52},{5,53},{6,54},{7,55},{8,56},{9,... | collective-permute-start | bytes 221192 | tf_op jit(solution)/shard_map/ppermute | solution.py:379
  70.8 4.4 %collective-permute-start.2 = (f32[144,128]{1,0:T(8,128)S(1)}, f32[144,128]{1,0:T(8,128)S(1)}, u32[]{:S(2)}, u32[]{:S(2)}) collective-permute-start(f32[144,128]{1,0:T(8,128)S(1)} %reduce_sum.9), channel_id=1, source_target_pairs={{0,16},{1,17},{2,18},{3,19},{4,20},{5,21},{6,22},{7,23},{8,24},{9,... | collective-permute-start | bytes 221192 | tf_op jit(solution)/shard_map/ppermute | solution.py:379
  71.4 5.1 %collective-permute-start.1 = (f32[144,128]{1,0:T(8,128)S(1)}, f32[144,128]{1,0:T(8,128)S(1)}, u32[]{:S(2)}, u32[]{:S(2)}) collective-permute-start(f32[144,128]{1,0:T(8,128)S(1)} %reduce_sum.9), channel_id=1, source_target_pairs={{0,32},{1,33},{2,34},{3,35},{4,36},{5,37},{6,38},{7,39},{8,40},{9,... | collective-permute-start | bytes 221192 | tf_op jit(solution)/shard_map/ppermute | solution.py:379
  95.1 7.6 %copy-start.1 = (f32[1024]{0:T(1024)S(1)}, f32[1024]{0:T(1024)}, u32[]{:S(2)}) copy-start(f32[1024]{0:T(1024)} %param.9) | copy-start | bytes 12292
  95.1 7.6 %collective-permute-start.4 = (f32[2304,128]{1,0:T(8,128)S(1)}, f32[2304,128]{1,0:T(8,128)}, u32[]{:S(2)}, u32[]{:S(2)}) collective-permute-start(f32[2304,128]{1,0:T(8,128)S(1)} %bitcast.16), channel_id=1, source_target_pairs={{0,64},{64,0},{1,65},{65,1},{2,66},{66,2},{3,67},{67,3},{4,68},{68... | collective-permute-start | bytes 3538952 | tf_op jit(solution)/shard_map/ppermute | solution.py:375
  99.0 33.2 %all-to-all-start.3 = ((f32[16,2,8,1024]{3,2,1,0:T(8,128)}), f32[16,2,8,1024]{3,2,1,0:T(8,128)S(1)}, u32[]{:S(2)}, u32[]{:S(2)}) async-start(f32[16,2,8,1024]{3,2,1,0:T(8,128)} %get-tuple-element.12), calls=%async_computation.3 | async-start | bytes 2097152 | tf_op jit(solution)/shard_map/all_to_all | solution.py:383
  102.7 29.5 %copy-start = (bf16[256,256]{1,0:T(8,128)(2,1)S(1)}, bf16[256,256]{1,0:T(8,128)(2,1)}, u32[]{:S(2)}) copy-start(bf16[256,256]{1,0:T(8,128)(2,1)} %constant.38.clone.table_ref) | copy-start | bytes 393220

commit v9 on v8

--- a/solution.py
+++ b/solution.py
@@ -10,6 +10,7 @@
 bf16 = jnp.bfloat16
 VMEM = pl.BlockSpec(memory_space=pltpu.VMEM)
 SMEM = pl.BlockSpec(memory_space=pltpu.SMEM)
+ANY = pl.BlockSpec(memory_space=pl.ANY)
 FEAT = 1024
 NB = 128
 PANELS = FEAT // NB
@@ -148,14 +149,20 @@
     )(keep_rows, y)
 
 
-def gram_kernel(ids_ref, v_ref, w_ref, g_ref, s_ref, high, low, flat):
+def gram_kernel(ids_ref, v_ref, w_hbm, g_ref, s_hbm, high, low, flat, w_ref, sems):
     core = ids_ref[0]
-    own = pl.ds(pl.multiple_of(core * 128, 128), 128)
+    fetch = pltpu.make_async_copy(w_hbm, w_ref, sems.at[0])
+    fetch.start()
+    send_mine = pltpu.make_async_copy(v_ref.at[core], s_hbm.at[:, 0], sems.at[1])
+    send_mine.start()
+    send_theirs = pltpu.make_async_copy(w_ref.at[core], s_hbm.at[:, 1], sems.at[2])
     for part, ref in enumerate((v_ref, w_ref)):
-        h, l = halves(ref[...])
+        if part:
+            fetch.wait()
+            send_theirs.start()
+        h, l = halves(ref[...].reshape(256, FEAT))
         high[256 * part : 256 * part + 256, :] = h
         low[256 * part : 256 * part + 256, :] = l
-        s_ref[:, part] = ref[own, :].reshape(16, 8, FEAT)
     for which, strips in enumerate(STRIPS):
 
         @pl.when(core == which)
@@ -171,37 +178,58 @@
 
     for piece in range(16):
         g_ref[piece] = flat[GRAM_ROWS * piece : GRAM_ROWS * (piece + 1), :]
+    send_mine.wait()
+    send_theirs.wait()
 
 
 def gram_half(ids, mine, theirs):
-    rows = mine.shape[0]
     return pl.pallas_call(
         gram_kernel,
         out_shape=(
             jax.ShapeDtypeStruct((16, GRAM_ROWS, NB), f32),
             jax.ShapeDtypeStruct((16, 2, 8, FEAT), f32),
         ),
-        in_specs=[SMEM, VMEM, VMEM],
-        out_specs=(VMEM, VMEM),
-        scratch_shapes=[pltpu.VMEM((2 * rows, FEAT), bf16)] * 2 + [pltpu.VMEM((16 * GRAM_ROWS, NB), f32)],
+        in_specs=[SMEM, VMEM, ANY],
+        out_specs=(VMEM, ANY),
+        scratch_shapes=[pltpu.VMEM((512, FEAT), bf16)] * 2
+        + [
+            pltpu.VMEM((16 * GRAM_ROWS, NB), f32),
+            pltpu.VMEM(mine.shape, f32),
+            pltpu.SemaphoreType.DMA((3,)),
+        ],
         compiler_params=params(),
     )(ids, mine, theirs)
 
 
-def final_kernel(ids_ref, table_ref, r_ref, o_ref):
-    high, low = halves(r_ref[...])
-    total = mm(table_ref[...], high) + mm(table_ref[...], low)
-    odd = (lax.broadcasted_iota(jnp.int32, total.shape, 0) >> 2) & 1
-    flip = (odd * ids_ref[0]) == 1
-    o_ref[...] = total * jnp.where(flip, -32.0, 32.0)
+def final_kernel(ids_ref, table_ref, r_ref, o_hbm, out, sems):
+    chunks, rows, cols = out.shape
+    odd = (lax.broadcasted_iota(jnp.int32, (rows, cols), 0) >> 2) & 1
+    factor = jnp.where((odd * ids_ref[0]) == 1, -32.0, 32.0)
+
+    def store(chunk):
+        target = o_hbm.at[:, cols * chunk : cols * chunk + cols]
+        return pltpu.make_async_copy(out.at[chunk], target, sems.at[chunk])
+
+    for chunk in range(chunks):
+        high, low = halves(r_ref[:, cols * chunk : cols * chunk + cols])
+        out[chunk] = (mm(table_ref[...], high) + mm(table_ref[...], low)) * factor
+        store(chunk).start()
+    for chunk in range(chunks):
+        store(chunk).wait()
 
 
 def final_mix(ids, received):
+    rows, features = received.shape
+    chunks = 4
     return pl.pallas_call(
         final_kernel,
         out_shape=jax.ShapeDtypeStruct(received.shape, f32),
         in_specs=[SMEM, VMEM, VMEM],
-        out_specs=VMEM,
+        out_specs=ANY,
+        scratch_shapes=[
+            pltpu.VMEM((chunks, rows, features // chunks), f32),
+            pltpu.SemaphoreType.DMA((chunks,)),
+        ],
         compiler_params=params(),
     )(ids, jnp.asarray(final_table()), received)
 
@@ -304,24 +332,28 @@
             w[after:, :] = cleared - update[after:, :]
 
 
-def factor_kernel(ids_ref, ridge_ref, own_ref, other_ref, o_ref, done_ref, a, w, upper, inverse, stack1, stack2):
+def factor_kernel(ids_ref, ridge_ref, own_ref, other_hbm, o_ref, done_ref, other_ref, sem, a, w, upper, inverse, stack1, stack2):
     core, position = ids_ref[0], ids_ref[1]
     done_ref[0], done_ref[1] = core, position
+    fetch = pltpu.make_async_copy(other_hbm, other_ref, sem)
+    fetch.start()
     eye = lax.broadcasted_iota(jnp.int32, (NB, NB), 0) == lax.broadcasted_iota(jnp.int32, (NB, NB), 1)
-    for which in range(2):
-
-        @pl.when(core == which)
-        def _():
-            for ref, strips in ((own_ref, STRIPS[which]), (other_ref, STRIPS[1 - which])):
-                slot = 0
-                for strip in strips:
-                    for block in range(strip, PANELS):
-                        piece = ref[NB * slot : NB * slot + NB, :]
-                        if block == strip:
-                            ridge = ridge_ref[0:1, NB * strip : NB * strip + NB]
-                            piece = piece + jnp.where(eye, ridge, 0.0)
-                        a[NB * strip : NB * strip + NB, NB * block : NB * block + NB] = piece
-                        slot += 1
+
+    def assemble(ref, strips):
+        slot = 0
+        for strip in strips:
+            for block in range(strip, PANELS):
+                piece = ref[NB * slot : NB * slot + NB, :]
+                if block == strip:
+                    piece = piece + jnp.where(eye, ridge_ref[0:1, NB * strip : NB * strip + NB], 0.0)
+                a[NB * strip : NB * strip + NB, NB * block : NB * block + NB] = piece
+                slot += 1
+
+    for ref, offset in ((own_ref, 0), (other_ref, 1)):
+        if offset:
+            fetch.wait()
+        for which in range(2):
+            pl.when(core == which)(lambda: assemble(ref, STRIPS[which ^ offset]))
 
     def body(panel, carry):
         at = pl.multiple_of(panel * NB, NB)
@@ -362,9 +394,10 @@
     return pl.pallas_call(
         factor_kernel,
         out_shape=(jax.ShapeDtypeStruct((8, FEAT), f32), jax.ShapeDtypeStruct((2,), jnp.int32)),
-        in_specs=[SMEM, VMEM, VMEM, VMEM],
+        in_specs=[SMEM, VMEM, VMEM, ANY],
         out_specs=(VMEM, SMEM),
-        scratch_shapes=[pltpu.VMEM((FEAT, FEAT), f32)] + [pltpu.VMEM((NB, NB), f32)] * 3
+        scratch_shapes=[pltpu.VMEM(other.shape, f32), pltpu.SemaphoreType.DMA(())]
+        + [pltpu.VMEM((FEAT, FEAT), f32)] + [pltpu.VMEM((NB, NB), f32)] * 3
         + [pltpu.VMEM((6 * NB, FEAT), bf16)] * 2,
         compiler_params=params(),
         cost_estimate=pl.CostEstimate(flops=40_000_000_000, bytes_accessed=2 << 20, transcendentals=0),
@@ -392,7 +425,7 @@
     along = lax.all_to_all(
         mixed.reshape(4, 128, FEAT), "inner", 0, 0, axis_index_groups=Z_GROUPS, tiled=True
     )
-    mine = select_rows(keep_rows, along).reshape(256, FEAT)
+    mine = select_rows(keep_rows, along).reshape(2, 16, 8, FEAT)
     theirs = swap_cores(mine)
     gram, to_send = gram_half(ids, mine, theirs)
     piece = jnp.sum(plane_exchange(gram), axis=0)

time: 135 us -> 134 us (level)
  no operation moved by 1% of the time
where the time goes in v9:
time: 134 us
  blocking collectives  43.1 us (32%)
  Pallas kernels  39.9 us (30%)
  waiting for transfers between devices  31.9 us (24%)
  starting transfers between devices  17.6 us (13%)
    all_to_all x2, blocking collectives, plane_exchange(): lax.all_to_all(x, 'inner', 0, 0, axis_index_groups=PLANES, tiled=True)  43.1 us
    pallas_call x1, Pallas kernels, factor_rows(): pl.pallas_call(factor_kernel, out_shape=(jax.ShapeDtypeStruct((8, FEAT),...  29.8 us
    all_to_all x1, waiting for transfers between devices, local(): lax.all_to_all(mixed.reshape(4, 128, FEAT), 'inner', 0, 0, axis_index_gro...  25.2 us
    ppermute x2, starting transfers between devices, swap_cores(): return lax.ppermute(x, 'outer', [(0, 1), (1, 0)])  5.87 us
    all_to_all x1, starting transfers between devices, local(): lax.all_to_all(mixed.reshape(4, 128, FEAT), 'inner', 0, 0, axis_index_gro...  5.87 us
    pallas_call x1, Pallas kernels, local_mix(): pl.pallas_call(local_mix_kernel, out_shape=jax.ShapeDtypeStruct((rows, fe...  4.94 us
    ppermute x3, waiting for transfers between devices, along_z(): lax.ppermute(x, 'inner', [(i, (i + 16 * distance) % 64) for i in range(64)])  4.42 us
    all_to_all x1, starting transfers between devices, plane_exchange(): lax.all_to_all(x, 'inner', 0, 0, axis_index_groups=PLANES, tiled=True)  3.66 us
  transfers between devices with their start and end apart: 7, of which 5 were waited for; matrix products, arithmetic and copies ran while one was open for 0% of the time, Pallas kernels for 22%

profile of v9, /device:TPU:1, one launch (start us, length us, event | category | flops | bytes accessed | tf_op | source)
XLA Modules:
  0.0 133.8 jit_solution(3677729178165886108)
XLA Ops:
  0.6 4.9 %shard_map.77 = f32[512,1024]{1,0:T(8,128)} custom-call(bf16[512,512]{1,0:T(8,128)(2,1)} %constant.37.clone.table_hbm, s32[1,512]{1,0:T(1,128)} %bitcast.23, f32[512,1024]{1,0:T(8,128)} %x_hbm.1), custom_call_target="tpu_custom_call" | custom-call | tf_op jit(solution)/shard_map/pallas_call | solution.py:99
  5.6 5.9 %all-to-all-start = ((f32[4,128,1024]{2,1,0:T(8,128)}), f32[4,128,1024]{2,1,0:T(8,128)S(1)}, u32[]{:S(2)}, u32[]{:S(2)}) async-start(f32[4,128,1024]{2,1,0:T(8,128)} %bitcast.20), calls=%async_computation | async-start | bytes 4194304 | tf_op jit(solution)/shard_map/all_to_all | solution.py:425
  11.5 0.1 reshape.34
  11.6 0.1 copy.10
  11.7 25.2 %all-to-all-done.y_ref = f32[4,128,1024]{2,1,0:T(8,128)S(1)} async-done(((f32[4,128,1024]{2,1,0:T(8,128)}), f32[4,128,1024]{2,1,0:T(8,128)S(1)}, u32[]{:S(2)}, u32[]{:S(2)}) %all-to-all-start) | async-done | bytes 2097184 | tf_op jit(solution)/shard_map/all_to_all | solution.py:425
  36.9 0.9 shard_map.78
  37.8 1.9 %collective-permute-start = (f32[2,16,8,1024]{3,2,1,0:T(8,128)S(1)}, f32[2,16,8,1024]{3,2,1,0:T(8,128)S(1)}, u32[]{:S(2)}, u32[]{:S(2)}) collective-permute-start(f32[2,16,8,1024]{3,2,1,0:T(8,128)S(1)} %bitcast.13), channel_id=1, source_target_pairs={{0,64},{64,0},{1,65},{65,1},{2,66},{66,2},{3,67},{67,3},{4,68},{68... | collective-permute-start | bytes 3145736 | tf_op jit(solution)/shard_map/ppermute | solution.py:408
  39.8 0.1 pad_add_fusion.ids_ref
  39.9 2.2 %collective-permute-done.w_hbm = f32[2,16,8,1024]{3,2,1,0:T(8,128)S(1)} collective-permute-done((f32[2,16,8,1024]{3,2,1,0:T(8,128)S(1)}, f32[2,16,8,1024]{3,2,1,0:T(8,128)S(1)}, u32[]{:S(2)}, u32[]{:S(2)}) %collective-permute-start) | collective-permute-done | bytes 1048608 | tf_op jit(solution)/shard_map/ppermute | solution.py:408
  42.1 2.3 %shard_map.79 = (f32[16,144,128]{2,1,0:T(8,128)S(1)}, f32[16,2,8,1024]{3,2,1,0:T(8,128)}) custom-call(s32[2]{0:T(128)S(1)} %pad_add_fusion.ids_ref, f32[2,16,8,1024]{3,2,1,0:T(8,128)S(1)} %bitcast.14, f32[2,16,8,1024]{3,2,1,0:T(8,128)S(1)} %collective-permute-done.w_hbm), custom_call_target="tpu_custom_call" | custom-call | tf_op jit(solution)/shard_map/pallas_call | solution.py:186
  44.4 24.6 %all_to_all.20 = f32[16,144,128]{2,1,0:T(8,128)S(1)} all-to-all(f32[16,144,128]{2,1,0:T(8,128)S(1)} %get-tuple-element.9), channel_id=1, replica_groups={{0,1,2,3,4,5,6,7,8,9,10,11,12,13,14,15},{16,17,18,19,20,21,22,23,24,25,..., dimensions={0} | all-to-all | bytes 2359296 | tf_op jit(solution)/shard_map/all_to_all | solution.py:416
  69.0 0.1 reduce_sum.9
  69.0 1.0 collective-permute-start.3
  70.0 0.6 collective-permute-start.2
  70.6 0.7 collective-permute-start.1
  71.3 1.0 collective-permute-done.3
  72.3 2.1 %collective-permute-done.2 = f32[144,128]{1,0:T(8,128)S(1)} collective-permute-done((f32[144,128]{1,0:T(8,128)S(1)}, f32[144,128]{1,0:T(8,128)S(1)}, u32[]{:S(2)}, u32[]{:S(2)}) %collective-permute-start.2) | collective-permute-done | bytes 73760 | tf_op jit(solution)/shard_map/ppermute | solution.py:412
  74.4 1.3 collective-permute-done.1
  75.7 0.1 broadcast_in_dim.10
  75.8 18.5 %all_to_all.21 = f32[16,144,128]{2,1,0:T(8,128)S(1)} all-to-all(f32[16,144,128]{2,1,0:T(8,128)S(1)} %broadcast_in_dim.10), channel_id=1, replica_groups={{0,1,2,3,4,5,6,7,8,9,10,11,12,13,14,15},{16,17,18,19,20,21,22,23,24,25,..., dimensions={0} | all-to-all | bytes 2359296 | tf_op jit(solution)/shard_map/all_to_all | solution.py:416
  94.3 3.9 %collective-permute-start.4 = (f32[2304,128]{1,0:T(8,128)S(1)}, f32[2304,128]{1,0:T(8,128)}, u32[]{:S(2)}, u32[]{:S(2)}) collective-permute-start(f32[2304,128]{1,0:T(8,128)S(1)} %bitcast.16), channel_id=1, source_target_pairs={{0,64},{64,0},{1,65},{65,1},{2,66},{66,2},{3,67},{67,3},{4,68},{68... | collective-permute-start | bytes 3538952 | tf_op jit(solution)/shard_map/ppermute | solution.py:408
  98.2 3.7 %all-to-all-start.3 = ((f32[16,2,8,1024]{3,2,1,0:T(8,128)}), f32[16,2,8,1024]{3,2,1,0:T(8,128)S(1)}, u32[]{:S(2)}, u32[]{:S(2)}) async-start(f32[16,2,8,1024]{3,2,1,0:T(8,128)} %get-tuple-element.12), calls=%async_computation.3 | async-start | bytes 2097152 | tf_op jit(solution)/shard_map/all_to_all | solution.py:416
  101.9 29.8 %shard_map.80 = (f32[8,1024]{1,0:T(8,128)}, s32[2]{0:T(128)S(1)}) custom-call(s32[2]{0:T(128)S(1)} %pad_add_fusion.ids_ref, f32[1,1024]{1,0:T(1,128)S(1)} %bitcast.19, f32[2304,128]{1,0:T(8,128)S(1)} %bitcast.17, f32[2304,128]{1,0:T(8,128)} %collective-permute-done.4.other_hbm), custom_call_target="tpu_custom_call" | custom-call | flops 40000000000 | bytes 2097152 | tf_op jit(solution)/shard_map/pallas_call | solution.py:394
  131.8 1.9 %shard_map.81 = f32[256,1024]{1,0:T(8,128)} custom-call(s32[2]{0:T(128)S(1)} %get-tuple-element.11.ids_ref, bf16[256,256]{1,0:T(8,128)(2,1)S(1)} %copy-done, f32[256,1024]{1,0:T(8,128)S(1)} %bitcast.15), custom_call_target="tpu_custom_call" | custom-call | tf_op jit(solution)/shard_map/pallas_call | solution.py:224
  (11 shorter events, 0.1 us)
Async XLA Ops:
  5.6 5.9 %copy-start.2 = (s32[128,2]{0,1:T(2,128)S(1)}, s32[128,2]{0,1:T(2,128)}, u32[]{:S(2)}) copy-start(s32[128,2]{0,1:T(2,128)} %param.8) | copy-start | bytes 3076
  5.6 31.3 %all-to-all-start = ((f32[4,128,1024]{2,1,0:T(8,128)}), f32[4,128,1024]{2,1,0:T(8,128)S(1)}, u32[]{:S(2)}, u32[]{:S(2)}) async-start(f32[4,128,1024]{2,1,0:T(8,128)} %bitcast.20), calls=%async_computation | async-start | bytes 4194304 | tf_op jit(solution)/shard_map/all_to_all | solution.py:425
  37.8 4.2 %collective-permute-start = (f32[2,16,8,1024]{3,2,1,0:T(8,128)S(1)}, f32[2,16,8,1024]{3,2,1,0:T(8,128)S(1)}, u32[]{:S(2)}, u32[]{:S(2)}) collective-permute-start(f32[2,16,8,1024]{3,2,1,0:T(8,128)S(1)} %bitcast.13), channel_id=1, source_target_pairs={{0,64},{64,0},{1,65},{65,1},{2,66},{66,2},{3,67},{67,3},{4,68},{68... | collective-permute-start | bytes 3145736 | tf_op jit(solution)/shard_map/ppermute | solution.py:408
  69.0 3.3 %collective-permute-start.3 = (f32[144,128]{1,0:T(8,128)S(1)}, f32[144,128]{1,0:T(8,128)S(1)}, u32[]{:S(2)}, u32[]{:S(2)}) collective-permute-start(f32[144,128]{1,0:T(8,128)S(1)} %reduce_sum.9), channel_id=1, source_target_pairs={{0,48},{1,49},{2,50},{3,51},{4,52},{5,53},{6,54},{7,55},{8,56},{9,... | collective-permute-start | bytes 221192 | tf_op jit(solution)/shard_map/ppermute | solution.py:412
  70.0 4.4 %collective-permute-start.2 = (f32[144,128]{1,0:T(8,128)S(1)}, f32[144,128]{1,0:T(8,128)S(1)}, u32[]{:S(2)}, u32[]{:S(2)}) collective-permute-start(f32[144,128]{1,0:T(8,128)S(1)} %reduce_sum.9), channel_id=1, source_target_pairs={{0,16},{1,17},{2,18},{3,19},{4,20},{5,21},{6,22},{7,23},{8,24},{9,... | collective-permute-start | bytes 221192 | tf_op jit(solution)/shard_map/ppermute | solution.py:412
  70.6 5.1 %collective-permute-start.1 = (f32[144,128]{1,0:T(8,128)S(1)}, f32[144,128]{1,0:T(8,128)S(1)}, u32[]{:S(2)}, u32[]{:S(2)}) collective-permute-start(f32[144,128]{1,0:T(8,128)S(1)} %reduce_sum.9), channel_id=1, source_target_pairs={{0,32},{1,33},{2,34},{3,35},{4,36},{5,37},{6,38},{7,39},{8,40},{9,... | collective-permute-start | bytes 221192 | tf_op jit(solution)/shard_map/ppermute | solution.py:412
  94.3 7.6 %copy-start.1 = (f32[1024]{0:T(1024)S(1)}, f32[1024]{0:T(1024)}, u32[]{:S(2)}) copy-start(f32[1024]{0:T(1024)} %param.9) | copy-start | bytes 12292
  94.3 7.6 %collective-permute-start.4 = (f32[2304,128]{1,0:T(8,128)S(1)}, f32[2304,128]{1,0:T(8,128)}, u32[]{:S(2)}, u32[]{:S(2)}) collective-permute-start(f32[2304,128]{1,0:T(8,128)S(1)} %bitcast.16), channel_id=1, source_target_pairs={{0,64},{64,0},{1,65},{65,1},{2,66},{66,2},{3,67},{67,3},{4,68},{68... | collective-permute-start | bytes 3538952 | tf_op jit(solution)/shard_map/ppermute | solution.py:408
  98.2 33.6 %all-to-all-start.3 = ((f32[16,2,8,1024]{3,2,1,0:T(8,128)}), f32[16,2,8,1024]{3,2,1,0:T(8,128)S(1)}, u32[]{:S(2)}, u32[]{:S(2)}) async-start(f32[16,2,8,1024]{3,2,1,0:T(8,128)} %get-tuple-element.12), calls=%async_computation.3 | async-start | bytes 2097152 | tf_op jit(solution)/shard_map/all_to_all | solution.py:416
  101.9 29.9 %copy-start = (bf16[256,256]{1,0:T(8,128)(2,1)S(1)}, bf16[256,256]{1,0:T(8,128)(2,1)}, u32[]{:S(2)}) copy-start(bf16[256,256]{1,0:T(8,128)(2,1)} %constant.38.clone.table_ref) | copy-start | bytes 393220

commit v10 on v9

--- a/solution.py
+++ b/solution.py
@@ -62,16 +62,15 @@
 
 
 def local_mix_kernel(table_hbm, sign_hbm, x_hbm, o_hbm, table, sign, signed, x, out, sems):
-    chunks, _, cols = x.shape
-
-    def columns(ref, chunk):
-        return ref.at[:, cols * chunk : cols * chunk + cols]
+    chunks, _, cols = out.shape
 
     def load(chunk):
-        return pltpu.make_async_copy(columns(x_hbm, chunk), x.at[chunk], sems.at[chunk])
+        part = pl.ds(128 * chunk, 128)
+        return pltpu.make_async_copy(x_hbm.at[part], x.at[part], sems.at[chunk])
 
     def store(chunk):
-        return pltpu.make_async_copy(out.at[chunk], columns(o_hbm, chunk), sems.at[chunks + chunk])
+        target = o_hbm.at[:, cols * chunk : cols * chunk + cols]
+        return pltpu.make_async_copy(out.at[chunk], target, sems.at[chunks + chunk])
 
     get_table = pltpu.make_async_copy(table_hbm, table, sems.at[2 * chunks])
     get_sign = pltpu.make_async_copy(sign_hbm, sign, sems.at[2 * chunks + 1])
@@ -84,7 +83,8 @@
     signed[...] = (table[...].astype(f32) * (sign[...].astype(f32) * 2.0**-13)).astype(bf16)
     for chunk in range(chunks):
         load(chunk).wait()
-        high, low = halves(x[chunk])
+    for chunk in range(chunks):
+        high, low = halves(x[:, cols * chunk : cols * chunk + cols])
         out[chunk] = mm(signed[...], high) + mm(signed[...], low)
         store(chunk).start()
     for chunk in range(chunks):
@@ -105,7 +105,7 @@
             pltpu.VMEM((rows, rows), bf16),
             pltpu.VMEM((1, rows), jnp.int32),
             pltpu.VMEM((rows, rows), bf16),
-            block,
+            pltpu.VMEM((rows, features), f32),
             block,
             pltpu.SemaphoreType.DMA((2 * chunks + 2,)),
         ],
@@ -249,11 +249,10 @@
     return tuple(part.astype(bf16) for part in thirds(x))
 
 
-def outer_sum(left, right):
-    lh, lm, ll = thirds(left)
-    rh, rm, rl = thirds(right)
-    stacked_left = jnp.concatenate([lh, lh, lh, lm, lm, ll], axis=0).astype(bf16)
-    stacked_right = jnp.concatenate([rh, rm, rl, rh, rm, rh], axis=0).astype(bf16)
+def square_sum(x):
+    parts = thirds(x)
+    stacked_left = jnp.concatenate([parts[k] for k in LEFT], axis=0).astype(bf16)
+    stacked_right = jnp.concatenate([parts[k] for k in RIGHT], axis=0).astype(bf16)
     return tmm(stacked_left, stacked_right)
 
 
@@ -304,7 +303,6 @@
             if b < 7:
                 for a in range(b + 1, 8):
                     e[a] = e[a] - multiplier * c[a]
-                rows = rows - multiplier * (row_splat(rows, b) * r)
                 aug = aug - multiplier * scaled
             for group in near:
                 column = columns[group]
@@ -312,13 +310,16 @@
                 for a in range(b + 1, 8):
                     column[a] = column[a] - multipliers[group][b] * c[a]
         scale = by_row(sub, scales)
-        left, right = rows * scale, aug * scale
+        right = aug * scale
+        left = right
+        for a in range(8):
+            left = jnp.where(lane == base + a, e[a] * scale, left)
         upper[base : base + 8, :] = jnp.where(lane >= base + sub, left, 0.0)
         inverse[base : base + 8, :] = jnp.where(lane <= base + sub, right, 0.0)
         if not near:
             break
         if last < groups - 1:
-            update = outer_sum(left, right)
+            update = square_sum(right)
         m = multipliers[step + 1]
         e = [start[a] - tree_sum([m[b] * row_splat(m[b], a) for b in range(8)]) for a in range(8)]
         for group in near:

time: 134 us -> 133 us (level)
  no operation moved by 1% of the time
where the time goes in v10:
time: 133 us
  blocking collectives  43.1 us (32%)
  Pallas kernels  39 us (29%)
  waiting for transfers between devices  31.9 us (24%)
  starting transfers between devices  17.6 us (13%)
    all_to_all x2, blocking collectives, plane_exchange(): lax.all_to_all(x, 'inner', 0, 0, axis_index_groups=PLANES, tiled=True)  43.1 us
    pallas_call x1, Pallas kernels, factor_rows(): pl.pallas_call(factor_kernel, out_shape=(jax.ShapeDtypeStruct((8, FEAT),...  29.8 us
    all_to_all x1, waiting for transfers between devices, local(): lax.all_to_all(mixed.reshape(4, 128, FEAT), 'inner', 0, 0, axis_index_gro...  25.2 us
    ppermute x2, starting transfers between devices, swap_cores(): return lax.ppermute(x, 'outer', [(0, 1), (1, 0)])  5.87 us
    all_to_all x1, starting transfers between devices, local(): lax.all_to_all(mixed.reshape(4, 128, FEAT), 'inner', 0, 0, axis_index_gro...  5.87 us
    ppermute x3, waiting for transfers between devices, along_z(): lax.ppermute(x, 'inner', [(i, (i + 16 * distance) % 64) for i in range(64)])  4.43 us
    pallas_call x1, Pallas kernels, local_mix(): pl.pallas_call(local_mix_kernel, out_shape=jax.ShapeDtypeStruct((rows, fe...  4.12 us
    all_to_all x1, starting transfers between devices, plane_exchange(): lax.all_to_all(x, 'inner', 0, 0, axis_index_groups=PLANES, tiled=True)  3.66 us
  transfers between devices with their start and end apart: 7, of which 5 were waited for; matrix products, arithmetic and copies ran while one was open for 0% of the time, Pallas kernels for 22%

profile of v10, /device:TPU:1, one launch (start us, length us, event | category | flops | bytes accessed | tf_op | source)
XLA Modules:
  0.0 132.9 jit_solution(6780963791050682590)
XLA Ops:
  0.6 4.1 %shard_map.77 = f32[512,1024]{1,0:T(8,128)} custom-call(bf16[512,512]{1,0:T(8,128)(2,1)} %constant.37.clone.table_hbm, s32[1,512]{1,0:T(1,128)} %bitcast.23, f32[512,1024]{1,0:T(8,128)} %x_hbm.1), custom_call_target="tpu_custom_call" | custom-call | tf_op jit(solution)/shard_map/pallas_call | solution.py:99
  4.8 5.9 %all-to-all-start = ((f32[4,128,1024]{2,1,0:T(8,128)}), f32[4,128,1024]{2,1,0:T(8,128)S(1)}, u32[]{:S(2)}, u32[]{:S(2)}) async-start(f32[4,128,1024]{2,1,0:T(8,128)} %bitcast.20), calls=%async_computation | async-start | bytes 4194304 | tf_op jit(solution)/shard_map/all_to_all | solution.py:426
  10.6 0.1 reshape.34
  10.7 0.1 copy.10
  10.8 25.2 %all-to-all-done.y_ref = f32[4,128,1024]{2,1,0:T(8,128)S(1)} async-done(((f32[4,128,1024]{2,1,0:T(8,128)}), f32[4,128,1024]{2,1,0:T(8,128)S(1)}, u32[]{:S(2)}, u32[]{:S(2)}) %all-to-all-start) | async-done | bytes 2097184 | tf_op jit(solution)/shard_map/all_to_all | solution.py:426
  36.1 0.9 shard_map.78
  37.0 1.9 %collective-permute-start = (f32[2,16,8,1024]{3,2,1,0:T(8,128)S(1)}, f32[2,16,8,1024]{3,2,1,0:T(8,128)S(1)}, u32[]{:S(2)}, u32[]{:S(2)}) collective-permute-start(f32[2,16,8,1024]{3,2,1,0:T(8,128)S(1)} %bitcast.13), channel_id=1, source_target_pairs={{0,64},{64,0},{1,65},{65,1},{2,66},{66,2},{3,67},{67,3},{4,68},{68... | collective-permute-start | bytes 3145736 | tf_op jit(solution)/shard_map/ppermute | solution.py:409
  39.0 0.1 pad_add_fusion.ids_ref
  39.0 2.2 %collective-permute-done.w_hbm = f32[2,16,8,1024]{3,2,1,0:T(8,128)S(1)} collective-permute-done((f32[2,16,8,1024]{3,2,1,0:T(8,128)S(1)}, f32[2,16,8,1024]{3,2,1,0:T(8,128)S(1)}, u32[]{:S(2)}, u32[]{:S(2)}) %collective-permute-start) | collective-permute-done | bytes 1048608 | tf_op jit(solution)/shard_map/ppermute | solution.py:409
  41.2 2.3 %shard_map.79 = (f32[16,144,128]{2,1,0:T(8,128)S(1)}, f32[16,2,8,1024]{3,2,1,0:T(8,128)}) custom-call(s32[2]{0:T(128)S(1)} %pad_add_fusion.ids_ref, f32[2,16,8,1024]{3,2,1,0:T(8,128)S(1)} %bitcast.14, f32[2,16,8,1024]{3,2,1,0:T(8,128)S(1)} %collective-permute-done.w_hbm), custom_call_target="tpu_custom_call" | custom-call | tf_op jit(solution)/shard_map/pallas_call | solution.py:186
  43.5 24.6 %all_to_all.20 = f32[16,144,128]{2,1,0:T(8,128)S(1)} all-to-all(f32[16,144,128]{2,1,0:T(8,128)S(1)} %get-tuple-element.9), channel_id=1, replica_groups={{0,1,2,3,4,5,6,7,8,9,10,11,12,13,14,15},{16,17,18,19,20,21,22,23,24,25,..., dimensions={0} | all-to-all | bytes 2359296 | tf_op jit(solution)/shard_map/all_to_all | solution.py:417
  68.2 0.1 reduce_sum.9
  68.2 1.0 collective-permute-start.3
  69.2 0.6 collective-permute-start.2
  69.8 0.7 collective-permute-start.1
  70.4 1.1 collective-permute-done.3
  71.5 2.1 %collective-permute-done.2 = f32[144,128]{1,0:T(8,128)S(1)} collective-permute-done((f32[144,128]{1,0:T(8,128)S(1)}, f32[144,128]{1,0:T(8,128)S(1)}, u32[]{:S(2)}, u32[]{:S(2)}) %collective-permute-start.2) | collective-permute-done | bytes 73760 | tf_op jit(solution)/shard_map/ppermute | solution.py:413
  73.6 1.3 collective-permute-done.1
  74.9 0.1 broadcast_in_dim.10
  75.0 18.5 %all_to_all.21 = f32[16,144,128]{2,1,0:T(8,128)S(1)} all-to-all(f32[16,144,128]{2,1,0:T(8,128)S(1)} %broadcast_in_dim.10), channel_id=1, replica_groups={{0,1,2,3,4,5,6,7,8,9,10,11,12,13,14,15},{16,17,18,19,20,21,22,23,24,25,..., dimensions={0} | all-to-all | bytes 2359296 | tf_op jit(solution)/shard_map/all_to_all | solution.py:417
  93.5 3.9 %collective-permute-start.4 = (f32[2304,128]{1,0:T(8,128)S(1)}, f32[2304,128]{1,0:T(8,128)}, u32[]{:S(2)}, u32[]{:S(2)}) collective-permute-start(f32[2304,128]{1,0:T(8,128)S(1)} %bitcast.16), channel_id=1, source_target_pairs={{0,64},{64,0},{1,65},{65,1},{2,66},{66,2},{3,67},{67,3},{4,68},{68... | collective-permute-start | bytes 3538952 | tf_op jit(solution)/shard_map/ppermute | solution.py:409
  97.4 3.7 %all-to-all-start.3 = ((f32[16,2,8,1024]{3,2,1,0:T(8,128)}), f32[16,2,8,1024]{3,2,1,0:T(8,128)S(1)}, u32[]{:S(2)}, u32[]{:S(2)}) async-start(f32[16,2,8,1024]{3,2,1,0:T(8,128)} %get-tuple-element.12), calls=%async_computation.3 | async-start | bytes 2097152 | tf_op jit(solution)/shard_map/all_to_all | solution.py:417
  101.1 29.8 %shard_map.80 = (f32[8,1024]{1,0:T(8,128)}, s32[2]{0:T(128)S(1)}) custom-call(s32[2]{0:T(128)S(1)} %pad_add_fusion.ids_ref, f32[1,1024]{1,0:T(1,128)S(1)} %bitcast.19, f32[2304,128]{1,0:T(8,128)S(1)} %bitcast.17, f32[2304,128]{1,0:T(8,128)} %collective-permute-done.4.other_hbm), custom_call_target="tpu_custom_call" | custom-call | flops 40000000000 | bytes 2097152 | tf_op jit(solution)/shard_map/pallas_call | solution.py:395
  130.9 1.9 %shard_map.81 = f32[256,1024]{1,0:T(8,128)} custom-call(s32[2]{0:T(128)S(1)} %get-tuple-element.11.ids_ref, bf16[256,256]{1,0:T(8,128)(2,1)S(1)} %copy-done, f32[256,1024]{1,0:T(8,128)S(1)} %bitcast.15), custom_call_target="tpu_custom_call" | custom-call | tf_op jit(solution)/shard_map/pallas_call | solution.py:224
  (11 shorter events, 0.1 us)
Async XLA Ops:
  4.8 5.9 %copy-start.2 = (s32[128,2]{0,1:T(2,128)S(1)}, s32[128,2]{0,1:T(2,128)}, u32[]{:S(2)}) copy-start(s32[128,2]{0,1:T(2,128)} %param.8) | copy-start | bytes 3076
  4.8 31.3 %all-to-all-start = ((f32[4,128,1024]{2,1,0:T(8,128)}), f32[4,128,1024]{2,1,0:T(8,128)S(1)}, u32[]{:S(2)}, u32[]{:S(2)}) async-start(f32[4,128,1024]{2,1,0:T(8,128)} %bitcast.20), calls=%async_computation | async-start | bytes 4194304 | tf_op jit(solution)/shard_map/all_to_all | solution.py:426
  37.0 4.2 %collective-permute-start = (f32[2,16,8,1024]{3,2,1,0:T(8,128)S(1)}, f32[2,16,8,1024]{3,2,1,0:T(8,128)S(1)}, u32[]{:S(2)}, u32[]{:S(2)}) collective-permute-start(f32[2,16,8,1024]{3,2,1,0:T(8,128)S(1)} %bitcast.13), channel_id=1, source_target_pairs={{0,64},{64,0},{1,65},{65,1},{2,66},{66,2},{3,67},{67,3},{4,68},{68... | collective-permute-start | bytes 3145736 | tf_op jit(solution)/shard_map/ppermute | solution.py:409
  68.2 3.3 %collective-permute-start.3 = (f32[144,128]{1,0:T(8,128)S(1)}, f32[144,128]{1,0:T(8,128)S(1)}, u32[]{:S(2)}, u32[]{:S(2)}) collective-permute-start(f32[144,128]{1,0:T(8,128)S(1)} %reduce_sum.9), channel_id=1, source_target_pairs={{0,48},{1,49},{2,50},{3,51},{4,52},{5,53},{6,54},{7,55},{8,56},{9,... | collective-permute-start | bytes 221192 | tf_op jit(solution)/shard_map/ppermute | solution.py:413
  69.2 4.4 %collective-permute-start.2 = (f32[144,128]{1,0:T(8,128)S(1)}, f32[144,128]{1,0:T(8,128)S(1)}, u32[]{:S(2)}, u32[]{:S(2)}) collective-permute-start(f32[144,128]{1,0:T(8,128)S(1)} %reduce_sum.9), channel_id=1, source_target_pairs={{0,16},{1,17},{2,18},{3,19},{4,20},{5,21},{6,22},{7,23},{8,24},{9,... | collective-permute-start | bytes 221192 | tf_op jit(solution)/shard_map/ppermute | solution.py:413
  69.8 5.1 %collective-permute-start.1 = (f32[144,128]{1,0:T(8,128)S(1)}, f32[144,128]{1,0:T(8,128)S(1)}, u32[]{:S(2)}, u32[]{:S(2)}) collective-permute-start(f32[144,128]{1,0:T(8,128)S(1)} %reduce_sum.9), channel_id=1, source_target_pairs={{0,32},{1,33},{2,34},{3,35},{4,36},{5,37},{6,38},{7,39},{8,40},{9,... | collective-permute-start | bytes 221192 | tf_op jit(solution)/shard_map/ppermute | solution.py:413
  93.5 7.6 %copy-start.1 = (f32[1024]{0:T(1024)S(1)}, f32[1024]{0:T(1024)}, u32[]{:S(2)}) copy-start(f32[1024]{0:T(1024)} %param.9) | copy-start | bytes 12292
  93.5 7.6 %collective-permute-start.4 = (f32[2304,128]{1,0:T(8,128)S(1)}, f32[2304,128]{1,0:T(8,128)}, u32[]{:S(2)}, u32[]{:S(2)}) collective-permute-start(f32[2304,128]{1,0:T(8,128)S(1)} %bitcast.16), channel_id=1, source_target_pairs={{0,64},{64,0},{1,65},{65,1},{2,66},{66,2},{3,67},{67,3},{4,68},{68... | collective-permute-start | bytes 3538952 | tf_op jit(solution)/shard_map/ppermute | solution.py:409
  97.4 33.5 %all-to-all-start.3 = ((f32[16,2,8,1024]{3,2,1,0:T(8,128)}), f32[16,2,8,1024]{3,2,1,0:T(8,128)S(1)}, u32[]{:S(2)}, u32[]{:S(2)}) async-start(f32[16,2,8,1024]{3,2,1,0:T(8,128)} %get-tuple-element.12), calls=%async_computation.3 | async-start | bytes 2097152 | tf_op jit(solution)/shard_map/all_to_all | solution.py:417
  101.1 29.8 %copy-start = (bf16[256,256]{1,0:T(8,128)(2,1)S(1)}, bf16[256,256]{1,0:T(8,128)(2,1)}, u32[]{:S(2)}) copy-start(bf16[256,256]{1,0:T(8,128)(2,1)} %constant.38.clone.table_ref) | copy-start | bytes 393220

commit v11 on v10

--- a/solution.py
+++ b/solution.py
@@ -409,10 +409,6 @@
     return lax.ppermute(x, "outer", [(0, 1), (1, 0)])
 
 
-def along_z(x, distance):
-    return lax.ppermute(x, "inner", [(i, (i + 16 * distance) % 64) for i in range(64)])
-
-
 def plane_exchange(x):
     return lax.all_to_all(x, "inner", 0, 0, axis_index_groups=PLANES, tiled=True)
 
@@ -430,7 +426,9 @@
     theirs = swap_cores(mine)
     gram, to_send = gram_half(ids, mine, theirs)
     piece = jnp.sum(plane_exchange(gram), axis=0)
-    piece = (piece + along_z(piece, 2)) + (along_z(piece, 1) + along_z(piece, 3))
+    by_plane = jnp.broadcast_to(piece[None], (4, GRAM_ROWS, NB))
+    by_plane = lax.all_to_all(by_plane, "inner", 0, 0, axis_index_groups=Z_GROUPS, tiled=True)
+    piece = (by_plane[0] + by_plane[1]) + (by_plane[2] + by_plane[3])
     own = plane_exchange(jnp.broadcast_to(piece[None], (16, GRAM_ROWS, NB))).reshape(16 * GRAM_ROWS, NB)
     to_send, own = lax.optimization_barrier((to_send, own))
     received = plane_exchange(to_send)

time: 133 us -> 135 us (1.015)
  blocking collectives: 43.1 us -> 52 us
  waiting for transfers between devices: 31.9 us -> 27.4 us
  starting transfers between devices: 17.6 us -> 14.9 us
    all_to_all x0 -> x1, blocking collectives: none -> 8.07 us  [local(): lax.all_to_all(by_plane, 'inner', 0, 0, axis_index_groups=Z_GROUPS, tiled...]
    ppermute x3 -> x0, waiting for transfers between devices: 4.43 us -> none  [along_z(): lax.ppermute(x, 'inner', [(i, (i + 16 * distance) % 64) for i in range(64)])]
    ppermute x3 -> x0, starting transfers between devices: 2.22 us -> none  [along_z(): lax.ppermute(x, 'inner', [(i, (i + 16 * distance) % 64) for i in range(64)])]
  transfers between devices with their start and end apart: 7 -> 4, of which waited for: 5 -> 2; matrix products, arithmetic and copies ran while one was open for 0% -> 0% of each run, Pallas kernels for 22% -> 22%
where the time goes in v11:
time: 135 us
  blocking collectives  52 us (39%)
  Pallas kernels  39 us (29%)
  waiting for transfers between devices  27.4 us (20%)
  starting transfers between devices  14.9 us (11%)
    all_to_all x2, blocking collectives, plane_exchange(): lax.all_to_all(x, 'inner', 0, 0, axis_index_groups=PLANES, tiled=True)  43.9 us
    pallas_call x1, Pallas kernels, factor_rows(): pl.pallas_call(factor_kernel, out_shape=(jax.ShapeDtypeStruct((8, FEAT),...  29.8 us
    all_to_all x1, waiting for transfers between devices, local(): lax.all_to_all(mixed.reshape(4, 128, FEAT), 'inner', 0, 0, axis_index_gro...  25.2 us
    all_to_all x1, blocking collectives, local(): lax.all_to_all(by_plane, 'inner', 0, 0, axis_index_groups=Z_GROUPS, tiled...  8.07 us
    all_to_all x1, starting transfers between devices, local(): lax.all_to_all(mixed.reshape(4, 128, FEAT), 'inner', 0, 0, axis_index_gro...  5.87 us
    ppermute x2, starting transfers between devices, swap_cores(): return lax.ppermute(x, 'outer', [(0, 1), (1, 0)])  5.37 us
    pallas_call x1, Pallas kernels, local_mix(): pl.pallas_call(local_mix_kernel, out_shape=jax.ShapeDtypeStruct((rows, fe...  4.12 us
    all_to_all x1, starting transfers between devices, plane_exchange(): lax.all_to_all(x, 'inner', 0, 0, axis_index_groups=PLANES, tiled=True)  3.66 us
  transfers between devices with their start and end apart: 4, of which 2 were waited for; matrix products, arithmetic and copies ran while one was open for 0% of the time, Pallas kernels for 22%

profile of v11, /device:TPU:1, one launch (start us, length us, event | category | flops | bytes accessed | tf_op | source)
XLA Modules:
  0.0 134.7 jit_solution(6700471161061509931)
XLA Ops:
  0.6 4.1 %shard_map.77 = f32[512,1024]{1,0:T(8,128)} custom-call(bf16[512,512]{1,0:T(8,128)(2,1)} %constant.37.clone.table_hbm, s32[1,512]{1,0:T(1,128)} %bitcast.25, f32[512,1024]{1,0:T(8,128)} %x_hbm.1), custom_call_target="tpu_custom_call" | custom-call | tf_op jit(solution)/shard_map/pallas_call | solution.py:99
  4.8 0.0 copy-start.2
  4.8 5.9 %all-to-all-start = ((f32[4,128,1024]{2,1,0:T(8,128)}), f32[4,128,1024]{2,1,0:T(8,128)S(1)}, u32[]{:S(2)}, u32[]{:S(2)}) async-start(f32[4,128,1024]{2,1,0:T(8,128)} %bitcast.22), calls=%async_computation | async-start | bytes 4194304 | tf_op jit(solution)/shard_map/all_to_all | solution.py:422
  10.6 0.0 copy-done.2
  10.6 0.1 reshape.34
  10.7 0.1 copy.10
  10.8 25.2 %all-to-all-done.y_ref = f32[4,128,1024]{2,1,0:T(8,128)S(1)} async-done(((f32[4,128,1024]{2,1,0:T(8,128)}), f32[4,128,1024]{2,1,0:T(8,128)S(1)}, u32[]{:S(2)}, u32[]{:S(2)}) %all-to-all-start) | async-done | bytes 2097184 | tf_op jit(solution)/shard_map/all_to_all | solution.py:422
  36.1 0.9 shard_map.78
  37.0 1.9 %collective-permute-start = (f32[2,16,8,1024]{3,2,1,0:T(8,128)S(1)}, f32[2,16,8,1024]{3,2,1,0:T(8,128)S(1)}, u32[]{:S(2)}, u32[]{:S(2)}) collective-permute-start(f32[2,16,8,1024]{3,2,1,0:T(8,128)S(1)} %bitcast.15), channel_id=1, source_target_pairs={{0,64},{64,0},{1,65},{65,1},{2,66},{66,2},{3,67},{67,3},{4,68},{68... | collective-permute-start | bytes 3145736 | tf_op jit(solution)/shard_map/ppermute | solution.py:409
  39.0 0.1 pad_add_fusion.ids_ref
  39.0 2.2 %collective-permute-done.w_hbm = f32[2,16,8,1024]{3,2,1,0:T(8,128)S(1)} collective-permute-done((f32[2,16,8,1024]{3,2,1,0:T(8,128)S(1)}, f32[2,16,8,1024]{3,2,1,0:T(8,128)S(1)}, u32[]{:S(2)}, u32[]{:S(2)}) %collective-permute-start) | collective-permute-done | bytes 1048608 | tf_op jit(solution)/shard_map/ppermute | solution.py:409
  41.2 2.3 %shard_map.79 = (f32[16,144,128]{2,1,0:T(8,128)S(1)}, f32[16,2,8,1024]{3,2,1,0:T(8,128)}) custom-call(s32[2]{0:T(128)S(1)} %pad_add_fusion.ids_ref, f32[2,16,8,1024]{3,2,1,0:T(8,128)S(1)} %bitcast.16, f32[2,16,8,1024]{3,2,1,0:T(8,128)S(1)} %collective-permute-done.w_hbm), custom_call_target="tpu_custom_call" | custom-call | tf_op jit(solution)/shard_map/pallas_call | solution.py:186
  43.5 24.6 %all_to_all.25 = f32[16,144,128]{2,1,0:T(8,128)S(1)} all-to-all(f32[16,144,128]{2,1,0:T(8,128)S(1)} %get-tuple-element.9), channel_id=1, replica_groups={{0,1,2,3,4,5,6,7,8,9,10,11,12,13,14,15},{16,17,18,19,20,21,22,23,24,25,..., dimensions={0} | all-to-all | bytes 2359296 | tf_op jit(solution)/shard_map/all_to_all | solution.py:413
  68.2 0.1 reduce_sum.9
  68.3 8.1 %all_to_all.26 = f32[4,144,128]{2,1,0:T(8,128)S(1)} all-to-all(f32[4,144,128]{2,1,0:T(8,128)S(1)} %broadcast_in_dim.18), channel_id=1, replica_groups={{0,16,32,48},{1,17,33,49},{2,18,34,50},{3,19,35,51},{4,20,36,52},{5,21,..., dimensions={0} | all-to-all | bytes 589824 | tf_op jit(solution)/shard_map/all_to_all | solution.py:430
  76.3 0.1 broadcast_in_dim.20
  76.4 19.3 %all_to_all.27 = f32[16,144,128]{2,1,0:T(8,128)S(1)} all-to-all(f32[16,144,128]{2,1,0:T(8,128)S(1)} %broadcast_in_dim.20), channel_id=1, replica_groups={{0,1,2,3,4,5,6,7,8,9,10,11,12,13,14,15},{16,17,18,19,20,21,22,23,24,25,..., dimensions={0} | all-to-all | bytes 2359296 | tf_op jit(solution)/shard_map/all_to_all | solution.py:413
  95.7 3.4 %collective-permute-start.1 = (f32[2304,128]{1,0:T(8,128)S(1)}, f32[2304,128]{1,0:T(8,128)}, u32[]{:S(2)}, u32[]{:S(2)}) collective-permute-start(f32[2304,128]{1,0:T(8,128)S(1)} %bitcast.18), channel_id=1, source_target_pairs={{0,64},{64,0},{1,65},{65,1},{2,66},{66,2},{3,67},{67,3},{4,68},{68... | collective-permute-start | bytes 3538952 | tf_op jit(solution)/shard_map/ppermute | solution.py:409
  99.1 3.7 %all-to-all-start.4 = ((f32[16,2,8,1024]{3,2,1,0:T(8,128)}), f32[16,2,8,1024]{3,2,1,0:T(8,128)S(1)}, u32[]{:S(2)}, u32[]{:S(2)}) async-start(f32[16,2,8,1024]{3,2,1,0:T(8,128)} %get-tuple-element.12), calls=%async_computation.4 | async-start | bytes 2097152 | tf_op jit(solution)/shard_map/all_to_all | solution.py:413
  102.8 0.0 collective-permute-done.1.other_hbm
  102.8 0.0 copy-start
  102.8 29.8 %shard_map.80 = (f32[8,1024]{1,0:T(8,128)}, s32[2]{0:T(128)S(1)}) custom-call(s32[2]{0:T(128)S(1)} %pad_add_fusion.ids_ref, f32[1,1024]{1,0:T(1,128)S(1)} %bitcast.21, f32[2304,128]{1,0:T(8,128)S(1)} %bitcast.19, f32[2304,128]{1,0:T(8,128)} %collective-permute-done.1.other_hbm), custom_call_target="tpu_custom_call" | custom-call | flops 40000000000 | bytes 2097152 | tf_op jit(solution)/shard_map/pallas_call | solution.py:395
  132.6 0.0 all-to-all-done.4
  132.6 1.9 %shard_map.81 = f32[256,1024]{1,0:T(8,128)} custom-call(s32[2]{0:T(128)S(1)} %get-tuple-element.11.ids_ref, bf16[256,256]{1,0:T(8,128)(2,1)S(1)} %copy-done, f32[256,1024]{1,0:T(8,128)S(1)} %bitcast.17), custom_call_target="tpu_custom_call" | custom-call | tf_op jit(solution)/shard_map/pallas_call | solution.py:224
  (7 shorter events, 0.1 us)
Async XLA Ops:
  4.8 5.9 %copy-start.2 = (s32[128,2]{0,1:T(2,128)S(1)}, s32[128,2]{0,1:T(2,128)}, u32[]{:S(2)}) copy-start(s32[128,2]{0,1:T(2,128)} %param.8) | copy-start | bytes 3076
  4.8 31.3 %all-to-all-start = ((f32[4,128,1024]{2,1,0:T(8,128)}), f32[4,128,1024]{2,1,0:T(8,128)S(1)}, u32[]{:S(2)}, u32[]{:S(2)}) async-start(f32[4,128,1024]{2,1,0:T(8,128)} %bitcast.22), calls=%async_computation | async-start | bytes 4194304 | tf_op jit(solution)/shard_map/all_to_all | solution.py:422
  37.0 4.2 %collective-permute-start = (f32[2,16,8,1024]{3,2,1,0:T(8,128)S(1)}, f32[2,16,8,1024]{3,2,1,0:T(8,128)S(1)}, u32[]{:S(2)}, u32[]{:S(2)}) collective-permute-start(f32[2,16,8,1024]{3,2,1,0:T(8,128)S(1)} %bitcast.15), channel_id=1, source_target_pairs={{0,64},{64,0},{1,65},{65,1},{2,66},{66,2},{3,67},{67,3},{4,68},{68... | collective-permute-start | bytes 3145736 | tf_op jit(solution)/shard_map/ppermute | solution.py:409
  95.7 7.1 %copy-start.1 = (f32[1024]{0:T(1024)S(1)}, f32[1024]{0:T(1024)}, u32[]{:S(2)}) copy-start(f32[1024]{0:T(1024)} %param.9) | copy-start | bytes 12292
  95.7 7.1 %collective-permute-start.1 = (f32[2304,128]{1,0:T(8,128)S(1)}, f32[2304,128]{1,0:T(8,128)}, u32[]{:S(2)}, u32[]{:S(2)}) collective-permute-start(f32[2304,128]{1,0:T(8,128)S(1)} %bitcast.18), channel_id=1, source_target_pairs={{0,64},{64,0},{1,65},{65,1},{2,66},{66,2},{3,67},{67,3},{4,68},{68... | collective-permute-start | bytes 3538952 | tf_op jit(solution)/shard_map/ppermute | solution.py:409
  99.1 33.5 %all-to-all-start.4 = ((f32[16,2,8,1024]{3,2,1,0:T(8,128)}), f32[16,2,8,1024]{3,2,1,0:T(8,128)S(1)}, u32[]{:S(2)}, u32[]{:S(2)}) async-start(f32[16,2,8,1024]{3,2,1,0:T(8,128)} %get-tuple-element.12), calls=%async_computation.4 | async-start | bytes 2097152 | tf_op jit(solution)/shard_map/all_to_all | solution.py:413
  102.8 29.8 %copy-start = (bf16[256,256]{1,0:T(8,128)(2,1)S(1)}, bf16[256,256]{1,0:T(8,128)(2,1)}, u32[]{:S(2)}) copy-start(bf16[256,256]{1,0:T(8,128)(2,1)} %constant.38.clone.table_ref) | copy-start | bytes 393220

commit v12 on v10

--- a/solution.py
+++ b/solution.py
@@ -378,10 +378,14 @@
                     for k in range(6):
                         stack1[NB * k : NB * k + NB, :width] = parts[LEFT[k]]
                         stack2[NB * k : NB * k + NB, :width] = parts[RIGHT[k]]
-                    for strip in range(fixed + 1, PANELS):
-                        b0, t0 = NB * (strip - fixed - 1), NB * strip
-                        update = tmm(stack1[:, b0 : b0 + NB], stack2[:, b0:width])
-                        a[t0 : t0 + NB, t0:] = a[t0 : t0 + NB, t0:] - update
+                    for strip in range(fixed + 1, PANELS, 2):
+                        t0, high = NB * strip, min(NB * strip + 2 * NB, FEAT)
+                        b0 = t0 - s1
+                        update = tmm(stack1[:, b0 : high - s1], stack2[:, b0:width])
+                        a[t0 : t0 + NB, t0:] = a[t0 : t0 + NB, t0:] - update[:NB]
+                        if high - t0 > NB:
+                            t1 = t0 + NB
+                            a[t1:high, t1:] = a[t1:high, t1:] - update[NB:, NB:]
 
         return carry
 

time: 133 us -> 133 us (level)
  no operation moved by 1% of the time
where the time goes in v12:
time: 133 us
  blocking collectives  43.1 us (32%)
  Pallas kernels  39.1 us (29%)
  waiting for transfers between devices  31.9 us (24%)
  starting transfers between devices  17.6 us (13%)
    all_to_all x2, blocking collectives, plane_exchange(): lax.all_to_all(x, 'inner', 0, 0, axis_index_groups=PLANES, tiled=True)  43.1 us
    pallas_call x1, Pallas kernels, factor_rows(): pl.pallas_call(factor_kernel, out_shape=(jax.ShapeDtypeStruct((8, FEAT),...  29.9 us
    all_to_all x1, waiting for transfers between devices, local(): lax.all_to_all(mixed.reshape(4, 128, FEAT), 'inner', 0, 0, axis_index_gro...  25.2 us
    ppermute x2, starting transfers between devices, swap_cores(): return lax.ppermute(x, 'outer', [(0, 1), (1, 0)])  5.87 us
    all_to_all x1, starting transfers between devices, local(): lax.all_to_all(mixed.reshape(4, 128, FEAT), 'inner', 0, 0, axis_index_gro...  5.87 us
    ppermute x3, waiting for transfers between devices, along_z(): lax.ppermute(x, 'inner', [(i, (i + 16 * distance) % 64) for i in range(64)])  4.43 us
    pallas_call x1, Pallas kernels, local_mix(): pl.pallas_call(local_mix_kernel, out_shape=jax.ShapeDtypeStruct((rows, fe...  4.12 us
    all_to_all x1, starting transfers between devices, plane_exchange(): lax.all_to_all(x, 'inner', 0, 0, axis_index_groups=PLANES, tiled=True)  3.66 us
  transfers between devices with their start and end apart: 7, of which 5 were waited for; matrix products, arithmetic and copies ran while one was open for 0% of the time, Pallas kernels for 22%

profile of v12, /device:TPU:1, one launch (start us, length us, event | category | flops | bytes accessed | tf_op | source)
XLA Modules:
  0.0 133.0 jit_solution(8799832280154383955)
XLA Ops:
  0.6 4.1 %shard_map.77 = f32[512,1024]{1,0:T(8,128)} custom-call(bf16[512,512]{1,0:T(8,128)(2,1)} %constant.37.clone.table_hbm, s32[1,512]{1,0:T(1,128)} %bitcast.23, f32[512,1024]{1,0:T(8,128)} %x_hbm.1), custom_call_target="tpu_custom_call" | custom-call | tf_op jit(solution)/shard_map/pallas_call | solution.py:99
  4.8 5.9 %all-to-all-start = ((f32[4,128,1024]{2,1,0:T(8,128)}), f32[4,128,1024]{2,1,0:T(8,128)S(1)}, u32[]{:S(2)}, u32[]{:S(2)}) async-start(f32[4,128,1024]{2,1,0:T(8,128)} %bitcast.20), calls=%async_computation | async-start | bytes 4194304 | tf_op jit(solution)/shard_map/all_to_all | solution.py:430
  10.6 0.1 reshape.34
  10.7 0.1 copy.10
  10.8 25.2 %all-to-all-done.y_ref = f32[4,128,1024]{2,1,0:T(8,128)S(1)} async-done(((f32[4,128,1024]{2,1,0:T(8,128)}), f32[4,128,1024]{2,1,0:T(8,128)S(1)}, u32[]{:S(2)}, u32[]{:S(2)}) %all-to-all-start) | async-done | bytes 2097184 | tf_op jit(solution)/shard_map/all_to_all | solution.py:430
  36.1 0.9 shard_map.78
  37.0 1.9 %collective-permute-start = (f32[2,16,8,1024]{3,2,1,0:T(8,128)S(1)}, f32[2,16,8,1024]{3,2,1,0:T(8,128)S(1)}, u32[]{:S(2)}, u32[]{:S(2)}) collective-permute-start(f32[2,16,8,1024]{3,2,1,0:T(8,128)S(1)} %bitcast.13), channel_id=1, source_target_pairs={{0,64},{64,0},{1,65},{65,1},{2,66},{66,2},{3,67},{67,3},{4,68},{68... | collective-permute-start | bytes 3145736 | tf_op jit(solution)/shard_map/ppermute | solution.py:413
  39.0 0.1 pad_add_fusion.ids_ref
  39.0 2.2 %collective-permute-done.w_hbm = f32[2,16,8,1024]{3,2,1,0:T(8,128)S(1)} collective-permute-done((f32[2,16,8,1024]{3,2,1,0:T(8,128)S(1)}, f32[2,16,8,1024]{3,2,1,0:T(8,128)S(1)}, u32[]{:S(2)}, u32[]{:S(2)}) %collective-permute-start) | collective-permute-done | bytes 1048608 | tf_op jit(solution)/shard_map/ppermute | solution.py:413
  41.2 2.3 %shard_map.79 = (f32[16,144,128]{2,1,0:T(8,128)S(1)}, f32[16,2,8,1024]{3,2,1,0:T(8,128)}) custom-call(s32[2]{0:T(128)S(1)} %pad_add_fusion.ids_ref, f32[2,16,8,1024]{3,2,1,0:T(8,128)S(1)} %bitcast.14, f32[2,16,8,1024]{3,2,1,0:T(8,128)S(1)} %collective-permute-done.w_hbm), custom_call_target="tpu_custom_call" | custom-call | tf_op jit(solution)/shard_map/pallas_call | solution.py:186
  43.5 24.6 %all_to_all.20 = f32[16,144,128]{2,1,0:T(8,128)S(1)} all-to-all(f32[16,144,128]{2,1,0:T(8,128)S(1)} %get-tuple-element.9), channel_id=1, replica_groups={{0,1,2,3,4,5,6,7,8,9,10,11,12,13,14,15},{16,17,18,19,20,21,22,23,24,25,..., dimensions={0} | all-to-all | bytes 2359296 | tf_op jit(solution)/shard_map/all_to_all | solution.py:421
  68.2 0.1 reduce_sum.9
  68.2 1.0 collective-permute-start.3
  69.2 0.6 collective-permute-start.2
  69.8 0.7 collective-permute-start.1
  70.4 1.1 collective-permute-done.3
  71.5 2.1 %collective-permute-done.2 = f32[144,128]{1,0:T(8,128)S(1)} collective-permute-done((f32[144,128]{1,0:T(8,128)S(1)}, f32[144,128]{1,0:T(8,128)S(1)}, u32[]{:S(2)}, u32[]{:S(2)}) %collective-permute-start.2) | collective-permute-done | bytes 73760 | tf_op jit(solution)/shard_map/ppermute | solution.py:417
  73.6 1.3 collective-permute-done.1
  74.9 0.1 broadcast_in_dim.10
  75.0 18.5 %all_to_all.21 = f32[16,144,128]{2,1,0:T(8,128)S(1)} all-to-all(f32[16,144,128]{2,1,0:T(8,128)S(1)} %broadcast_in_dim.10), channel_id=1, replica_groups={{0,1,2,3,4,5,6,7,8,9,10,11,12,13,14,15},{16,17,18,19,20,21,22,23,24,25,..., dimensions={0} | all-to-all | bytes 2359296 | tf_op jit(solution)/shard_map/all_to_all | solution.py:421
  93.5 3.9 %collective-permute-start.4 = (f32[2304,128]{1,0:T(8,128)S(1)}, f32[2304,128]{1,0:T(8,128)}, u32[]{:S(2)}, u32[]{:S(2)}) collective-permute-start(f32[2304,128]{1,0:T(8,128)S(1)} %bitcast.16), channel_id=1, source_target_pairs={{0,64},{64,0},{1,65},{65,1},{2,66},{66,2},{3,67},{67,3},{4,68},{68... | collective-permute-start | bytes 3538952 | tf_op jit(solution)/shard_map/ppermute | solution.py:413
  97.4 3.7 %all-to-all-start.3 = ((f32[16,2,8,1024]{3,2,1,0:T(8,128)}), f32[16,2,8,1024]{3,2,1,0:T(8,128)S(1)}, u32[]{:S(2)}, u32[]{:S(2)}) async-start(f32[16,2,8,1024]{3,2,1,0:T(8,128)} %get-tuple-element.12), calls=%async_computation.3 | async-start | bytes 2097152 | tf_op jit(solution)/shard_map/all_to_all | solution.py:421
  101.1 29.9 %shard_map.80 = (f32[8,1024]{1,0:T(8,128)}, s32[2]{0:T(128)S(1)}) custom-call(s32[2]{0:T(128)S(1)} %pad_add_fusion.ids_ref, f32[1,1024]{1,0:T(1,128)S(1)} %bitcast.19, f32[2304,128]{1,0:T(8,128)S(1)} %bitcast.17, f32[2304,128]{1,0:T(8,128)} %collective-permute-done.4.other_hbm), custom_call_target="tpu_custom_call" | custom-call | flops 40000000000 | bytes 2097152 | tf_op jit(solution)/shard_map/pallas_call | solution.py:399
  131.0 1.9 %shard_map.81 = f32[256,1024]{1,0:T(8,128)} custom-call(s32[2]{0:T(128)S(1)} %get-tuple-element.11.ids_ref, bf16[256,256]{1,0:T(8,128)(2,1)S(1)} %copy-done, f32[256,1024]{1,0:T(8,128)S(1)} %bitcast.15), custom_call_target="tpu_custom_call" | custom-call | tf_op jit(solution)/shard_map/pallas_call | solution.py:224
  (11 shorter events, 0.1 us)
Async XLA Ops:
  4.8 5.9 %copy-start.2 = (s32[128,2]{0,1:T(2,128)S(1)}, s32[128,2]{0,1:T(2,128)}, u32[]{:S(2)}) copy-start(s32[128,2]{0,1:T(2,128)} %param.8) | copy-start | bytes 3076
  4.8 31.3 %all-to-all-start = ((f32[4,128,1024]{2,1,0:T(8,128)}), f32[4,128,1024]{2,1,0:T(8,128)S(1)}, u32[]{:S(2)}, u32[]{:S(2)}) async-start(f32[4,128,1024]{2,1,0:T(8,128)} %bitcast.20), calls=%async_computation | async-start | bytes 4194304 | tf_op jit(solution)/shard_map/all_to_all | solution.py:430
  37.0 4.2 %collective-permute-start = (f32[2,16,8,1024]{3,2,1,0:T(8,128)S(1)}, f32[2,16,8,1024]{3,2,1,0:T(8,128)S(1)}, u32[]{:S(2)}, u32[]{:S(2)}) collective-permute-start(f32[2,16,8,1024]{3,2,1,0:T(8,128)S(1)} %bitcast.13), channel_id=1, source_target_pairs={{0,64},{64,0},{1,65},{65,1},{2,66},{66,2},{3,67},{67,3},{4,68},{68... | collective-permute-start | bytes 3145736 | tf_op jit(solution)/shard_map/ppermute | solution.py:413
  68.2 3.3 %collective-permute-start.3 = (f32[144,128]{1,0:T(8,128)S(1)}, f32[144,128]{1,0:T(8,128)S(1)}, u32[]{:S(2)}, u32[]{:S(2)}) collective-permute-start(f32[144,128]{1,0:T(8,128)S(1)} %reduce_sum.9), channel_id=1, source_target_pairs={{0,48},{1,49},{2,50},{3,51},{4,52},{5,53},{6,54},{7,55},{8,56},{9,... | collective-permute-start | bytes 221192 | tf_op jit(solution)/shard_map/ppermute | solution.py:417
  69.2 4.4 %collective-permute-start.2 = (f32[144,128]{1,0:T(8,128)S(1)}, f32[144,128]{1,0:T(8,128)S(1)}, u32[]{:S(2)}, u32[]{:S(2)}) collective-permute-start(f32[144,128]{1,0:T(8,128)S(1)} %reduce_sum.9), channel_id=1, source_target_pairs={{0,16},{1,17},{2,18},{3,19},{4,20},{5,21},{6,22},{7,23},{8,24},{9,... | collective-permute-start | bytes 221192 | tf_op jit(solution)/shard_map/ppermute | solution.py:417
  69.8 5.1 %collective-permute-start.1 = (f32[144,128]{1,0:T(8,128)S(1)}, f32[144,128]{1,0:T(8,128)S(1)}, u32[]{:S(2)}, u32[]{:S(2)}) collective-permute-start(f32[144,128]{1,0:T(8,128)S(1)} %reduce_sum.9), channel_id=1, source_target_pairs={{0,32},{1,33},{2,34},{3,35},{4,36},{5,37},{6,38},{7,39},{8,40},{9,... | collective-permute-start | bytes 221192 | tf_op jit(solution)/shard_map/ppermute | solution.py:417
  93.5 7.6 %copy-start.1 = (f32[1024]{0:T(1024)S(1)}, f32[1024]{0:T(1024)}, u32[]{:S(2)}) copy-start(f32[1024]{0:T(1024)} %param.9) | copy-start | bytes 12292
  93.5 7.6 %collective-permute-start.4 = (f32[2304,128]{1,0:T(8,128)S(1)}, f32[2304,128]{1,0:T(8,128)}, u32[]{:S(2)}, u32[]{:S(2)}) collective-permute-start(f32[2304,128]{1,0:T(8,128)S(1)} %bitcast.16), channel_id=1, source_target_pairs={{0,64},{64,0},{1,65},{65,1},{2,66},{66,2},{3,67},{67,3},{4,68},{68... | collective-permute-start | bytes 3538952 | tf_op jit(solution)/shard_map/ppermute | solution.py:413
  97.4 33.6 %all-to-all-start.3 = ((f32[16,2,8,1024]{3,2,1,0:T(8,128)}), f32[16,2,8,1024]{3,2,1,0:T(8,128)S(1)}, u32[]{:S(2)}, u32[]{:S(2)}) async-start(f32[16,2,8,1024]{3,2,1,0:T(8,128)} %get-tuple-element.12), calls=%async_computation.3 | async-start | bytes 2097152 | tf_op jit(solution)/shard_map/all_to_all | solution.py:421
  101.1 29.9 %copy-start = (bf16[256,256]{1,0:T(8,128)(2,1)S(1)}, bf16[256,256]{1,0:T(8,128)(2,1)}, u32[]{:S(2)}) copy-start(bf16[256,256]{1,0:T(8,128)(2,1)} %constant.38.clone.table_ref) | copy-start | bytes 393220

commit v13 on v10

--- a/solution.py
+++ b/solution.py
@@ -134,7 +134,7 @@
 
 
 def select_rows(keep_rows, y):
-    cols = 256
+    cols = 512
     features = y.shape[2]
     return pl.pallas_call(
         select_kernel,

time: 133 us -> 133 us (level)
  no operation moved by 1% of the time
where the time goes in v13:
time: 133 us
  blocking collectives  43.1 us (32%)
  Pallas kernels  38.8 us (29%)
  waiting for transfers between devices  31.9 us (24%)
  starting transfers between devices  17.6 us (13%)
    all_to_all x2, blocking collectives, plane_exchange(): lax.all_to_all(x, 'inner', 0, 0, axis_index_groups=PLANES, tiled=True)  43.1 us
    pallas_call x1, Pallas kernels, factor_rows(): pl.pallas_call(factor_kernel, out_shape=(jax.ShapeDtypeStruct((8, FEAT),...  29.8 us
    all_to_all x1, waiting for transfers between devices, local(): lax.all_to_all(mixed.reshape(4, 128, FEAT), 'inner', 0, 0, axis_index_gro...  25.2 us
    ppermute x2, starting transfers between devices, swap_cores(): return lax.ppermute(x, 'outer', [(0, 1), (1, 0)])  5.87 us
    all_to_all x1, starting transfers between devices, local(): lax.all_to_all(mixed.reshape(4, 128, FEAT), 'inner', 0, 0, axis_index_gro...  5.87 us
    ppermute x3, waiting for transfers between devices, along_z(): lax.ppermute(x, 'inner', [(i, (i + 16 * distance) % 64) for i in range(64)])  4.42 us
    pallas_call x1, Pallas kernels, local_mix(): pl.pallas_call(local_mix_kernel, out_shape=jax.ShapeDtypeStruct((rows, fe...  4.12 us
    all_to_all x1, starting transfers between devices, plane_exchange(): lax.all_to_all(x, 'inner', 0, 0, axis_index_groups=PLANES, tiled=True)  3.66 us
  transfers between devices with their start and end apart: 7, of which 5 were waited for; matrix products, arithmetic and copies ran while one was open for 0% of the time, Pallas kernels for 22%

profile of v13, /device:TPU:1, one launch (start us, length us, event | category | flops | bytes accessed | tf_op | source)
XLA Modules:
  0.0 132.8 jit_solution(9119729448701126545)
XLA Ops:
  0.6 4.1 %shard_map.77 = f32[512,1024]{1,0:T(8,128)} custom-call(bf16[512,512]{1,0:T(8,128)(2,1)} %constant.37.clone.table_hbm, s32[1,512]{1,0:T(1,128)} %bitcast.23, f32[512,1024]{1,0:T(8,128)} %x_hbm.1), custom_call_target="tpu_custom_call" | custom-call | tf_op jit(solution)/shard_map/pallas_call | solution.py:99
  4.8 5.9 %all-to-all-start = ((f32[4,128,1024]{2,1,0:T(8,128)}), f32[4,128,1024]{2,1,0:T(8,128)S(1)}, u32[]{:S(2)}, u32[]{:S(2)}) async-start(f32[4,128,1024]{2,1,0:T(8,128)} %bitcast.20), calls=%async_computation | async-start | bytes 4194304 | tf_op jit(solution)/shard_map/all_to_all | solution.py:426
  10.6 0.1 reshape.34
  10.7 0.1 copy.10
  10.8 25.2 %all-to-all-done.y_ref = f32[4,128,1024]{2,1,0:T(8,128)S(1)} async-done(((f32[4,128,1024]{2,1,0:T(8,128)}), f32[4,128,1024]{2,1,0:T(8,128)S(1)}, u32[]{:S(2)}, u32[]{:S(2)}) %all-to-all-start) | async-done | bytes 2097184 | tf_op jit(solution)/shard_map/all_to_all | solution.py:426
  36.1 0.8 shard_map.78
  36.8 1.9 %collective-permute-start = (f32[2,16,8,1024]{3,2,1,0:T(8,128)S(1)}, f32[2,16,8,1024]{3,2,1,0:T(8,128)S(1)}, u32[]{:S(2)}, u32[]{:S(2)}) collective-permute-start(f32[2,16,8,1024]{3,2,1,0:T(8,128)S(1)} %bitcast.13), channel_id=1, source_target_pairs={{0,64},{64,0},{1,65},{65,1},{2,66},{66,2},{3,67},{67,3},{4,68},{68... | collective-permute-start | bytes 3145736 | tf_op jit(solution)/shard_map/ppermute | solution.py:409
  38.8 0.1 pad_add_fusion.ids_ref
  38.9 2.2 %collective-permute-done.w_hbm = f32[2,16,8,1024]{3,2,1,0:T(8,128)S(1)} collective-permute-done((f32[2,16,8,1024]{3,2,1,0:T(8,128)S(1)}, f32[2,16,8,1024]{3,2,1,0:T(8,128)S(1)}, u32[]{:S(2)}, u32[]{:S(2)}) %collective-permute-start) | collective-permute-done | bytes 1048608 | tf_op jit(solution)/shard_map/ppermute | solution.py:409
  41.1 2.3 %shard_map.79 = (f32[16,144,128]{2,1,0:T(8,128)S(1)}, f32[16,2,8,1024]{3,2,1,0:T(8,128)}) custom-call(s32[2]{0:T(128)S(1)} %pad_add_fusion.ids_ref, f32[2,16,8,1024]{3,2,1,0:T(8,128)S(1)} %bitcast.14, f32[2,16,8,1024]{3,2,1,0:T(8,128)S(1)} %collective-permute-done.w_hbm), custom_call_target="tpu_custom_call" | custom-call | tf_op jit(solution)/shard_map/pallas_call | solution.py:186
  43.4 24.6 %all_to_all.20 = f32[16,144,128]{2,1,0:T(8,128)S(1)} all-to-all(f32[16,144,128]{2,1,0:T(8,128)S(1)} %get-tuple-element.9), channel_id=1, replica_groups={{0,1,2,3,4,5,6,7,8,9,10,11,12,13,14,15},{16,17,18,19,20,21,22,23,24,25,..., dimensions={0} | all-to-all | bytes 2359296 | tf_op jit(solution)/shard_map/all_to_all | solution.py:417
  68.0 0.1 reduce_sum.9
  68.1 1.0 collective-permute-start.3
  69.0 0.6 collective-permute-start.2
  69.6 0.7 collective-permute-start.1
  70.3 1.1 collective-permute-done.3
  71.4 2.1 %collective-permute-done.2 = f32[144,128]{1,0:T(8,128)S(1)} collective-permute-done((f32[144,128]{1,0:T(8,128)S(1)}, f32[144,128]{1,0:T(8,128)S(1)}, u32[]{:S(2)}, u32[]{:S(2)}) %collective-permute-start.2) | collective-permute-done | bytes 73760 | tf_op jit(solution)/shard_map/ppermute | solution.py:413
  73.4 1.3 collective-permute-done.1
  74.7 0.1 broadcast_in_dim.10
  74.8 18.5 %all_to_all.21 = f32[16,144,128]{2,1,0:T(8,128)S(1)} all-to-all(f32[16,144,128]{2,1,0:T(8,128)S(1)} %broadcast_in_dim.10), channel_id=1, replica_groups={{0,1,2,3,4,5,6,7,8,9,10,11,12,13,14,15},{16,17,18,19,20,21,22,23,24,25,..., dimensions={0} | all-to-all | bytes 2359296 | tf_op jit(solution)/shard_map/all_to_all | solution.py:417
  93.3 3.9 %collective-permute-start.4 = (f32[2304,128]{1,0:T(8,128)S(1)}, f32[2304,128]{1,0:T(8,128)}, u32[]{:S(2)}, u32[]{:S(2)}) collective-permute-start(f32[2304,128]{1,0:T(8,128)S(1)} %bitcast.16), channel_id=1, source_target_pairs={{0,64},{64,0},{1,65},{65,1},{2,66},{66,2},{3,67},{67,3},{4,68},{68... | collective-permute-start | bytes 3538952 | tf_op jit(solution)/shard_map/ppermute | solution.py:409
  97.2 3.7 %all-to-all-start.3 = ((f32[16,2,8,1024]{3,2,1,0:T(8,128)}), f32[16,2,8,1024]{3,2,1,0:T(8,128)S(1)}, u32[]{:S(2)}, u32[]{:S(2)}) async-start(f32[16,2,8,1024]{3,2,1,0:T(8,128)} %get-tuple-element.12), calls=%async_computation.3 | async-start | bytes 2097152 | tf_op jit(solution)/shard_map/all_to_all | solution.py:417
  100.9 29.8 %shard_map.80 = (f32[8,1024]{1,0:T(8,128)}, s32[2]{0:T(128)S(1)}) custom-call(s32[2]{0:T(128)S(1)} %pad_add_fusion.ids_ref, f32[1,1024]{1,0:T(1,128)S(1)} %bitcast.19, f32[2304,128]{1,0:T(8,128)S(1)} %bitcast.17, f32[2304,128]{1,0:T(8,128)} %collective-permute-done.4.other_hbm), custom_call_target="tpu_custom_call" | custom-call | flops 40000000000 | bytes 2097152 | tf_op jit(solution)/shard_map/pallas_call | solution.py:395
  130.7 1.9 %shard_map.81 = f32[256,1024]{1,0:T(8,128)} custom-call(s32[2]{0:T(128)S(1)} %get-tuple-element.11.ids_ref, bf16[256,256]{1,0:T(8,128)(2,1)S(1)} %copy-done, f32[256,1024]{1,0:T(8,128)S(1)} %bitcast.15), custom_call_target="tpu_custom_call" | custom-call | tf_op jit(solution)/shard_map/pallas_call | solution.py:224
  (11 shorter events, 0.1 us)
Async XLA Ops:
  4.8 5.9 %copy-start.2 = (s32[128,2]{0,1:T(2,128)S(1)}, s32[128,2]{0,1:T(2,128)}, u32[]{:S(2)}) copy-start(s32[128,2]{0,1:T(2,128)} %param.8) | copy-start | bytes 3076
  4.8 31.3 %all-to-all-start = ((f32[4,128,1024]{2,1,0:T(8,128)}), f32[4,128,1024]{2,1,0:T(8,128)S(1)}, u32[]{:S(2)}, u32[]{:S(2)}) async-start(f32[4,128,1024]{2,1,0:T(8,128)} %bitcast.20), calls=%async_computation | async-start | bytes 4194304 | tf_op jit(solution)/shard_map/all_to_all | solution.py:426
  36.8 4.2 %collective-permute-start = (f32[2,16,8,1024]{3,2,1,0:T(8,128)S(1)}, f32[2,16,8,1024]{3,2,1,0:T(8,128)S(1)}, u32[]{:S(2)}, u32[]{:S(2)}) collective-permute-start(f32[2,16,8,1024]{3,2,1,0:T(8,128)S(1)} %bitcast.13), channel_id=1, source_target_pairs={{0,64},{64,0},{1,65},{65,1},{2,66},{66,2},{3,67},{67,3},{4,68},{68... | collective-permute-start | bytes 3145736 | tf_op jit(solution)/shard_map/ppermute | solution.py:409
  68.1 3.3 %collective-permute-start.3 = (f32[144,128]{1,0:T(8,128)S(1)}, f32[144,128]{1,0:T(8,128)S(1)}, u32[]{:S(2)}, u32[]{:S(2)}) collective-permute-start(f32[144,128]{1,0:T(8,128)S(1)} %reduce_sum.9), channel_id=1, source_target_pairs={{0,48},{1,49},{2,50},{3,51},{4,52},{5,53},{6,54},{7,55},{8,56},{9,... | collective-permute-start | bytes 221192 | tf_op jit(solution)/shard_map/ppermute | solution.py:413
  69.0 4.4 %collective-permute-start.2 = (f32[144,128]{1,0:T(8,128)S(1)}, f32[144,128]{1,0:T(8,128)S(1)}, u32[]{:S(2)}, u32[]{:S(2)}) collective-permute-start(f32[144,128]{1,0:T(8,128)S(1)} %reduce_sum.9), channel_id=1, source_target_pairs={{0,16},{1,17},{2,18},{3,19},{4,20},{5,21},{6,22},{7,23},{8,24},{9,... | collective-permute-start | bytes 221192 | tf_op jit(solution)/shard_map/ppermute | solution.py:413
  69.6 5.1 %collective-permute-start.1 = (f32[144,128]{1,0:T(8,128)S(1)}, f32[144,128]{1,0:T(8,128)S(1)}, u32[]{:S(2)}, u32[]{:S(2)}) collective-permute-start(f32[144,128]{1,0:T(8,128)S(1)} %reduce_sum.9), channel_id=1, source_target_pairs={{0,32},{1,33},{2,34},{3,35},{4,36},{5,37},{6,38},{7,39},{8,40},{9,... | collective-permute-start | bytes 221192 | tf_op jit(solution)/shard_map/ppermute | solution.py:413
  93.3 7.6 %copy-start.1 = (f32[1024]{0:T(1024)S(1)}, f32[1024]{0:T(1024)}, u32[]{:S(2)}) copy-start(f32[1024]{0:T(1024)} %param.9) | copy-start | bytes 12292
  93.3 7.6 %collective-permute-start.4 = (f32[2304,128]{1,0:T(8,128)S(1)}, f32[2304,128]{1,0:T(8,128)}, u32[]{:S(2)}, u32[]{:S(2)}) collective-permute-start(f32[2304,128]{1,0:T(8,128)S(1)} %bitcast.16), channel_id=1, source_target_pairs={{0,64},{64,0},{1,65},{65,1},{2,66},{66,2},{3,67},{67,3},{4,68},{68... | collective-permute-start | bytes 3538952 | tf_op jit(solution)/shard_map/ppermute | solution.py:409
  97.2 33.5 %all-to-all-start.3 = ((f32[16,2,8,1024]{3,2,1,0:T(8,128)}), f32[16,2,8,1024]{3,2,1,0:T(8,128)S(1)}, u32[]{:S(2)}, u32[]{:S(2)}) async-start(f32[16,2,8,1024]{3,2,1,0:T(8,128)} %get-tuple-element.12), calls=%async_computation.3 | async-start | bytes 2097152 | tf_op jit(solution)/shard_map/all_to_all | solution.py:417
  100.9 29.8 %copy-start = (bf16[256,256]{1,0:T(8,128)(2,1)S(1)}, bf16[256,256]{1,0:T(8,128)(2,1)}, u32[]{:S(2)}) copy-start(bf16[256,256]{1,0:T(8,128)(2,1)} %constant.38.clone.table_ref) | copy-start | bytes 393220
